TPU v7x, 32 devices: a whole 2x2x4 slice. The times are simulated.
32 devices in a mesh: seq: 8 (over z, y), head: 4 (over x, core).
Axes of the slice: x: 2, y: 2, z: 4, core: 2. Of those that a mesh axis runs over, the one named last changes fastest.
Arguments:
- queries: bfloat16 [1, 8192, 4096], P(None, ('seq', 'head')), may hold values from -4 to 4
- keys: bfloat16 [1, 8192, 4096], P(None, ('seq', 'head')), may hold values from -4 to 4
- values: bfloat16 [1, 8192, 4096], P(None, ('seq', 'head')), may hold values from -6 to 6
- features: bfloat16 [32, 256, 128], P('head'), may hold values from -4 to 4
Outputs:
- attended: bfloat16 [1, 8192, 4096], P(None, ('seq', 'head'))
All inputs are finite; a program needn't handle non-finite values.
Results may differ from a plain program's by a relative error of at most 0.0065.
Values may be sent and summed in bfloat16 or wider, within the bound.
No kernel may reach another device: no remote copies, remote signals or barrier semaphores. Data moves between devices by JAX's collectives and lax.ppermute only.
A program may use at most 128 MiB of HBM per device.

v0:
```python
import math

import jax
import jax.numpy as jnp
from jax import lax
from jax.sharding import PartitionSpec as P


def carried_in(shard, axis, combine, identity):
    size, mine = (lax.axis_size(axis), lax.axis_index(axis))
    everything = jax.tree.map(lambda part: lax.all_gather(part, axis), shard)
    start = jax.tree.map(
        lambda part, zero: jnp.broadcast_to(jnp.asarray(zero, part.dtype), part.shape),
        shard,
        identity,
    )

    def turn(k, before):
        reached = k < mine
        new = combine(before, jax.tree.map(lambda part: part[k], everything))
        return jax.tree.map(lambda a, b: jnp.where(reached, a, b), new, before)

    return lax.fori_loop(0, size, turn, start)


def combine(earlier, later):
    return (earlier[0] + later[0], earlier[1] + later[1])


def attend(queries, keys, values, features):
    batch_count, seg_rows, local_width = queries.shape
    head_count, feat_count, head_size = features.shape
    root_scale = head_size ** (-0.25)
    wide_dirs = features.astype(jnp.float32)
    dir_factor = lax.rsqrt(jnp.mean(wide_dirs * wide_dirs, axis=-1) + 1e-06)

    def mapped(source):
        split_into_heads = source.reshape(batch_count, seg_rows, head_count, head_size)
        projected = jnp.einsum(
            "kqae,age->kaqg", split_into_heads, features, preferred_element_type=jnp.float32
        )
        widened = split_into_heads.astype(jnp.float32)
        square_sum = jnp.sum(widened * widened, axis=-1)
        square_sum = jnp.transpose(square_sum, (0, 2, 1))[..., None]
        row_factor = lax.rsqrt(square_sum / head_size + 1e-06)
        projected = projected * row_factor * dir_factor[None, :, None, :] * root_scale
        halved = 0.5 * root_scale * root_scale * square_sum * row_factor * row_factor
        return (jnp.exp(projected - halved) * (1.0 / math.sqrt(feat_count))).astype(jnp.bfloat16)

    phi_q = mapped(queries)
    phi_k = mapped(keys)
    value_heads = jnp.transpose(
        values.reshape(batch_count, seg_rows, head_count, head_size), (0, 2, 1, 3)
    )
    states = jnp.einsum("bhsm,bhsd->bhmd", phi_k, value_heads, preferred_element_type=jnp.float32)
    totals = jnp.sum(phi_k.astype(jnp.float32), axis=2)
    identity = (jnp.zeros_like(states), jnp.zeros_like(totals))
    carried, carried_totals = carried_in((states, totals), "seq", combine, identity)
    causal_mask = jnp.tril(jnp.ones((seg_rows, seg_rows), dtype=bool))

    def per_batch(pieces):
        batch_q, batch_k, batch_v, batch_running_state, batch_total = pieces
        scores = jnp.einsum("hsm,htm->hst", batch_q, batch_k, preferred_element_type=jnp.float32)
        scores = jnp.where(causal_mask[None], scores, jnp.float32(0.0))
        widened_query = batch_q.astype(jnp.float32)
        denominator = jnp.sum(scores, axis=2) + jnp.einsum(
            "hsm,hm->hs", widened_query, batch_total, precision=lax.Precision.HIGHEST
        )
        weights = scores.astype(jnp.bfloat16)
        numerator_sum = jnp.einsum(
            "hst,htd->hsd", weights, batch_v, preferred_element_type=jnp.float32
        )
        numerator_sum = numerator_sum + jnp.einsum(
            "pen,pnv->pev", widened_query, batch_running_state, precision=lax.Precision.HIGHEST
        )
        return (numerator_sum / denominator[..., None]).astype(jnp.bfloat16)

    result_list = lax.map(per_batch, (phi_q, phi_k, value_heads, carried, carried_totals))
    return jnp.transpose(result_list, (0, 2, 1, 3)).reshape(batch_count, seg_rows, local_width)


def body(queries, keys, values, features):
    moved = (
        lax.all_to_all(queries, "head", split_axis=2, concat_axis=1, tiled=True),
        lax.all_to_all(keys, "head", split_axis=2, concat_axis=1, tiled=True),
        lax.all_to_all(values, "head", split_axis=2, concat_axis=1, tiled=True),
    )
    attended = attend(moved[0], moved[1], moved[2], features)
    return lax.all_to_all(attended, "head", split_axis=1, concat_axis=2, tiled=True)


def solution(mesh):
    placed = (
        P(None, ("seq", "head"), None),
        P(None, ("seq", "head"), None),
        P(None, ("seq", "head"), None),
        P("head", None, None),
    )
    return jax.shard_map(
        body, mesh=mesh, in_specs=placed, out_specs=P(None, ("seq", "head"), None), check_vma=False
    )
```

profile of v0, /device:TPU:0, one launch (start us, length us, event | category | flops | bytes accessed | tf_op | source)
XLA Modules:
  0.0 382.9 jit_solution(12050893695163474145)
XLA Ops:
  6.5 10.0 %copy.76 = bf16[1,256,4096]{1,0,2:T(2,128)(2,1)} copy(bf16[1,256,4096]{2,1,0:T(8,128)(2,1)} %param.7) | data formatting | bytes 4194304 | tf_op args[1]
  17.1 21.6 %reduce.6 = bf16[4096,256]{1,0:T(8,128)(2,1)S(1)} reduce(bf16[4096,1,256]{2,1,0:T(2,128)(2,1)} %bitcast.151, bf16[]{:T(256)} %broadcast.154), dimensions={1}, to_apply=%bitcast.130.reduce_sub_computation | reduce | bytes 4194306
  40.7 4.2 %all-to-all-start.1 = ((bf16[4,2,131072]{2,1,0:T(2,128)(2,1)}), bf16[4,2,131072]{2,1,0:T(2,128)(2,1)S(1)}, u32[]{:S(2)}, u32[]{:S(2)}) async-start(bf16[4,2,131072]{2,1,0:T(2,128)(2,1)} %reshape.178), calls=%async_computation.1 | async-start | bytes 4194304 | tf_op jit(solution)/shard_map/all_to_all | solution.py:85
  44.9 10.0 %copy.84 = bf16[1,256,4096]{1,0,2:T(2,128)(2,1)} copy(bf16[1,256,4096]{2,1,0:T(8,128)(2,1)} %param.8) | data formatting | bytes 4194304 | tf_op args[2]
  54.9 22.9 %reduce.7 = bf16[4096,256]{1,0:T(8,128)(2,1)} reduce(bf16[4096,1,256]{2,1,0:T(2,128)(2,1)} %bitcast.157, bf16[]{:T(256)} %broadcast.154), dimensions={1}, to_apply=%bitcast.132.reduce_sub_computation | reduce | bytes 4194306
  81.9 4.5 %all-to-all-start.2 = ((bf16[4,2,131072]{2,1,0:T(2,128)(2,1)}), bf16[4,2,131072]{2,1,0:T(2,128)(2,1)}, u32[]{:S(2)}, u32[]{:S(2)}) async-start(bf16[4,2,131072]{2,1,0:T(2,128)(2,1)} %reshape.180), calls=%async_computation.2 | async-start | bytes 4194304 | tf_op jit(solution)/shard_map/all_to_all | solution.py:86
  101.1 5.4 %copy.79 = f32[1,4,256,1024]{3,2,1,0:T(8,128)} copy(f32[1,4,256,1024]{2,3,1,0:T(8,128)} %convert_multiply_fusion) | data formatting | bytes 8388608 | tf_op jit(solution)/shard_map/mul | solution.py:43
  106.5 5.2 %copy.109 = f32[128,8,8,128]{3,2,1,0:T(8,128)} copy(f32[128,8,8,128]{3,1,2,0:T(8,128)} %bitcast.160) | data formatting | bytes 8388608
  115.6 5.0 %reshape.181 = bf16[4096,1,256]{2,1,0:T(2,128)(2,1)} reshape(bf16[4,2,131072]{2,1,0:T(2,128)(2,1)} %all-to-all-done.2) | data formatting | bytes 4194304
  127.5 5.4 %convert_reduce_fusion = (f32[8,256]{1,0:T(8,128)S(1)}, bf16[8,256,1,1024]{3,1,0,2:T(8,128)(2,1)S(1)}) fusion(f32[8,1024]{1,0:T(8,128)S(1)} %copy.81, f32[8,256]{1,0:T(8,128)S(1)} %add_rsqrt_fusion, f32[8,1024]{1,0:T(8,128)S(1)} %copy.80, bf16[8,256,128]{2,1,0:T(8,128)(2,1)S(1)} %copy-done.4, bf16[1024,8,128]{2,1,0:T(8,128)(2,1)} %bitcast.170), kind=kOutput, calls=%fused_computation.21 | convolution fusion | flops 553646080 | bytes 6897664 | tf_op jit(solution)/shard_map/kqae,age->kaqg/dot_general | solution.py:39
  137.1 7.4 %copy.70 = bf16[1,256,4096]{1,0,2:T(2,128)(2,1)} copy(bf16[1,256,4096]{2,1,0:T(8,128)(2,1)S(1)} %copy-done.1) | data formatting | bytes 4194304 | tf_op args[0]
  144.6 21.8 %reduce.5 = bf16[4096,256]{1,0:T(8,128)(2,1)S(1)} reduce(bf16[4096,1,256]{2,1,0:T(2,128)(2,1)} %bitcast.158, bf16[]{:T(256)} %broadcast.154), dimensions={1}, to_apply=%bitcast.128.reduce_sub_computation | reduce | bytes 4194306
  173.4 24.3 %all-to-all-done = bf16[4,2,131072]{2,1,0:T(2,128)(2,1)S(1)} async-done(((bf16[4,2,131072]{2,1,0:T(2,128)(2,1)}), bf16[4,2,131072]{2,1,0:T(2,128)(2,1)S(1)}, u32[]{:S(2)}, u32[]{:S(2)}) %all-to-all-start) | async-done | bytes 2097184 | tf_op jit(solution)/shard_map/all_to_all | solution.py:84
  211.9 5.4 %copy.73 = f32[1,4,256,1024]{3,2,1,0:T(8,128)} copy(f32[1,4,256,1024]{2,3,1,0:T(8,128)} %convert_multiply_fusion.1) | data formatting | bytes 8388608 | tf_op jit(solution)/shard_map/mul | solution.py:43
  217.3 5.1 %copy.107 = f32[128,8,8,128]{3,2,1,0:T(8,128)} copy(f32[128,8,8,128]{3,1,2,0:T(8,128)} %bitcast.162) | data formatting | bytes 8388608
  226.4 32.0 %all-gather.1 = f32[64,256]{1,0:T(8,128)S(1)} all-gather(f32[8,256]{1,0:T(8,128)S(1)} %get-tuple-element.206), channel_id=3, replica_groups=mesh['seq'=8,'head'=4] {'seq'}, dimensions={0}, use_global_device_ids=true | all-gather | bytes 73728 | tf_op jit(solution)/shard_map/all_gather | solution.py:11
  258.4 6.4 %fusion.15 = bf16[8,1024,256]{1,2,0:T(8,128)(2,1)} fusion(f32[8,1024]{1,0:T(8,128)S(1)} %copy.75, f32[8,256]{1,0:T(8,128)S(1)} %add_rsqrt_fusion, f32[8,1024]{1,0:T(8,128)S(1)} %copy.74, bf16[8,256,128]{2,1,0:T(8,128)(2,1)S(1)} %copy-done.5, bf16[1024,8,128]{2,1,0:T(8,128)(2,1)} %bitcast.171), kind=kOutput, calls=%fused_computation.22 | convolution fusion | flops 549453824 | bytes 6889472 | tf_op jit(solution)/shard_map/kqae,age->kaqg/dot_general | solution.py:39
  264.8 12.5 %select_reduce_fusion = (f32[8,1024]{1,0:T(8,128)S(1)}, bf16[8,1024,1024]{1,2,0:T(8,128)(2,1)}) fusion(pred[1024,1024]{0,1:T(8,128)(4,1)} %iota_compare_fusion, bf16[8,1024,256]{1,2,0:T(8,128)(2,1)} %fusion.15, bf16[8,256,1,1024]{3,1,0,2:T(8,128)(2,1)} %copy-done.6), kind=kOutput, calls=%fused_computation.2 | convolution fusion | flops 4320124928 | bytes 26247168 | tf_op jit(solution)/shard_map/while/body/eval_jaxpr/hsm,htm->hst/dot_general | solution.py:63
  277.3 10.8 %fusion = f32[8,1024,128]{1,2,0:T(8,128)} fusion(bf16[8,1024,1024]{1,2,0:T(8,128)(2,1)} %get-tuple-element.205, pred[1024,1024]{0,1:T(8,128)(4,1)} %iota_compare_fusion, bf16[1,1024,8,128]{1,3,2,0:T(8,128)(2,1)S(1)} %copy-done.3), kind=kOutput, calls=%fused_computation.4 | convolution fusion | flops 2155872256 | bytes 24117248 | tf_op jit(solution)/shard_map/while/body/eval_jaxpr/hst,htd->hsd/dot_general | solution.py:70
  288.1 13.0 %while.20 = (s32[]{:T(128)}, f32[1,8,256,128]{3,2,1,0:T(8,128)S(1)}, f32[1,8,256]{2,1,0:T(8,128)S(1)}, s32[]{:T(128)}, f32[8,1,8,256,128]{4,3,2,1,0:T(8,128)}, /...) while((s32[]{:T(128)}, f32[1,8,256,128]{3,2,1,0:T(8,128)S(1)}, f32[1,8,256]{2,1,0:T(8,128)S(1)}, ...), condition=%wide.region_5.6_spmd.clone, body=%wide.region_4.5_spmd.clone.sunk | while | flops 792580 | bytes 3170427 | solution.py:23
  305.2 4.5 %divide_convert_fusion = bf16[8,1024,128]{1,2,0:T(8,128)(2,1)S(1)} fusion(f32[8,1024,128]{1,2,0:T(8,128)} %fusion, bf16[8,1024,256]{1,2,0:T(8,128)(2,1)S(1)} %copy-done, f32[8,1024]{1,0:T(8,128)S(1)} %bitcast_add_fusion, f32[1,8,256,128]{3,2,1,0:T(8,128)S(1)} %get-tuple-element.139), kind=kOutput, calls=%fused_computation.27 | convolution fusion | flops 3224371200 | bytes 11567104 | tf_op jit(solution)/shard_map/while/body/eval_jaxpr/pen,pnv->pev/dot_general | solution.py:73
  309.7 8.0 %copy.91 = bf16[1,1024,1024]{2,0,1:T(2,128)(2,1)} copy(bf16[1,1024,1024]{1,2,0:T(8,128)(2,1)S(1)} %bitcast.169) | data formatting | bytes 4194304 | tf_op jit(solution)/shard_map/reshape | solution.py:79
  317.7 12.8 %reduce.8 = bf16[1024,1024]{1,0:T(8,128)(2,1)S(1)} reduce(bf16[1024,1,1024]{2,1,0:T(2,128)(2,1)} %bitcast.152, bf16[]{:T(256)} %broadcast.154), dimensions={1}, to_apply=%bitcast.134.reduce_sub_computation | reduce | bytes 4194306
  333.3 29.3 %all_to_all.63 = bf16[4,2,131072]{2,1,0:T(2,128)(2,1)S(1)} all-to-all(bf16[4,2,131072]{2,1,0:T(2,128)(2,1)} %reshape.182), channel_id=1, replica_groups=mesh['seq'=8,'head'=4] {'head'}, dimensions={0} | all-to-all | bytes 4194304 | tf_op jit(solution)/shard_map/all_to_all | solution.py:89
  (76 shorter events, 94.1 us)
Async XLA Ops:
  40.7 41.2 %all-to-all-start.1 = ((bf16[4,2,131072]{2,1,0:T(2,128)(2,1)}), bf16[4,2,131072]{2,1,0:T(2,128)(2,1)S(1)}, u32[]{:S(2)}, u32[]{:S(2)}) async-start(bf16[4,2,131072]{2,1,0:T(2,128)(2,1)} %reshape.178), calls=%async_computation.1 | async-start | bytes 4194304 | tf_op jit(solution)/shard_map/all_to_all | solution.py:85
  77.8 8.8 %copy-start.4 = (bf16[8,256,128]{2,1,0:T(8,128)(2,1)S(1)}, bf16[8,256,128]{2,1,0:T(8,128)(2,1)}, u32[]{:S(2)}) copy-start(bf16[8,256,128]{2,1,0:T(8,128)(2,1)} %param.9) | copy-start | bytes 1572868
  81.9 33.7 %all-to-all-start.2 = ((bf16[4,2,131072]{2,1,0:T(2,128)(2,1)}), bf16[4,2,131072]{2,1,0:T(2,128)(2,1)}, u32[]{:S(2)}, u32[]{:S(2)}) async-start(bf16[4,2,131072]{2,1,0:T(2,128)(2,1)} %reshape.180), calls=%async_computation.2 | async-start | bytes 4194304 | tf_op jit(solution)/shard_map/all_to_all | solution.py:86
  86.4 201.7 %all-gather.4.cloned.1.call-start = ((), (), s32[]{:S(2)}) async-start(), calls=%async_computation.4 | async-start | bytes 9437184 | tf_op jit(solution)/shard_map/all_gather | solution.py:11
  127.5 7.4 %copy-start.2 = (bf16[1,1024,8,128]{1,3,2,0:T(8,128)(2,1)S(1)}, bf16[1,1024,8,128]{1,3,2,0:T(8,128)(2,1)}, u32[]{:S(2)}) copy-start(bf16[1,1024,8,128]{1,3,2,0:T(8,128)(2,1)} %reshape.168) | copy-start | bytes 6291460
  132.9 1.9 copy-start.6
  134.9 2.3 copy-start.1
  168.4 29.3 %all-to-all-start = ((bf16[4,2,131072]{2,1,0:T(2,128)(2,1)}), bf16[4,2,131072]{2,1,0:T(2,128)(2,1)S(1)}, u32[]{:S(2)}, u32[]{:S(2)}) async-start(bf16[4,2,131072]{2,1,0:T(2,128)(2,1)} %reshape.176), calls=%async_computation | async-start | bytes 4194304 | tf_op jit(solution)/shard_map/all_to_all | solution.py:84
  222.5 36.0 %copy-start.5 = (bf16[8,256,128]{2,1,0:T(8,128)(2,1)S(1)}, bf16[8,256,128]{2,1,0:T(8,128)(2,1)}, u32[]{:S(2)}) copy-start(bf16[8,256,128]{2,1,0:T(8,128)(2,1)} %param.9) | copy-start | bytes 1572868
  264.8 12.5 %copy-start.3 = (bf16[1,1024,8,128]{1,3,2,0:T(8,128)(2,1)S(1)}, bf16[1,1024,8,128]{1,3,2,0:T(8,128)(2,1)}, u32[]{:S(2)}) copy-start(bf16[1,1024,8,128]{1,3,2,0:T(8,128)(2,1)} %reshape.168) | copy-start | bytes 6291460
  301.1 4.1 %copy-start = (bf16[8,1024,256]{1,2,0:T(8,128)(2,1)S(1)}, bf16[8,1024,256]{1,2,0:T(8,128)(2,1)}, u32[]{:S(2)}) copy-start(bf16[8,1024,256]{1,2,0:T(8,128)(2,1)} %fusion.15) | copy-start | bytes 12582916
Sparse Core Ops, SparseCore 0:
  137.3 128.1 all-gather.3
where the time goes:
time: 390 us; the launch traced here: 383 us
  local copies, waits for them, and re-layouts  119 us (31%)
  other arithmetic  105 us (27%)
  blocking collectives  61.3 us (16%)
  matrix products  45.8 us (12%)
  waiting for transfers between devices  24.4 us (6%)
  between operations  14.1 us (4%)
  starting transfers between devices  12.5 us (3%)
    unnamed x34, local copies, waits for them, and re-layouts  84 us
    unnamed x6, other arithmetic  79 us
    all_gather x1, blocking collectives, carried_in(): everything = jax.tree.map(lambda part: lax.all_gather(part, axis), shard)  32 us
    all_to_all x1, blocking collectives, body(): lax.all_to_all(attended, 'head', split_axis=1, concat_axis=2, tiled=True)  29.3 us
    all_to_all x1, waiting for transfers between devices, body(): lax.all_to_all(queries, 'head', split_axis=2, concat_axis=1, tiled=True)  24.3 us
    select_n x16, other arithmetic, turn(): return jax.tree.map(lambda a, b: jnp.where(reached, a, b), new, before)  12.8 us
    dot_general x1, matrix products, per_batch(): jnp.einsum('hsm,htm->hst', batch_q, batch_k, preferred_element_type=jnp.f...  12.5 us
    dot_general x2, matrix products, mapped(): jnp.einsum('kqae,age->kaqg', split_into_heads, features, preferred_elemen...  11.8 us
  transfers between devices with their start and end apart: 4, of which 1 were waited for; matrix products, arithmetic and copies ran while one was open for 41% of the time, Pallas kernels for 0%

commit v1 on v0

v1 whole, which is shorter than its diff:
```python
import functools
import math

import jax
import jax.numpy as jnp
from jax import lax
from jax.experimental import pallas as pl
from jax.experimental.pallas import tpu as pltpu
from jax.sharding import PartitionSpec as P

F32, BF16 = jnp.float32, jnp.bfloat16
LOG2E = math.log2(math.e)
TOTAL_ROWS = 16
VMEM = 48 * 1024 * 1024


def feature_map(x, w):
    size, count = x.shape[1], w.shape[0]
    c = size ** (-0.25)
    p = lax.dot_general(x, w, (((1,), (1,)), ((), ())), preferred_element_type=F32)
    wide = x.astype(F32)
    square = jnp.sum(wide * wide, axis=1, keepdims=True)
    r = lax.rsqrt(square / size + 1e-06)
    half = square * r * r * (0.5 * c * c * LOG2E) + 0.5 * math.log2(count)
    ww = w.astype(F32)
    ww = ww * ww
    high = ww.astype(BF16)
    low = (ww - high.astype(F32)).astype(BF16)
    ones = jnp.ones((16, size), BF16)
    nt = (((1,), (1,)), ((), ()))
    total = lax.dot_general(ones, high, nt, preferred_element_type=F32)
    total = total + lax.dot_general(ones, low, nt, preferred_element_type=F32)
    s = lax.rsqrt(total[:1] / size + 1e-06)
    return jnp.exp2(p * (r * (c * LOG2E)) * s - half).astype(BF16)


def pick(first, f0, f1, h):
    return jnp.where(first, f0[h], f1[h])


def states_kernel(group, size, pos, k, v, f0, f1, phi, state):
    first = pl.program_id(0) == 0
    rows = []
    for h in range(group):
        cols = slice(h * size, (h + 1) * size)
        ph = feature_map(k[:, cols], pick(first, f0, f1, h))
        phi[0, 0, h] = ph
        st = lax.dot_general(
            v[:, cols], ph, (((0,), (0,)), ((), ())), preferred_element_type=F32
        )
        state[0, 0, h * size : (h + 1) * size] = st.astype(BF16)
        rows.append(jnp.sum(ph.astype(F32), axis=0, keepdims=True))
    rows.append(jnp.zeros((TOTAL_ROWS - group, rows[0].shape[1]), F32))
    state[0, 0, group * size :] = jnp.concatenate(rows, axis=0).astype(BF16)


def weights_kernel(group, size, pos, q, f0, f1, phi_k, phi_q, weights):
    first = pl.program_id(0) == 0
    tokens = q.shape[0]
    row = lax.broadcasted_iota(jnp.int32, (tokens, tokens), 0)
    col = lax.broadcasted_iota(jnp.int32, (tokens, tokens), 1)
    mask = col <= row
    for h in range(group):
        cols = slice(h * size, (h + 1) * size)
        ph = feature_map(q[:, cols], pick(first, f0, f1, h))
        phi_q[0, 0, h] = ph
        sc = lax.dot_general(
            ph, phi_k[0, 0, h], (((1,), (1,)), ((), ())), preferred_element_type=F32
        )
        weights[0, 0, h] = jnp.where(mask, sc, 0.0).astype(BF16)


def output_kernel(group, size, parts, pos, phi_q, weights, v, other, *rest):
    pieces, out, held = rest[: 2 * parts], rest[-2], rest[-1]
    step = pl.program_id(0) * parts + pl.program_id(1)
    add = (pos[1] == 1).astype(F32)
    for i in range(2 * parts):

        @pl.when(step == i)
        def _():
            held[...] = pieces[i][...].astype(F32) + add * other[0, 0].astype(F32)

    tokens, count = phi_q.shape[-2:]
    ones = jnp.ones((tokens, size), BF16)
    for h in range(group):
        cols = slice(h * size, (h + 1) * size)
        st = held[h * size : (h + 1) * size].astype(BF16)
        tot = held[group * size + h : group * size + h + 1]
        tot = jnp.broadcast_to(tot, (size, count)).astype(BF16)
        acc = lax.dot_general(
            phi_q[0, 0, h],
            jnp.concatenate([st, tot], axis=0),
            (((1,), (1,)), ((), ())),
            preferred_element_type=F32,
        )
        acc = acc + jnp.dot(
            weights[0, 0, h],
            jnp.concatenate([v[:, cols], ones], axis=1),
            preferred_element_type=F32,
        )
        out[:, cols] = (acc[:, :size] / acc[:, size:]).astype(BF16)


def body(seqs, heads, queries, keys, values, features):
    tokens, width = queries.shape[1:]
    q, k, v = (a.reshape(tokens, width) for a in (queries, keys, values))
    own, count, size = features.shape
    cores = 2
    nx = heads // cores
    ny = nx if seqs % nx == 0 else 1
    nz = seqs // ny
    flip = 1 if nx > 1 else 0
    group = own // ny
    srows = group * size
    rows = srows + TOTAL_ROWS

    hi, si = lax.axis_index("head"), lax.axis_index("seq")
    x, c = hi // cores, hi % cores
    z, y = si // ny, si % ny
    pos = jnp.stack([x, c, y]).astype(jnp.int32)

    def head_swap(a, bits):
        return lax.ppermute(a, "head", [(i, i ^ bits) for i in range(heads)])

    def seq_swap(a, bits):
        return lax.ppermute(a, "seq", [(i, i ^ bits) for i in range(seqs)])

    def plane_swap(a, dx, dy):
        if dy == 0:
            return head_swap(a, dx * cores)
        if dx == 0:
            return seq_swap(a, dy)
        pairs = [
            (s * heads + h, (s ^ dy) * heads + (h ^ (dx * cores)))
            for s in range(seqs)
            for h in range(heads)
        ]
        return lax.ppermute(a, ("seq", "head"), pairs)

    def column(dx):
        return lambda i, j, p: (
            0,
            ((p[0] ^ dx ^ flip) * cores + (p[1] ^ i)) * ny + (p[2] ^ j),
        )

    def feature_specs():
        shape = (group, count, size)
        return [
            pl.BlockSpec(shape, lambda i, j, p: (jnp.where(i == 0, p[2] ^ j, p[2] ^ (ny - 1)), 0, 0)),
            pl.BlockSpec(shape, lambda i, j, p: (jnp.where(i == 1, p[2] ^ j, p[2]), 0, 0)),
        ]

    def per_head(a, b):
        return pl.BlockSpec((1, 1, group, a, b), lambda i, j, p: (i, j, 0, 0, 0))

    def call(kernel, ins, outs, shapes, flops, extra=(), alias={}):
        return pl.pallas_call(
            kernel,
            out_shape=shapes,
            grid_spec=pltpu.PrefetchScalarGridSpec(
                num_scalar_prefetch=1,
                grid=(cores, ny),
                in_specs=ins,
                out_specs=outs,
                scratch_shapes=extra,
            ),
            input_output_aliases=alias,
            compiler_params=pltpu.CompilerParams(vmem_limit_bytes=VMEM),
            cost_estimate=pl.CostEstimate(
                flops=flops, bytes_accessed=8 << 20, transcendentals=0
            ),
        )

    def token_spec(dx):
        return pl.BlockSpec((tokens, group * size), column(dx))

    dirs = {}
    for ox in range(nx):
        mine = features if ox == 0 else head_swap(features, ox * cores)
        dirs[ox] = (mine, head_swap(mine, 1))

    def states(dx):
        f0, f1 = dirs[dx ^ flip]
        return call(
            functools.partial(states_kernel, group, size),
            [token_spec(dx), token_spec(dx), *feature_specs()],
            [per_head(tokens, count), pl.BlockSpec((1, 1, rows, count), lambda i, j, p: (i, j, 0, 0))],
            [
                jax.ShapeDtypeStruct((cores, ny, group, tokens, count), BF16),
                jax.ShapeDtypeStruct((cores, ny, rows, count), BF16),
            ],
            2 * 2 * tokens * count * size * own * cores,
        )(pos, k, v, f0, f1)

    def weights(dx, phi_k):
        f0, f1 = dirs[dx ^ flip]
        return call(
            functools.partial(weights_kernel, group, size),
            [token_spec(dx), *feature_specs(), per_head(tokens, count)],
            [per_head(tokens, count), per_head(tokens, tokens)],
            [
                jax.ShapeDtypeStruct((cores, ny, group, tokens, count), BF16),
                jax.ShapeDtypeStruct((cores, ny, group, tokens, tokens), BF16),
            ],
            2 * tokens * count * (size + tokens) * own * cores,
        )(pos, q, f0, f1, phi_k)

    order_x = [flip] + [dx for dx in range(nx) if dx != flip]
    phi_k, other, piece, got = {}, {}, {}, {}
    for dx in order_x:
        phi_k[dx], state = states(dx)
        other[dx] = head_swap(state, 1)
        for dy in range(ny):
            t = state[0, dy].astype(F32) + other[dx][1, dy].astype(F32)
            piece[dx, dy] = t.astype(BF16)
        for dy in range(ny):
            if (dx, dy) != (0, 0):
                got[dx, dy] = plane_swap(piece[dx, dy], dx, dy)
    got[0, 0] = piece[0, 0]

    wide = {key: a.astype(F32) for key, a in got.items()}
    plane = functools.reduce(lambda a, b: a + b, wide.values()).astype(BF16)
    zrows = srows // nz
    plane_totals = plane[srows:]
    heard = []
    for j in range(nz):
        part = lax.dynamic_slice_in_dim(plane, (z ^ j) * zrows, zrows, 0)
        part = jnp.concatenate([part, plane_totals], axis=0)
        heard.append(part if j == 0 else seq_swap(part, j * ny))
    heard_wide = [a.astype(F32) for a in heard]

    def before(target):
        total = 0.0
        for j in range(nz):
            total = total + jnp.where((z ^ j) < target, heard_wide[j], 0.0)
        return total

    prefix = []
    for j in range(nz):
        e = before(z ^ j)[:zrows].astype(BF16)
        prefix.append(e if j == 0 else seq_swap(e, j * ny))
    parts = []
    for p in range(nz):
        part = prefix[0]
        for j in range(1, nz):
            part = jnp.where((z ^ j) == p, prefix[j], part)
        parts.append(part.astype(F32))
    base = jnp.concatenate([*parts, before(z)[zrows:]], axis=0)

    place = y * nx + x
    result = {}
    for dx, dy in got:
        target = (y ^ dy) * nx + (x ^ dx)
        total = base
        for ex, ey in got:
            source = (y ^ ey) * nx + (x ^ ex)
            total = total + jnp.where(source < target, wide[ex, ey], 0.0)
        total = total.astype(BF16)
        result[dx, dy] = total if (dx, dy) == (0, 0) else plane_swap(total, dx, dy)

    phi_w = {dx: weights(dx, phi_k[dx]) for dx in order_x}

    out = None
    for dx in range(nx):
        near = [result[dx, dy] for dy in range(ny)]
        far = [head_swap(a, 1) for a in near]
        whole = pl.BlockSpec((rows, count), lambda i, j, p: (0, 0))
        args = [pos, *phi_w[dx], v, other[dx], *near, *far]
        specs = [
            per_head(tokens, count),
            per_head(tokens, tokens),
            token_spec(dx),
            pl.BlockSpec((1, 1, rows, count), lambda i, j, p: (1 - i, j, 0, 0)),
            *[whole] * (cores * ny),
        ]
        kernel = functools.partial(output_kernel, group, size, ny)
        alias = {}
        if out is not None:
            args.append(out)
            specs.append(pl.BlockSpec(memory_space=pl.ANY))
            alias = {len(args) - 1: 0}
        out = call(
            kernel,
            specs,
            token_spec(dx),
            jax.ShapeDtypeStruct((tokens, width), BF16),
            2 * 2 * tokens * count * (2 * size) * own * cores,
            [pltpu.VMEM((rows, count), F32)],
            alias,
        )(*args)
    return out.reshape(queries.shape)


def solution(mesh):
    token = P(None, ("seq", "head"), None)
    return jax.shard_map(
        functools.partial(body, mesh.shape["seq"], mesh.shape["head"]),
        mesh=mesh,
        in_specs=(token, token, token, P("head", None, None)),
        out_specs=token,
        check_vma=False,
    )
```

time: 390 us -> 117 us (0.30); the launches traced: 383 us -> 116 us
  local copies, waits for them, and re-layouts: 119 us -> 6.43 us
  other arithmetic: 105 us -> 11.2 us
  blocking collectives: 61.3 us -> 0 us
  matrix products: 45.8 us -> 0 us
  Pallas kernels: 0 us -> 38.1 us
  waiting for transfers between devices: 24.4 us -> 41.6 us
  between operations: 14.1 us -> 0.19 us
  starting transfers between devices: 12.5 us -> 18.9 us
    unnamed x6 -> x4, other arithmetic: 79 us -> 0.14 us
    unnamed x34 -> x20, local copies, waits for them, and re-layouts: 84 us -> 6.4 us
    dot_general x7 -> x0, matrix products: 45.8 us -> none  [the longest x1 12.5 us: per_batch(): jnp.einsum('hsm,htm->hst', batch_q, batch_k, preferred_element_type=jnp.f...]
    ppermute x0 -> x21, waiting for transfers between devices: none -> 41.6 us  [the longest x11 18.1 us: head_swap(): return lax.ppermute(a, 'head', [(i, i ^ bits) for i in range(heads)])]
    pallas_call x0 -> x6, Pallas kernels: none -> 38.1 us  [the longest x2 13.8 us: weights(): call(functools.partial(weights_kernel, group, size), [token_spec(dx), *fe...]
    all_gather x1 -> x0, blocking collectives: 32 us -> none  [carried_in(): everything = jax.tree.map(lambda part: lax.all_gather(part, axis), shard)]
    all_to_all x1 -> x0, blocking collectives: 29.3 us -> none  [body(): lax.all_to_all(attended, 'head', split_axis=1, concat_axis=2, tiled=True)]
    all_to_all x3 -> x0, waiting for transfers between devices: 24.3 us -> none  [the longest x1 24.3 us: body(): lax.all_to_all(queries, 'head', split_axis=2, concat_axis=1, tiled=True)]
  transfers between devices with their start and end apart: 4 -> 21, of which waited for: 1 -> 12; matrix products, arithmetic and copies ran while one was open for 41% -> 4% of each run, Pallas kernels for 0% -> 28%
where the time goes in v1:
time: 117 us; the launch traced here: 116 us
  waiting for transfers between devices  41.6 us (36%)
  Pallas kernels  38.1 us (33%)
  starting transfers between devices  18.9 us (16%)
  other arithmetic  11.2 us (10%)
  local copies, waits for them, and re-layouts  6.43 us (5%)
    ppermute x11, waiting for transfers between devices, head_swap(): return lax.ppermute(a, 'head', [(i, i ^ bits) for i in range(heads)])  18.1 us
    ppermute x8, waiting for transfers between devices, seq_swap(): return lax.ppermute(a, 'seq', [(i, i ^ bits) for i in range(seqs)])  16.8 us
    pallas_call x2, Pallas kernels, weights(): call(functools.partial(weights_kernel, group, size), [token_spec(dx), *fe...  13.8 us
    pallas_call x2, Pallas kernels, states(): call(functools.partial(states_kernel, group, size), [token_spec(dx), toke...  13.7 us
    pallas_call x2, Pallas kernels, body(): call(kernel, specs, token_spec(dx), jax.ShapeDtypeStruct((tokens, width),...  10.6 us
    ppermute x8, starting transfers between devices, seq_swap(): return lax.ppermute(a, 'seq', [(i, i ^ bits) for i in range(seqs)])  8.76 us
    ppermute x2, waiting for transfers between devices, plane_swap(): return lax.ppermute(a, ('seq', 'head'), pairs)  6.64 us
    unnamed x20, local copies, waits for them, and re-layouts  6.4 us
  transfers between devices with their start and end apart: 21, of which 12 were waited for; matrix products, arithmetic and copies ran while one was open for 4% of the time, Pallas kernels for 28%

profile of v1, /device:TPU:0, one launch (start us, length us, event | category | flops | bytes accessed | tf_op | source)
XLA Modules:
  0.0 116.5 jit_solution(1122287242977726031)
XLA Ops:
  0.0 2.9 %collective-permute-start.4 = (bf16[8,256,128]{2,1,0:T(8,128)(2,1)}, bf16[8,256,128]{2,1,0:T(8,128)(2,1)S(1)}, u32[]{:S(2)}, u32[]{:S(2)}) collective-permute-start(bf16[8,256,128]{2,1,0:T(8,128)(2,1)} %f0.3), channel_id=1, source_target_pairs={{0,2},{1,3},{2,0},{3,1},{4,6},{5,7},{6,4},{7,5},{8,10},{9,11},{10,... | collective-permute-start | bytes 1572872 | tf_op jit(solution)/shard_map/ppermute | solution.py:123
  2.9 12.1 %collective-permute-done.4.f0 = bf16[8,256,128]{2,1,0:T(8,128)(2,1)S(1)} collective-permute-done((bf16[8,256,128]{2,1,0:T(8,128)(2,1)}, bf16[8,256,128]{2,1,0:T(8,128)(2,1)S(1)}, u32[]{:S(2)}, u32[]{:S(2)}) %collective-permute-start.4) | collective-permute-done | bytes 524320 | tf_op jit(solution)/shard_map/ppermute | solution.py:123
  16.2 6.9 %shard_map.46 = (bf16[2,2,4,256,256]{4,3,2,1,0:T(8,128)(2,1)S(1)}, bf16[2,2,528,256]{3,2,1,0:T(8,128)(2,1)S(1)}) custom-call(s32[3]{0:T(128)S(1)} %pad_add_fusion.pos, bf16[256,4096]{1,0:T(8,128)(2,1)} %bitcast.21, bf16[256,4096]{1,0:T(8,128)(2,1)} %bitcast.17, bf16[8,256,128]{2,1,0:T(8,128)(2,1)S(1)} %copy-done.4, ...), custom_call_target="tpu_custom_call" | custom-call | flops 536870912 | bytes 8388608 | tf_op jit(solution)/shard_map/pallas_call | solution.py:184
  24.9 6.9 %shard_map.48 = (bf16[2,2,4,256,256]{4,3,2,1,0:T(8,128)(2,1)S(1)}, bf16[2,2,528,256]{3,2,1,0:T(8,128)(2,1)S(1)}) custom-call(s32[3]{0:T(128)S(1)} %pad_add_fusion.pos, bf16[256,4096]{1,0:T(8,128)(2,1)} %bitcast.22, bf16[256,4096]{1,0:T(8,128)(2,1)} %bitcast.18, bf16[8,256,128]{2,1,0:T(8,128)(2,1)S(1)} %collective-permute-done.4.f0, ...), custom_call_target="tpu_custom_call" | custom-call | flops 536870912 | bytes 8388608 | tf_op jit(solution)/shard_map/pallas_call | solution.py:184
  31.8 1.3 %copy-done.2 = bf16[2,2,4,256,256]{4,3,2,1,0:T(8,128)(2,1)} copy-done((bf16[2,2,4,256,256]{4,3,2,1,0:T(8,128)(2,1)}, bf16[2,2,4,256,256]{4,3,2,1,0:T(8,128)(2,1)S(1)}, u32[]{:S(2)}) %copy-start.2) | copy-done | bytes 2097176
  34.4 1.7 %collective-permute-start.2 = (bf16[528,256]{1,0:T(8,128)(2,1)}, bf16[528,256]{1,0:T(8,128)(2,1)S(1)}, u32[]{:S(2)}, u32[]{:S(2)}) collective-permute-start(bf16[528,256]{1,0:T(8,128)(2,1)} %get-tuple-element.25), channel_id=1, source_target_pairs={{0,2},{1,3},{2,0},{3,1},{4,6},{5,7},{6,4},{7,5},{8,10},{9,11},{10,... | collective-permute-start | bytes 811016 | tf_op jit(solution)/shard_map/ppermute | solution.py:123
  36.1 1.5 %collective-permute-start.3 = (bf16[528,256]{1,0:T(8,128)(2,1)}, bf16[528,256]{1,0:T(8,128)(2,1)}, u32[]{:S(2)}, u32[]{:S(2)}) collective-permute-start(bf16[528,256]{1,0:T(8,128)(2,1)} %get-tuple-element.26), channel_id=1, source_target_pairs={{0,6},{1,7},{2,4},{3,5},{4,2},{5,3},{6,0},{7,1},{8,14},{9,15},{10,... | collective-permute-start | bytes 811016 | tf_op jit(solution)/shard_map/ppermute | solution.py:138
  38.6 5.2 %collective-permute-done.2 = bf16[528,256]{1,0:T(8,128)(2,1)S(1)} collective-permute-done((bf16[528,256]{1,0:T(8,128)(2,1)}, bf16[528,256]{1,0:T(8,128)(2,1)S(1)}, u32[]{:S(2)}, u32[]{:S(2)}) %collective-permute-start.2) | collective-permute-done | bytes 270368 | tf_op jit(solution)/shard_map/ppermute | solution.py:123
  43.9 6.6 %collective-permute-done.3 = bf16[528,256]{1,0:T(8,128)(2,1)} collective-permute-done((bf16[528,256]{1,0:T(8,128)(2,1)}, bf16[528,256]{1,0:T(8,128)(2,1)}, u32[]{:S(2)}, u32[]{:S(2)}) %collective-permute-start.3) | collective-permute-done | bytes 270368 | tf_op jit(solution)/shard_map/ppermute | solution.py:138
  50.5 2.2 %collective-permute-done.7 = bf16[528,256]{1,0:T(8,128)(2,1)} collective-permute-done((bf16[528,256]{1,0:T(8,128)(2,1)}, bf16[528,256]{1,0:T(8,128)(2,1)}, u32[]{:S(2)}, u32[]{:S(2)}) %collective-permute-start.7) | collective-permute-done | bytes 270368 | tf_op jit(solution)/shard_map/ppermute | solution.py:126
  52.7 2.0 %fusion.16 = (bf16[528,256]{1,0:T(8,128)(2,1)S(1)}, bf16[528,256]{1,0:T(8,128)(2,1)}) fusion(bf16[528,256]{1,0:T(8,128)(2,1)} %collective-permute-done.7, bf16[528,256]{1,0:T(8,128)(2,1)} %collective-permute-done.3, bf16[528,256]{1,0:T(8,128)(2,1)S(1)} %collective-permute-done.2, bf16[2,2,528,256]{3,2,1,0:T(8,128)(2,1)S(1)} %collective-permute-done.6.other, ...), kind=kLoop, calls=%fused_computation.31 | loop fusion | flops 1622016 | bytes 1892352 | tf_op jit(solution)/shard_map/convert_element_type | solution.py:222
  55.4 1.6 %collective-permute-start.8 = (bf16[144,256]{1,0:T(8,128)(2,1)}, bf16[144,256]{1,0:T(8,128)(2,1)}, u32[]{:S(2)}, u32[]{:S(2)}) collective-permute-start(bf16[144,256]{1,0:T(8,128)(2,1)} %get-tuple-element.39), channel_id=1, source_target_pairs={{0,8},{4,12},{8,0},{12,4},{16,24},{20,28},{24,16},{28,20},{1,9},{5... | collective-permute-start | bytes 221192 | tf_op jit(solution)/shard_map/ppermute | solution.py:126
  57.0 2.6 %collective-permute-start.9 = (bf16[144,256]{1,0:T(8,128)(2,1)}, bf16[144,256]{1,0:T(8,128)(2,1)}, u32[]{:S(2)}, u32[]{:S(2)}) collective-permute-start(bf16[144,256]{1,0:T(8,128)(2,1)} %get-tuple-element.40), channel_id=1, source_target_pairs={{0,16},{4,20},{8,24},{12,28},{16,0},{20,4},{24,8},{28,12},{1,17},{... | collective-permute-start | bytes 221192 | tf_op jit(solution)/shard_map/ppermute | solution.py:126
  61.7 2.4 %collective-permute-done.9 = bf16[144,256]{1,0:T(8,128)(2,1)} collective-permute-done((bf16[144,256]{1,0:T(8,128)(2,1)}, bf16[144,256]{1,0:T(8,128)(2,1)}, u32[]{:S(2)}, u32[]{:S(2)}) %collective-permute-start.9) | collective-permute-done | bytes 73760 | tf_op jit(solution)/shard_map/ppermute | solution.py:126
  68.0 2.7 %collective-permute-start.10 = (bf16[128,256]{1,0:T(8,128)(2,1)S(1)}, bf16[128,256]{1,0:T(8,128)(2,1)S(1)}, u32[]{:S(2)}, u32[]{:S(2)}) collective-permute-start(bf16[128,256]{1,0:T(8,128)(2,1)S(1)} %get-tuple-element.32), channel_id=1, source_target_pairs={{0,24},{4,28},{8,16},{12,20},{16,8},{20,12},{24,0},{28,4},{1,25},{... | collective-permute-start | bytes 196616 | tf_op jit(solution)/shard_map/ppermute | solution.py:126
  72.9 1.4 %collective-permute-done.10 = bf16[128,256]{1,0:T(8,128)(2,1)S(1)} collective-permute-done((bf16[128,256]{1,0:T(8,128)(2,1)S(1)}, bf16[128,256]{1,0:T(8,128)(2,1)S(1)}, u32[]{:S(2)}, u32[]{:S(2)}) %collective-permute-start.10) | collective-permute-done | bytes 65568 | tf_op jit(solution)/shard_map/ppermute | solution.py:126
  74.3 2.3 %collective-permute-done.12 = bf16[128,256]{1,0:T(8,128)(2,1)S(1)} collective-permute-done((bf16[128,256]{1,0:T(8,128)(2,1)S(1)}, bf16[128,256]{1,0:T(8,128)(2,1)S(1)}, u32[]{:S(2)}, u32[]{:S(2)}) %collective-permute-start.12) | collective-permute-done | bytes 65568 | tf_op jit(solution)/shard_map/ppermute | solution.py:126
  76.8 1.6 %fusion.11 = (bf16[528,256]{1,0:T(8,128)(2,1)S(1)}, bf16[528,256]{1,0:T(8,128)(2,1)S(1)}, bf16[528,256]{1,0:T(8,128)(2,1)S(1)}, bf16[528,256]{1,0:T(8,128)(2,1)S(1)}) fusion(f32[528,256]{1,0:T(8,128)S(1)} %slice_dynamic-update-slice_fusion, bf16[528,256]{1,0:T(8,128)(2,1)S(1)} %collective-permute-done.2, bf16[528,256]{1,0:T(8,128)(2,1)} %collective-permute-done.3, ...), kind=kLoop, calls=%fused_computation.26 | loop fusion | flops 4325376 | bytes 2703372 | tf_op jit(solution)/shard_map/convert_element_type | solution.py:258
  79.0 2.5 %collective-permute-start.15 = (bf16[528,256]{1,0:T(8,128)(2,1)S(1)}, bf16[528,256]{1,0:T(8,128)(2,1)S(1)}, u32[]{:S(2)}, u32[]{:S(2)}) collective-permute-start(bf16[528,256]{1,0:T(8,128)(2,1)S(1)} %get-tuple-element.29), channel_id=1, source_target_pairs={{0,6},{1,7},{2,4},{3,5},{4,2},{5,3},{6,0},{7,1},{8,14},{9,15},{10,... | collective-permute-start | bytes 811016 | tf_op jit(solution)/shard_map/ppermute | solution.py:138
  82.0 6.1 %collective-permute-done.18.rest_1_ = bf16[528,256]{1,0:T(8,128)(2,1)S(1)} collective-permute-done((bf16[528,256]{1,0:T(8,128)(2,1)S(1)}, bf16[528,256]{1,0:T(8,128)(2,1)S(1)}, u32[]{:S(2)}, u32[]{:S(2)}) %collective-permute-start.18) | collective-permute-done | bytes 270368 | tf_op jit(solution)/shard_map/ppermute | solution.py:126
  89.4 6.9 %shard_map.47 = (bf16[2,2,4,256,256]{4,3,2,1,0:T(8,128)(2,1)S(1)}, bf16[2,2,4,256,256]{4,3,2,1,0:T(8,128)(2,1)S(1)}) custom-call(s32[3]{0:T(128)S(1)} %pad_add_fusion.pos, bf16[256,4096]{1,0:T(8,128)(2,1)} %bitcast.23, bf16[8,256,128]{2,1,0:T(8,128)(2,1)S(1)} %copy-done.5, bf16[8,256,128]{2,1,0:T(8,128)(2,1)S(1)} %collective-permute-done.f1, ...), custom_call_target="tpu_custom_call" | custom-call | flops 805306368 | bytes 8388608 | tf_op jit(solution)/shard_map/pallas_call | solution.py:197
  97.6 6.9 %shard_map.49 = (bf16[2,2,4,256,256]{4,3,2,1,0:T(8,128)(2,1)S(1)}, bf16[2,2,4,256,256]{4,3,2,1,0:T(8,128)(2,1)S(1)}) custom-call(s32[3]{0:T(128)S(1)} %pad_add_fusion.pos, bf16[256,4096]{1,0:T(8,128)(2,1)} %bitcast.24, bf16[8,256,128]{2,1,0:T(8,128)(2,1)S(1)} %collective-permute-done.4.f0, bf16[8,256,128]{2,1,0:T(8,128)(2,1)S(1)} %copy-done.7, ...), custom_call_target="tpu_custom_call" | custom-call | flops 805306368 | bytes 8388608 | tf_op jit(solution)/shard_map/pallas_call | solution.py:197
  105.9 5.3 %shard_map.50.rest_4_ = bf16[256,4096]{1,0:T(8,128)(2,1)} custom-call(s32[3]{0:T(128)S(1)} %pad_add_fusion.pos, bf16[2,2,4,256,256]{4,3,2,1,0:T(8,128)(2,1)S(1)} %get-tuple-element.19.phi_q, bf16[2,2,4,256,256]{4,3,2,1,0:T(8,128)(2,1)} %copy-done.3, bf16[256,4096]{1,0:T(8,128)(2,1)} %bitcast.19, bf16[2,2,528,256]{3,2,1,0:T(8,128)(2,1)S(1)} %collective-permute-done.6.other, ...), custom_call_target="tpu_custom_call" | custom-call | flops 1073741824 | bytes 8388608 | tf_op jit(solution)/shard_map/pallas_call | solution.py:282
  111.2 5.3 %shard_map.51 = bf16[256,4096]{1,0:T(8,128)(2,1)} custom-call(s32[3]{0:T(128)S(1)} %pad_add_fusion.pos, bf16[2,2,4,256,256]{4,3,2,1,0:T(8,128)(2,1)S(1)} %get-tuple-element.14.phi_q, bf16[2,2,4,256,256]{4,3,2,1,0:T(8,128)(2,1)} %copy-done, bf16[256,4096]{1,0:T(8,128)(2,1)} %bitcast.20, ...), custom_call_target="tpu_custom_call", output_to_operand_aliasing={{}: (9, {})} | custom-call | flops 1073741824 | bytes 8388608 | tf_op jit(solution)/shard_map/pallas_call | solution.py:282
  (62 shorter events, 19.3 us)
Async XLA Ops:
  0.0 15.1 %collective-permute-start.4 = (bf16[8,256,128]{2,1,0:T(8,128)(2,1)}, bf16[8,256,128]{2,1,0:T(8,128)(2,1)S(1)}, u32[]{:S(2)}, u32[]{:S(2)}) collective-permute-start(bf16[8,256,128]{2,1,0:T(8,128)(2,1)} %f0.3), channel_id=1, source_target_pairs={{0,2},{1,3},{2,0},{3,1},{4,6},{5,7},{6,4},{7,5},{8,10},{9,11},{10,... | collective-permute-start | bytes 1572872 | tf_op jit(solution)/shard_map/ppermute | solution.py:123
  2.9 12.2 %collective-permute-start = (bf16[8,256,128]{2,1,0:T(8,128)(2,1)}, bf16[8,256,128]{2,1,0:T(8,128)(2,1)S(1)}, u32[]{:S(2)}, u32[]{:S(2)}) collective-permute-start(bf16[8,256,128]{2,1,0:T(8,128)(2,1)} %f0.3), channel_id=1, source_target_pairs={{0,1},{1,0},{2,3},{3,2},{4,5},{5,4},{6,7},{7,6},{8,9},{9,8},{10,11... | collective-permute-start | bytes 1572872 | tf_op jit(solution)/shard_map/ppermute | solution.py:123
  15.1 9.8 %collective-permute-start.5 = (bf16[8,256,128]{2,1,0:T(8,128)(2,1)S(1)}, bf16[8,256,128]{2,1,0:T(8,128)(2,1)S(1)}, u32[]{:S(2)}, u32[]{:S(2)}) collective-permute-start(bf16[8,256,128]{2,1,0:T(8,128)(2,1)S(1)} %collective-permute-done.4.f0), channel_id=1, source_target_pairs={{0,1},{1,0},{2,3},{3,2},{4,5},{5,4},{6,7},{7,6},{8,9},{9,8},{10,11... | collective-permute-start | bytes 1572872 | tf_op jit(solution)/shard_map/ppermute | solution.py:123
  24.4 8.8 %collective-permute-start.1 = (bf16[2,2,528,256]{3,2,1,0:T(8,128)(2,1)S(1)}, bf16[2,2,528,256]{3,2,1,0:T(8,128)(2,1)S(1)}, u32[]{:S(2)}, u32[]{:S(2)}) collective-permute-start(bf16[2,2,528,256]{3,2,1,0:T(8,128)(2,1)S(1)} %get-tuple-element.16), channel_id=1, source_target_pairs={{0,1},{1,0},{2,3},{3,2},{4,5},{5,4},{6,7},{7,6},{8,9},{9,8},{10,11... | collective-permute-start | bytes 3244040 | tf_op jit(solution)/shard_map/ppermute | solution.py:123
  33.2 4.4 %collective-permute-start.6 = (bf16[2,2,528,256]{3,2,1,0:T(8,128)(2,1)S(1)}, bf16[2,2,528,256]{3,2,1,0:T(8,128)(2,1)S(1)}, u32[]{:S(2)}, u32[]{:S(2)}) collective-permute-start(bf16[2,2,528,256]{3,2,1,0:T(8,128)(2,1)S(1)} %get-tuple-element.17), channel_id=1, source_target_pairs={{0,1},{1,0},{2,3},{3,2},{4,5},{5,4},{6,7},{7,6},{8,9},{9,8},{10,11... | collective-permute-start | bytes 3244040 | tf_op jit(solution)/shard_map/ppermute | solution.py:123
  34.4 9.5 %collective-permute-start.2 = (bf16[528,256]{1,0:T(8,128)(2,1)}, bf16[528,256]{1,0:T(8,128)(2,1)S(1)}, u32[]{:S(2)}, u32[]{:S(2)}) collective-permute-start(bf16[528,256]{1,0:T(8,128)(2,1)} %get-tuple-element.25), channel_id=1, source_target_pairs={{0,2},{1,3},{2,0},{3,1},{4,6},{5,7},{6,4},{7,5},{8,10},{9,11},{10,... | collective-permute-start | bytes 811016 | tf_op jit(solution)/shard_map/ppermute | solution.py:123
  36.1 14.4 %collective-permute-start.3 = (bf16[528,256]{1,0:T(8,128)(2,1)}, bf16[528,256]{1,0:T(8,128)(2,1)}, u32[]{:S(2)}, u32[]{:S(2)}) collective-permute-start(bf16[528,256]{1,0:T(8,128)(2,1)} %get-tuple-element.26), channel_id=1, source_target_pairs={{0,6},{1,7},{2,4},{3,5},{4,2},{5,3},{6,0},{7,1},{8,14},{9,15},{10,... | collective-permute-start | bytes 811016 | tf_op jit(solution)/shard_map/ppermute | solution.py:138
  38.4 14.3 %collective-permute-start.7 = (bf16[528,256]{1,0:T(8,128)(2,1)}, bf16[528,256]{1,0:T(8,128)(2,1)}, u32[]{:S(2)}, u32[]{:S(2)}) collective-permute-start(bf16[528,256]{1,0:T(8,128)(2,1)} %fusion.19), channel_id=1, source_target_pairs={{0,4},{4,0},{8,12},{12,8},{16,20},{20,16},{24,28},{28,24},{1,5},{5... | collective-permute-start | bytes 811016 | tf_op jit(solution)/shard_map/ppermute | solution.py:126
  55.4 5.4 %collective-permute-start.8 = (bf16[144,256]{1,0:T(8,128)(2,1)}, bf16[144,256]{1,0:T(8,128)(2,1)}, u32[]{:S(2)}, u32[]{:S(2)}) collective-permute-start(bf16[144,256]{1,0:T(8,128)(2,1)} %get-tuple-element.39), channel_id=1, source_target_pairs={{0,8},{4,12},{8,0},{12,4},{16,24},{20,28},{24,16},{28,20},{1,9},{5... | collective-permute-start | bytes 221192 | tf_op jit(solution)/shard_map/ppermute | solution.py:126
  57.0 7.2 %collective-permute-start.9 = (bf16[144,256]{1,0:T(8,128)(2,1)}, bf16[144,256]{1,0:T(8,128)(2,1)}, u32[]{:S(2)}, u32[]{:S(2)}) collective-permute-start(bf16[144,256]{1,0:T(8,128)(2,1)} %get-tuple-element.40), channel_id=1, source_target_pairs={{0,16},{4,20},{8,24},{12,28},{16,0},{20,4},{24,8},{28,12},{1,17},{... | collective-permute-start | bytes 221192 | tf_op jit(solution)/shard_map/ppermute | solution.py:126
  59.6 6.5 %collective-permute-start.11 = (bf16[144,256]{1,0:T(8,128)(2,1)}, bf16[144,256]{1,0:T(8,128)(2,1)}, u32[]{:S(2)}, u32[]{:S(2)}) collective-permute-start(bf16[144,256]{1,0:T(8,128)(2,1)} %get-tuple-element.38), channel_id=1, source_target_pairs={{0,24},{4,28},{8,16},{12,20},{16,8},{20,12},{24,0},{28,4},{1,25},{... | collective-permute-start | bytes 221192 | tf_op jit(solution)/shard_map/ppermute | solution.py:126
  59.8 17.0 %copy-start.9 = (bf16[528,256]{1,0:T(8,128)(2,1)S(1)}, bf16[528,256]{1,0:T(8,128)(2,1)}, u32[]{:S(2)}) copy-start(bf16[528,256]{1,0:T(8,128)(2,1)} %get-tuple-element.24) | copy-start | bytes 811012
  68.0 4.9 %collective-permute-start.13 = (bf16[128,256]{1,0:T(8,128)(2,1)S(1)}, bf16[128,256]{1,0:T(8,128)(2,1)S(1)}, u32[]{:S(2)}, u32[]{:S(2)}) collective-permute-start(bf16[128,256]{1,0:T(8,128)(2,1)S(1)} %get-tuple-element.31), channel_id=1, source_target_pairs={{0,8},{4,12},{8,0},{12,4},{16,24},{20,28},{24,16},{28,20},{1,9},{5... | collective-permute-start | bytes 196616 | tf_op jit(solution)/shard_map/ppermute | solution.py:126
  68.0 6.2 %collective-permute-start.10 = (bf16[128,256]{1,0:T(8,128)(2,1)S(1)}, bf16[128,256]{1,0:T(8,128)(2,1)S(1)}, u32[]{:S(2)}, u32[]{:S(2)}) collective-permute-start(bf16[128,256]{1,0:T(8,128)(2,1)S(1)} %get-tuple-element.32), channel_id=1, source_target_pairs={{0,24},{4,28},{8,16},{12,20},{16,8},{20,12},{24,0},{28,4},{1,25},{... | collective-permute-start | bytes 196616 | tf_op jit(solution)/shard_map/ppermute | solution.py:126
  70.7 5.9 %collective-permute-start.12 = (bf16[128,256]{1,0:T(8,128)(2,1)S(1)}, bf16[128,256]{1,0:T(8,128)(2,1)S(1)}, u32[]{:S(2)}, u32[]{:S(2)}) collective-permute-start(bf16[128,256]{1,0:T(8,128)(2,1)S(1)} %get-tuple-element.33), channel_id=1, source_target_pairs={{0,16},{4,20},{8,24},{12,28},{16,0},{20,4},{24,8},{28,12},{1,17},{... | collective-permute-start | bytes 196616 | tf_op jit(solution)/shard_map/ppermute | solution.py:126
  72.5 16.9 %copy-start.5 = (bf16[8,256,128]{2,1,0:T(8,128)(2,1)S(1)}, bf16[8,256,128]{2,1,0:T(8,128)(2,1)}, u32[]{:S(2)}) copy-start(bf16[8,256,128]{2,1,0:T(8,128)(2,1)} %f0.3) | copy-start | bytes 1572868
  78.4 9.7 %collective-permute-start.18 = (bf16[528,256]{1,0:T(8,128)(2,1)S(1)}, bf16[528,256]{1,0:T(8,128)(2,1)S(1)}, u32[]{:S(2)}, u32[]{:S(2)}) collective-permute-start(bf16[528,256]{1,0:T(8,128)(2,1)S(1)} %get-tuple-element.27), channel_id=1, source_target_pairs={{0,4},{4,0},{8,12},{12,8},{16,20},{20,16},{24,28},{28,24},{1,5},{5... | collective-permute-start | bytes 811016 | tf_op jit(solution)/shard_map/ppermute | solution.py:126
  79.0 9.1 %collective-permute-start.15 = (bf16[528,256]{1,0:T(8,128)(2,1)S(1)}, bf16[528,256]{1,0:T(8,128)(2,1)S(1)}, u32[]{:S(2)}, u32[]{:S(2)}) collective-permute-start(bf16[528,256]{1,0:T(8,128)(2,1)S(1)} %get-tuple-element.29), channel_id=1, source_target_pairs={{0,6},{1,7},{2,4},{3,5},{4,2},{5,3},{6,0},{7,1},{8,14},{9,15},{10,... | collective-permute-start | bytes 811016 | tf_op jit(solution)/shard_map/ppermute | solution.py:138
  81.4 7.9 %collective-permute-start.14 = (bf16[528,256]{1,0:T(8,128)(2,1)S(1)}, bf16[528,256]{1,0:T(8,128)(2,1)S(1)}, u32[]{:S(2)}, u32[]{:S(2)}) collective-permute-start(bf16[528,256]{1,0:T(8,128)(2,1)S(1)} %get-tuple-element.30), channel_id=1, source_target_pairs={{0,2},{1,3},{2,0},{3,1},{4,6},{5,7},{6,4},{7,5},{8,10},{9,11},{10,... | collective-permute-start | bytes 811016 | tf_op jit(solution)/shard_map/ppermute | solution.py:123
  82.0 23.9 %collective-permute-start.19 = (bf16[528,256]{1,0:T(8,128)(2,1)S(1)}, bf16[528,256]{1,0:T(8,128)(2,1)S(1)}, u32[]{:S(2)}, u32[]{:S(2)}) collective-permute-start(bf16[528,256]{1,0:T(8,128)(2,1)S(1)} %get-tuple-element.28.rest_0_), channel_id=1, source_target_pairs={{0,1},{1,0},{2,3},{3,2},{4,5},{5,4},{6,7},{7,6},{8,9},{9,8},{10,11... | collective-permute-start | bytes 811016 | tf_op jit(solution)/shard_map/ppermute | solution.py:123
  88.1 17.8 %collective-permute-start.20 = (bf16[528,256]{1,0:T(8,128)(2,1)S(1)}, bf16[528,256]{1,0:T(8,128)(2,1)S(1)}, u32[]{:S(2)}, u32[]{:S(2)}) collective-permute-start(bf16[528,256]{1,0:T(8,128)(2,1)S(1)} %collective-permute-done.18.rest_1_), channel_id=1, source_target_pairs={{0,1},{1,0},{2,3},{3,2},{4,5},{5,4},{6,7},{7,6},{8,9},{9,8},{10,11... | collective-permute-start | bytes 811016 | tf_op jit(solution)/shard_map/ppermute | solution.py:123
  88.1 23.1 %collective-permute-start.17 = (bf16[528,256]{1,0:T(8,128)(2,1)S(1)}, bf16[528,256]{1,0:T(8,128)(2,1)S(1)}, u32[]{:S(2)}, u32[]{:S(2)}) collective-permute-start(bf16[528,256]{1,0:T(8,128)(2,1)S(1)} %collective-permute-done.15.rest_1_), channel_id=1, source_target_pairs={{0,1},{1,0},{2,3},{3,2},{4,5},{5,4},{6,7},{7,6},{8,9},{9,8},{10,11... | collective-permute-start | bytes 811016 | tf_op jit(solution)/shard_map/ppermute | solution.py:123
  89.4 21.8 %collective-permute-start.16 = (bf16[528,256]{1,0:T(8,128)(2,1)S(1)}, bf16[528,256]{1,0:T(8,128)(2,1)S(1)}, u32[]{:S(2)}, u32[]{:S(2)}) collective-permute-start(bf16[528,256]{1,0:T(8,128)(2,1)S(1)} %collective-permute-done.14.rest_0_), channel_id=1, source_target_pairs={{0,1},{1,0},{2,3},{3,2},{4,5},{5,4},{6,7},{7,6},{8,9},{9,8},{10,11... | collective-permute-start | bytes 811016 | tf_op jit(solution)/shard_map/ppermute | solution.py:123
  89.4 8.2 %copy-start.7 = (bf16[8,256,128]{2,1,0:T(8,128)(2,1)S(1)}, bf16[8,256,128]{2,1,0:T(8,128)(2,1)}, u32[]{:S(2)}) copy-start(bf16[8,256,128]{2,1,0:T(8,128)(2,1)} %copy-done.6) | copy-start | bytes 1572868
  (7 other events, 17.7 us)

commit v2 on v0

v2 whole, which is shorter than its diff:
```python
import functools
import math

import jax
import jax.numpy as jnp
from jax import lax
from jax.experimental import pallas as pl
from jax.experimental.pallas import tpu as pltpu
from jax.sharding import PartitionSpec as P

F32, BF16 = jnp.float32, jnp.bfloat16
LOG2E = math.log2(math.e)
TOTAL_ROWS = 16
VMEM = 12 * 1024 * 1024


def feature_map(x, w):
    size, count = x.shape[1], w.shape[0]
    c = size ** (-0.25)
    p = lax.dot_general(x, w, (((1,), (1,)), ((), ())), preferred_element_type=F32)
    wide = x.astype(F32)
    square = jnp.sum(wide * wide, axis=1, keepdims=True)
    r = lax.rsqrt(square / size + 1e-06)
    half = square * r * r * (0.5 * c * c * LOG2E) + 0.5 * math.log2(count)
    ww = w.astype(F32)
    ww = ww * ww
    high = ww.astype(BF16)
    low = (ww - high.astype(F32)).astype(BF16)
    ones = jnp.ones((16, size), BF16)
    nt = (((1,), (1,)), ((), ()))
    total = lax.dot_general(ones, high, nt, preferred_element_type=F32)
    total = total + lax.dot_general(ones, low, nt, preferred_element_type=F32)
    s = lax.rsqrt(total[:1] / size + 1e-06)
    return jnp.exp2(p * (r * (c * LOG2E)) * s - half).astype(BF16)


def place_of(pos, key, nx, ny, core):
    flip = 1 if nx > 1 else 0
    part = pos[2] ^ key[1]
    return ((pos[0] ^ key[0] ^ flip) * 2 + (pos[1] ^ core)) * ny + part, part


def heads_of(pos, key, shape, f0, f1):
    nx, ny, group, size = shape
    for core, f in ((1, f1), (0, f0)):
        place, part = place_of(pos, key, nx, ny, core)
        first = 0 if f.shape[0] == group else part * group
        for h in range(group):
            start = pl.multiple_of((place * group + h) * size, size)
            yield (1 - core) * group + h, pl.ds(start, size), f, first + h


def states_kernel(key, shape, pos, k, v, f0, f1, *rest):
    phi, other, mine = rest[-3:]
    group, size = shape[2:]
    heads = list(heads_of(pos, key, shape, f0, f1))
    totals = []
    for i, cols, f, at in heads:
        ph = feature_map(k[:, cols], f[at])
        phi[i] = ph
        totals.append(jnp.sum(ph.astype(F32), axis=0, keepdims=True))
    for i, cols, _, _ in heads:
        out, h = (mine if i >= group else other), i % group
        st = lax.dot_general(
            v[:, cols], phi[i], (((0,), (0,)), ((), ())), preferred_element_type=F32
        )
        out[h * size : (h + 1) * size] = st.astype(BF16)
    pad = jnp.zeros((TOTAL_ROWS - group, totals[0].shape[1]), F32)
    other[group * size :] = jnp.concatenate([*totals[:group], pad], axis=0).astype(BF16)
    mine[group * size :] = jnp.concatenate([*totals[group:], pad], axis=0).astype(BF16)


def weights_kernel(key, shape, pos, q, f0, f1, phi_k, *rest):
    phi_q, weights = rest[-2:]
    tokens = q.shape[0]
    heads = list(heads_of(pos, key, shape, f0, f1))
    for i, cols, f, at in heads:
        phi_q[i] = feature_map(q[:, cols], f[at])
    row = lax.broadcasted_iota(jnp.int32, (tokens, tokens), 0)
    col = lax.broadcasted_iota(jnp.int32, (tokens, tokens), 1)
    mask = col <= row
    for i, _, _, _ in heads:
        sc = lax.dot_general(
            phi_q[i], phi_k[i], (((1,), (1,)), ((), ())), preferred_element_type=F32
        )
        weights[i] = jnp.where(mask, sc, 0.0).astype(BF16)


def output_kernel(key, shape, pos, phi_q, weights, v, far, far_add, near, near_add, *rest):
    out, held, ready, sems = rest[-4:]
    nx, ny, group, size = shape
    tokens, count = phi_q.shape[-2:]
    add = (pos[1] == 1).astype(F32)
    ones = jnp.ones((tokens, size), BF16)
    copies = []
    for half, (base, extra) in enumerate(((far, far_add), (near, near_add))):
        place = place_of(pos, key, nx, ny, 1 - half)[0]
        held[half] = (base[...].astype(F32) + add * extra[...].astype(F32)).astype(BF16)
        totals = held[half, group * size :].astype(F32)
        for h in range(group):
            st = held[half, h * size : (h + 1) * size]
            tot = jnp.broadcast_to(totals[h : h + 1], (size, count)).astype(BF16)
            acc = lax.dot_general(
                phi_q[half * group + h],
                jnp.concatenate([st, tot], axis=0),
                (((1,), (1,)), ((), ())),
                preferred_element_type=F32,
            )
            start = pl.multiple_of((place * group + h) * size, size)
            acc = acc + jnp.dot(
                weights[half * group + h],
                jnp.concatenate([v[:, pl.ds(start, size)], ones], axis=1),
                preferred_element_type=F32,
            )
            ready[half, :, h * size : (h + 1) * size] = (acc[:, :size] / acc[:, size:]).astype(BF16)
        wide = group * size
        copy = pltpu.make_async_copy(
            ready.at[half],
            out.at[:, pl.ds(pl.multiple_of(place * wide, wide), wide)],
            sems.at[half],
        )
        copy.start()
        copies.append(copy)
    for copy in copies:
        copy.wait()


def plane_kernel(count, zrows, pos, *refs):
    held, z = refs[-1], pos[3]
    pieces, outs = refs[:count], refs[-1 - (held.shape[0] - TOTAL_ROWS) // zrows : -1]
    total = pieces[0][...].astype(F32)
    for piece in pieces[1:]:
        total = total + piece[...].astype(F32)
    held[...] = total
    srows = len(outs) * zrows
    for j, out in enumerate(outs):
        start = pl.multiple_of((z ^ j) * zrows, zrows)
        out[:zrows] = held[pl.ds(start, zrows)].astype(BF16)
        out[zrows:] = held[srows:].astype(BF16)


def prefix_kernel(count, zrows, pos, *refs):
    heard, outs, totals = refs[:count], refs[-1 - count : -1], refs[-1]
    z = pos[3]
    for j, out in enumerate(outs):
        total = jnp.zeros(out.shape, F32)
        for i, part in enumerate(heard):
            total = total + jnp.where((z ^ i) < (z ^ j), part[:zrows].astype(F32), 0.0)
        out[...] = total.astype(BF16)
    total = jnp.zeros(totals.shape, F32)
    for i, part in enumerate(heard):
        total = total + jnp.where((z ^ i) < z, part[zrows:].astype(F32), 0.0)
    totals[...] = total


def place_kernel(nx, ny, count, zrows, pos, *refs):
    keys = [(dx, dy) for dx in range(nx) for dy in range(ny)]
    prefix, totals = refs[:count], refs[count]
    pieces, outs = refs[count + 1 : count + 1 + len(keys)], refs[-1 - len(keys) : -1]
    held = refs[-1]
    x, y, z = pos[0], pos[2], pos[3]
    for j in range(count):
        start = pl.multiple_of((z ^ j) * zrows, zrows)
        held[pl.ds(start, zrows)] = prefix[j][...].astype(F32)
    held[count * zrows :] = totals[...]
    for (dx, dy), out in zip(keys, outs):
        target = (y ^ dy) * nx + (x ^ dx)
        total = held[...]
        for (ex, ey), piece in zip(keys, pieces):
            source = (y ^ ey) * nx + (x ^ ex)
            total = total + jnp.where(source < target, piece[...].astype(F32), 0.0)
        out[...] = total.astype(BF16)


def body(seqs, heads, queries, keys, values, features):
    tokens, width = queries.shape[1:]
    q, k, v = (a.reshape(tokens, width) for a in (queries, keys, values))
    own, count, size = features.shape
    cores = 2
    nx = heads // cores
    ny = nx if seqs % nx == 0 else 1
    nz = seqs // ny
    flip = 1 if nx > 1 else 0
    group = own // ny
    srows = group * size
    zrows = srows // nz
    rows = srows + TOTAL_ROWS
    plane = [(dx, dy) for dx in range(nx) for dy in range(ny)]

    hi, si = lax.axis_index("head"), lax.axis_index("seq")
    x, c = hi // cores, hi % cores
    z, y = si // ny, si % ny
    pos = jnp.stack([x, c, y, z]).astype(jnp.int32)

    def head_swap(a, bits):
        return lax.ppermute(a, "head", [(i, i ^ bits) for i in range(heads)])

    def seq_swap(a, bits):
        return lax.ppermute(a, "seq", [(i, i ^ bits) for i in range(seqs)])

    def plane_swap(a, dx, dy):
        if dy == 0:
            return head_swap(a, dx * cores)
        if dx == 0:
            return seq_swap(a, dy)
        pairs = [
            (s * heads + h, (s ^ dy) * heads + (h ^ (dx * cores)))
            for s in range(seqs)
            for h in range(heads)
        ]
        return lax.ppermute(a, ("seq", "head"), pairs)

    anywhere = pl.BlockSpec(memory_space=pl.ANY)

    shape = (nx, ny, group, size)
    near, smem = pl.BlockSpec(memory_space=pltpu.VMEM), pl.BlockSpec(memory_space=pltpu.SMEM)

    def call(kernel, out, args, after=(), outs=near, scratch=(), alias={}):
        return pl.pallas_call(
            kernel,
            out_shape=out,
            in_specs=[smem] + [near] * len(args) + [anywhere] * len(after),
            out_specs=jax.tree.map(lambda _: outs, out),
            scratch_shapes=scratch,
            input_output_aliases=alias,
            compiler_params=pltpu.CompilerParams(vmem_limit_bytes=VMEM),
        )(pos, *args, *after)

    def per_head(a, b):
        return jax.ShapeDtypeStruct((cores * group, a, b), BF16)

    whole = jax.ShapeDtypeStruct((rows, count), BF16)

    dirs, phi_k, phi_w, piece, got, theirs = {}, {}, {}, {}, {}, {}

    def states(key, after=()):
        phi_k[key], other, mine = call(
            functools.partial(states_kernel, key, shape),
            [per_head(tokens, count), whole, whole],
            [k, v, *dirs[key]],
            after,
        )
        theirs[key] = [head_swap(other, 1), head_swap(mine, 1)]
        piece[key] = (mine.astype(F32) + theirs[key][0].astype(F32)).astype(BF16)
        got[key] = piece[key] if key == (0, 0) else plane_swap(piece[key], *key)
        return mine

    def weights(key, after=()):
        phi_w[key] = call(
            functools.partial(weights_kernel, key, shape),
            [per_head(tokens, count), per_head(tokens, tokens)],
            [q, *dirs[key], phi_k[key]],
            after,
        )
        return phi_w[key][0]

    near_dirs = head_swap(features, 1)
    for dy in range(ny):
        dirs[flip, dy] = (features, near_dirs)
    for ox in range(1, nx):
        if ny == 2:
            part = lax.dynamic_slice_in_dim(features, (y ^ 1) * group, group, 0)
            part = head_swap(part, ox * cores)
            rest = seq_swap(part, 1)
            dirs[ox ^ flip, 1] = (part, head_swap(part, 1))
            dirs[ox ^ flip, 0] = (rest, head_swap(rest, 1))
        else:
            full = head_swap(features, ox * cores)
            full = (full, head_swap(full, 1))
            for dy in range(ny):
                dirs[ox ^ flip, dy] = full

    first = [(flip, dy) for dy in range(ny)]
    later = [(dx, dy) for dx in range(nx) for dy in reversed(range(ny)) if dx != flip]
    for key in first:
        last = states(key)
    for i, key in enumerate(later):
        last = states(key, [piece[first[min(i, ny - 1)]]])

    done = weights(first[0], [last])
    summed = call(
        functools.partial(plane_kernel, len(plane), zrows),
        [jax.ShapeDtypeStruct((zrows + TOTAL_ROWS, count), BF16)] * nz,
        [got[key] for key in plane],
        [done],
        scratch=[pltpu.VMEM((rows, count), F32)],
    )
    heard = [a if j == 0 else seq_swap(a, j * ny) for j, a in enumerate(summed)]
    done = [weights(key, [summed[-1]]) for key in [*first[1:], *later[:-1]]]
    *prefix, totals = call(
        functools.partial(prefix_kernel, nz, zrows),
        [jax.ShapeDtypeStruct((zrows, count), BF16)] * nz
        + [jax.ShapeDtypeStruct((TOTAL_ROWS, count), F32)],
        heard,
        done,
    )
    done = [weights(later[-1], [prefix[-1]])] if later else []
    prefix = [a if j == 0 else seq_swap(a, j * ny) for j, a in enumerate(prefix)]
    placed = call(
        functools.partial(place_kernel, nx, ny, nz, zrows),
        [whole] * len(plane),
        [*prefix, totals, *[got[key] for key in plane]],
        done,
        scratch=[pltpu.VMEM((rows, count), F32)],
    )

    out = None
    for key, base in zip(plane, placed):
        if key != (0, 0):
            base = plane_swap(base, *key)
        args = [*phi_w[key], v, head_swap(base, 1), theirs[key][1], base, theirs[key][0]]
        out = call(
            functools.partial(output_kernel, key, shape),
            jax.ShapeDtypeStruct((tokens, width), BF16),
            args,
            [] if out is None else [out],
            anywhere,
            [
                pltpu.VMEM((cores, rows, count), BF16),
                pltpu.VMEM((cores, tokens, group * size), BF16),
                pltpu.SemaphoreType.DMA((cores,)),
            ],
            {} if out is None else {1 + len(args): 0},
        )
    return out.reshape(queries.shape)


def solution(mesh):
    token = P(None, ("seq", "head"), None)
    return jax.shard_map(
        functools.partial(body, mesh.shape["seq"], mesh.shape["head"]),
        mesh=mesh,
        in_specs=(token, token, token, P("head", None, None)),
        out_specs=token,
        check_vma=False,
    )
```

time: 390 us -> 87.4 us (0.22); the launches traced: 383 us -> 87.1 us
  local copies, waits for them, and re-layouts: 119 us -> 5.22 us
  other arithmetic: 105 us -> 0.37 us
  blocking collectives: 61.3 us -> 0 us
  matrix products: 45.8 us -> 0 us
  Pallas kernels: 0 us -> 26.7 us
  between operations: 14.1 us -> 0.42 us
  starting transfers between devices: 12.5 us -> 23.4 us
  waiting for transfers between devices: 24.4 us -> 31 us
    unnamed x34 -> x14, local copies, waits for them, and re-layouts: 84 us -> 4.25 us
    unnamed x6 -> x0, other arithmetic: 79 us -> none
    dot_general x7 -> x0, matrix products: 45.8 us -> none  [the longest x1 12.5 us: per_batch(): jnp.einsum('hsm,htm->hst', batch_q, batch_k, preferred_element_type=jnp.f...]
    all_gather x1 -> x0, blocking collectives: 32 us -> none  [carried_in(): everything = jax.tree.map(lambda part: lax.all_gather(part, axis), shard)]
    ppermute x0 -> x29, waiting for transfers between devices: none -> 31 us  [the longest x9 14.1 us: seq_swap(): return lax.ppermute(a, 'seq', [(i, i ^ bits) for i in range(seqs)])]
    all_to_all x1 -> x0, blocking collectives: 29.3 us -> none  [body(): lax.all_to_all(attended, 'head', split_axis=1, concat_axis=2, tiled=True)]
    pallas_call x0 -> x15, Pallas kernels: none -> 26.7 us  [call(): pl.pallas_call(kernel, out_shape=out, in_specs=[smem] + [near] * len(args...]
    all_to_all x3 -> x0, waiting for transfers between devices: 24.3 us -> none  [the longest x1 24.3 us: body(): lax.all_to_all(queries, 'head', split_axis=2, concat_axis=1, tiled=True)]
  transfers between devices with their start and end apart: 4 -> 29, of which waited for: 1 -> 12; matrix products, arithmetic and copies ran while one was open for 41% -> 2% of each run, Pallas kernels for 0% -> 28%
where the time goes in v2:
time: 87.4 us; the launch traced here: 87.1 us
  waiting for transfers between devices  31 us (35%)
  Pallas kernels  26.7 us (31%)
  starting transfers between devices  23.4 us (27%)
  local copies, waits for them, and re-layouts  5.22 us (6%)
    pallas_call x15, Pallas kernels, call(): pl.pallas_call(kernel, out_shape=out, in_specs=[smem] + [near] * len(args...  26.7 us
    ppermute x9, waiting for transfers between devices, seq_swap(): return lax.ppermute(a, 'seq', [(i, i ^ bits) for i in range(seqs)])  14.1 us
    ppermute x2, waiting for transfers between devices, plane_swap(): return lax.ppermute(a, ('seq', 'head'), pairs)  12.6 us
    ppermute x9, starting transfers between devices, seq_swap(): return lax.ppermute(a, 'seq', [(i, i ^ bits) for i in range(seqs)])  11.5 us
    ppermute x18, starting transfers between devices, head_swap(): return lax.ppermute(a, 'head', [(i, i ^ bits) for i in range(heads)])  8.79 us
    ppermute x18, waiting for transfers between devices, head_swap(): return lax.ppermute(a, 'head', [(i, i ^ bits) for i in range(heads)])  4.35 us
    unnamed x14, local copies, waits for them, and re-layouts  4.25 us
    ppermute x2, starting transfers between devices, plane_swap(): return lax.ppermute(a, ('seq', 'head'), pairs)  3.08 us
  transfers between devices with their start and end apart: 29, of which 12 were waited for; matrix products, arithmetic and copies ran while one was open for 2% of the time, Pallas kernels for 28%

profile of v2, /device:TPU:0, one launch (start us, length us, event | category | flops | bytes accessed | tf_op | source)
XLA Modules:
  0.0 87.1 jit_solution(10360599708956299665)
XLA Ops:
  1.4 2.6 %collective-permute-start.1 = (bf16[4,256,128]{2,1,0:T(8,128)(2,1)S(1)}, bf16[4,256,128]{2,1,0:T(8,128)(2,1)S(1)}, u32[]{:S(2)}, u32[]{:S(2)}) collective-permute-start(bf16[4,256,128]{2,1,0:T(8,128)(2,1)S(1)} %constant_dynamic-slice_fusion), channel_id=1, source_target_pairs={{0,2},{1,3},{2,0},{3,1},{4,6},{5,7},{6,4},{7,5},{8,10},{9,11},{10,... | collective-permute-start | bytes 786440 | tf_op jit(solution)/shard_map/ppermute | solution.py:196
  8.3 2.0 %shard_map.48 = (bf16[8,256,256]{2,1,0:T(8,128)(2,1)S(1)}, bf16[528,256]{1,0:T(8,128)(2,1)S(1)}, bf16[528,256]{1,0:T(8,128)(2,1)S(1)}) custom-call(s32[4]{0:T(128)S(1)} %pad_add_fusion.pos, bf16[256,4096]{1,0:T(8,128)(2,1)S(1)} %bitcast.16, bf16[256,4096]{1,0:T(8,128)(2,1)S(1)} %bitcast.8, bf16[8,256,128]{2,1,0:T(8,128)(2,1)S(1)} %copy-done.5, ...), custom_call_target="tpu_custom_call" | custom-call | tf_op jit(solution)/shard_map/pallas_call | solution.py:219
  11.0 1.8 %collective-permute-start.2 = (bf16[4,256,128]{2,1,0:T(8,128)(2,1)S(1)}, bf16[4,256,128]{2,1,0:T(8,128)(2,1)S(1)}, u32[]{:S(2)}, u32[]{:S(2)}) collective-permute-start(bf16[4,256,128]{2,1,0:T(8,128)(2,1)S(1)} %collective-permute-done.1.f0), channel_id=1, source_target_pairs={{0,4},{4,0},{8,12},{12,8},{16,20},{20,16},{24,28},{28,24},{1,5},{5... | collective-permute-start | bytes 786440 | tf_op jit(solution)/shard_map/ppermute | solution.py:199
  12.7 2.0 %shard_map.46 = (bf16[8,256,256]{2,1,0:T(8,128)(2,1)S(1)}, bf16[528,256]{1,0:T(8,128)(2,1)S(1)}, bf16[528,256]{1,0:T(8,128)(2,1)S(1)}) custom-call(s32[4]{0:T(128)S(1)} %pad_add_fusion.pos, bf16[256,4096]{1,0:T(8,128)(2,1)S(1)} %bitcast.17, bf16[256,4096]{1,0:T(8,128)(2,1)S(1)} %bitcast.9, bf16[8,256,128]{2,1,0:T(8,128)(2,1)S(1)} %copy-done.5, ...), custom_call_target="tpu_custom_call" | custom-call | tf_op jit(solution)/shard_map/pallas_call | solution.py:219
  15.1 2.0 %shard_map.49 = (bf16[8,256,256]{2,1,0:T(8,128)(2,1)S(1)}, bf16[528,256]{1,0:T(8,128)(2,1)S(1)}, bf16[528,256]{1,0:T(8,128)(2,1)S(1)}) custom-call(s32[4]{0:T(128)S(1)} %pad_add_fusion.pos, bf16[256,4096]{1,0:T(8,128)(2,1)S(1)} %bitcast.18, bf16[256,4096]{1,0:T(8,128)(2,1)S(1)} %bitcast.10, bf16[4,256,128]{2,1,0:T(8,128)(2,1)S(1)} %collective-permute-done.1.f0, ...), custom_call_target="tpu_custom_call" | custom-call | tf_op jit(solution)/shard_map/pallas_call | solution.py:219
  17.5 2.2 %collective-permute-done.2.f0 = bf16[4,256,128]{2,1,0:T(8,128)(2,1)S(1)} collective-permute-done((bf16[4,256,128]{2,1,0:T(8,128)(2,1)S(1)}, bf16[4,256,128]{2,1,0:T(8,128)(2,1)S(1)}, u32[]{:S(2)}, u32[]{:S(2)}) %collective-permute-start.2) | collective-permute-done | bytes 262176 | tf_op jit(solution)/shard_map/ppermute | solution.py:199
  19.7 1.7 %collective-permute-start.10 = (bf16[528,256]{1,0:T(8,128)(2,1)S(1)}, bf16[528,256]{1,0:T(8,128)(2,1)S(1)}, u32[]{:S(2)}, u32[]{:S(2)}) collective-permute-start(bf16[528,256]{1,0:T(8,128)(2,1)S(1)} %add_convert_fusion.1.rest_0_), channel_id=1, source_target_pairs={{0,2},{1,3},{2,0},{3,1},{4,6},{5,7},{6,4},{7,5},{8,10},{9,11},{10,... | collective-permute-start | bytes 811016 | tf_op jit(solution)/shard_map/ppermute | solution.py:196
  23.1 2.0 %shard_map.47 = (bf16[8,256,256]{2,1,0:T(8,128)(2,1)S(1)}, bf16[528,256]{1,0:T(8,128)(2,1)S(1)}, bf16[528,256]{1,0:T(8,128)(2,1)S(1)}) custom-call(s32[4]{0:T(128)S(1)} %pad_add_fusion.pos, bf16[256,4096]{1,0:T(8,128)(2,1)S(1)} %bitcast.19, bf16[256,4096]{1,0:T(8,128)(2,1)S(1)} %bitcast.11, bf16[4,256,128]{2,1,0:T(8,128)(2,1)S(1)} %collective-permute-done.2.f0, ...), custom_call_target="tpu_custom_call" | custom-call | tf_op jit(solution)/shard_map/pallas_call | solution.py:219
  25.9 1.8 %shard_map.50 = (bf16[8,256,256]{2,1,0:T(8,128)(2,1)S(1)}, bf16[8,256,256]{2,1,0:T(8,128)(2,1)S(1)}) custom-call(s32[4]{0:T(128)S(1)} %pad_add_fusion.pos, bf16[256,4096]{1,0:T(8,128)(2,1)S(1)} %bitcast.20, bf16[8,256,128]{2,1,0:T(8,128)(2,1)S(1)} %copy-done.6, bf16[8,256,128]{2,1,0:T(8,128)(2,1)S(1)} %collective-permute-done.f1, ...), custom_call_target="tpu_custom_call" | custom-call | tf_op jit(solution)/shard_map/pallas_call | solution.py:219
  29.0 6.7 %collective-permute-done.11.refs_3_.refs_8_ = bf16[528,256]{1,0:T(8,128)(2,1)S(1)} collective-permute-done((bf16[528,256]{1,0:T(8,128)(2,1)S(1)}, bf16[528,256]{1,0:T(8,128)(2,1)S(1)}, u32[]{:S(2)}, u32[]{:S(2)}) %collective-permute-start.11) | collective-permute-done | bytes 270368 | tf_op jit(solution)/shard_map/ppermute | solution.py:211
  35.7 4.3 %collective-permute-done.9.refs_1_.refs_6_ = bf16[528,256]{1,0:T(8,128)(2,1)S(1)} collective-permute-done((bf16[528,256]{1,0:T(8,128)(2,1)S(1)}, bf16[528,256]{1,0:T(8,128)(2,1)S(1)}, u32[]{:S(2)}, u32[]{:S(2)}) %collective-permute-start.9) | collective-permute-done | bytes 270368 | tf_op jit(solution)/shard_map/ppermute | solution.py:199
  42.4 2.6 %collective-permute-start.13 = (bf16[144,256]{1,0:T(8,128)(2,1)S(1)}, bf16[144,256]{1,0:T(8,128)(2,1)S(1)}, u32[]{:S(2)}, u32[]{:S(2)}) collective-permute-start(bf16[144,256]{1,0:T(8,128)(2,1)S(1)} %get-tuple-element.54), channel_id=1, source_target_pairs={{0,16},{4,20},{8,24},{12,28},{16,0},{20,4},{24,8},{28,12},{1,17},{... | collective-permute-start | bytes 221192 | tf_op jit(solution)/shard_map/ppermute | solution.py:199
  45.2 1.8 %shard_map.53 = (bf16[8,256,256]{2,1,0:T(8,128)(2,1)S(1)}, bf16[8,256,256]{2,1,0:T(8,128)(2,1)S(1)}) custom-call(s32[4]{0:T(128)S(1)} %pad_add_fusion.pos, bf16[256,4096]{1,0:T(8,128)(2,1)S(1)} %bitcast.21, bf16[4,256,128]{2,1,0:T(8,128)(2,1)S(1)} %collective-permute-done.1.f0, bf16[4,256,128]{2,1,0:T(8,128)(2,1)S(1)} %collective-permute-done.6.f1, ...), custom_call_target="tpu_custom_call" | custom-call | tf_op jit(solution)/shard_map/pallas_call | solution.py:219
  47.0 1.8 %shard_map.52 = (bf16[8,256,256]{2,1,0:T(8,128)(2,1)S(1)}, bf16[8,256,256]{2,1,0:T(8,128)(2,1)S(1)}) custom-call(s32[4]{0:T(128)S(1)} %pad_add_fusion.pos, bf16[256,4096]{1,0:T(8,128)(2,1)S(1)} %bitcast.22, bf16[8,256,128]{2,1,0:T(8,128)(2,1)S(1)} %copy-done.6, bf16[8,256,128]{2,1,0:T(8,128)(2,1)S(1)} %collective-permute-done.f1, ...), custom_call_target="tpu_custom_call" | custom-call | tf_op jit(solution)/shard_map/pallas_call | solution.py:219
  54.7 1.7 %collective-permute-start.17 = (bf16[128,256]{1,0:T(8,128)(2,1)S(1)}, bf16[128,256]{1,0:T(8,128)(2,1)S(1)}, u32[]{:S(2)}, u32[]{:S(2)}) collective-permute-start(bf16[128,256]{1,0:T(8,128)(2,1)S(1)} %get-tuple-element.60.rest_0_), channel_id=1, source_target_pairs={{0,24},{4,28},{8,16},{12,20},{16,8},{20,12},{24,0},{28,4},{1,25},{... | collective-permute-start | bytes 196616 | tf_op jit(solution)/shard_map/ppermute | solution.py:199
  56.4 2.0 %shard_map.55 = (bf16[8,256,256]{2,1,0:T(8,128)(2,1)S(1)}, bf16[8,256,256]{2,1,0:T(8,128)(2,1)S(1)}) custom-call(s32[4]{0:T(128)S(1)} %pad_add_fusion.pos, bf16[256,4096]{1,0:T(8,128)(2,1)S(1)} %bitcast.23, bf16[4,256,128]{2,1,0:T(8,128)(2,1)S(1)} %collective-permute-done.2.f0, bf16[4,256,128]{2,1,0:T(8,128)(2,1)S(1)} %collective-permute-done.3.f1, ...), custom_call_target="tpu_custom_call" | custom-call | tf_op jit(solution)/shard_map/pallas_call | solution.py:219
  60.8 1.8 %shard_map.56 = (bf16[528,256]{1,0:T(8,128)(2,1)S(1)}, bf16[528,256]{1,0:T(8,128)(2,1)S(1)}, bf16[528,256]{1,0:T(8,128)(2,1)S(1)}, bf16[528,256]{1,0:T(8,128)(2,1)S(1)}) custom-call(s32[4]{0:T(128)S(1)} %pad_add_fusion.pos, bf16[128,256]{1,0:T(8,128)(2,1)S(1)} %get-tuple-element.57.refs_0_, bf16[128,256]{1,0:T(8,128)(2,1)S(1)} %collective-permute-done.15.refs_1_, ...), custom_call_target="tpu_custom_call" | custom-call | tf_op jit(solution)/shard_map/pallas_call | solution.py:219
  66.3 2.7 %collective-permute-done.24.near = bf16[528,256]{1,0:T(8,128)(2,1)S(1)} collective-permute-done((bf16[528,256]{1,0:T(8,128)(2,1)S(1)}, bf16[528,256]{1,0:T(8,128)(2,1)S(1)}, u32[]{:S(2)}, u32[]{:S(2)}) %collective-permute-start.24) | collective-permute-done | bytes 270368 | tf_op jit(solution)/shard_map/ppermute | solution.py:199
  69.6 2.8 %collective-permute-done.21.near = bf16[528,256]{1,0:T(8,128)(2,1)S(1)} collective-permute-done((bf16[528,256]{1,0:T(8,128)(2,1)S(1)}, bf16[528,256]{1,0:T(8,128)(2,1)S(1)}, u32[]{:S(2)}, u32[]{:S(2)}) %collective-permute-start.21) | collective-permute-done | bytes 270368 | tf_op jit(solution)/shard_map/ppermute | solution.py:196
  72.9 5.9 %collective-permute-done.18.near = bf16[528,256]{1,0:T(8,128)(2,1)S(1)} collective-permute-done((bf16[528,256]{1,0:T(8,128)(2,1)S(1)}, bf16[528,256]{1,0:T(8,128)(2,1)S(1)}, u32[]{:S(2)}, u32[]{:S(2)}) %collective-permute-start.18) | collective-permute-done | bytes 270368 | tf_op jit(solution)/shard_map/ppermute | solution.py:211
  78.8 2.0 %shard_map.57.rest_0_ = bf16[256,4096]{1,0:T(8,128)(2,1)} custom-call(s32[4]{0:T(128)S(1)} %pad_add_fusion.pos, bf16[8,256,256]{2,1,0:T(8,128)(2,1)S(1)} %get-tuple-element.63.refs_9_.phi_q, bf16[8,256,256]{2,1,0:T(8,128)(2,1)S(1)} %get-tuple-element.69.weights, bf16[256,4096]{1,0:T(8,128)(2,1)S(1)} %bitcast.12, ...), custom_call_target="tpu_custom_call" | custom-call | tf_op jit(solution)/shard_map/pallas_call | solution.py:219
  80.8 2.0 %shard_map.58.rest_0_ = bf16[256,4096]{1,0:T(8,128)(2,1)} custom-call(s32[4]{0:T(128)S(1)} %pad_add_fusion.pos, bf16[8,256,256]{2,1,0:T(8,128)(2,1)S(1)} %get-tuple-element.56.refs_5_.phi_q, bf16[8,256,256]{2,1,0:T(8,128)(2,1)S(1)} %get-tuple-element.67.weights, bf16[256,4096]{1,0:T(8,128)(2,1)S(1)} %bitcast.13, ...), custom_call_target="tpu_custom_call", output_to_operand_aliasing={{}: (8, {})} | custom-call | tf_op jit(solution)/shard_map/pallas_call | solution.py:219
  82.9 2.0 %shard_map.59.rest_0_ = bf16[256,4096]{1,0:T(8,128)(2,1)} custom-call(s32[4]{0:T(128)S(1)} %pad_add_fusion.pos, bf16[8,256,256]{2,1,0:T(8,128)(2,1)S(1)} %get-tuple-element.48.refs_4_.phi_q, bf16[8,256,256]{2,1,0:T(8,128)(2,1)S(1)} %get-tuple-element.65.weights, bf16[256,4096]{1,0:T(8,128)(2,1)S(1)} %bitcast.14, ...), custom_call_target="tpu_custom_call", output_to_operand_aliasing={{}: (8, {})} | custom-call | tf_op jit(solution)/shard_map/pallas_call | solution.py:219
  84.9 2.0 %shard_map.60 = bf16[256,4096]{1,0:T(8,128)(2,1)} custom-call(s32[4]{0:T(128)S(1)} %pad_add_fusion.pos, bf16[8,256,256]{2,1,0:T(8,128)(2,1)S(1)} %get-tuple-element.50.refs_4_.phi_q, bf16[8,256,256]{2,1,0:T(8,128)(2,1)S(1)} %get-tuple-element.51.weights, bf16[256,4096]{1,0:T(8,128)(2,1)S(1)} %bitcast.15, ...), custom_call_target="tpu_custom_call", output_to_operand_aliasing={{}: (8, {})} | custom-call | tf_op jit(solution)/shard_map/pallas_call | solution.py:219
  (69 shorter events, 26.4 us)
Async XLA Ops:
  1.4 9.5 %collective-permute-start.1 = (bf16[4,256,128]{2,1,0:T(8,128)(2,1)S(1)}, bf16[4,256,128]{2,1,0:T(8,128)(2,1)S(1)}, u32[]{:S(2)}, u32[]{:S(2)}) collective-permute-start(bf16[4,256,128]{2,1,0:T(8,128)(2,1)S(1)} %constant_dynamic-slice_fusion), channel_id=1, source_target_pairs={{0,2},{1,3},{2,0},{3,1},{4,6},{5,7},{6,4},{7,5},{8,10},{9,11},{10,... | collective-permute-start | bytes 786440 | tf_op jit(solution)/shard_map/ppermute | solution.py:196
  11.0 8.7 %collective-permute-start.2 = (bf16[4,256,128]{2,1,0:T(8,128)(2,1)S(1)}, bf16[4,256,128]{2,1,0:T(8,128)(2,1)S(1)}, u32[]{:S(2)}, u32[]{:S(2)}) collective-permute-start(bf16[4,256,128]{2,1,0:T(8,128)(2,1)S(1)} %collective-permute-done.1.f0), channel_id=1, source_target_pairs={{0,4},{4,0},{8,12},{12,8},{16,20},{20,16},{24,28},{28,24},{1,5},{5... | collective-permute-start | bytes 786440 | tf_op jit(solution)/shard_map/ppermute | solution.py:199
  14.7 6.7 %collective-permute-start.4 = (bf16[528,256]{1,0:T(8,128)(2,1)S(1)}, bf16[528,256]{1,0:T(8,128)(2,1)S(1)}, u32[]{:S(2)}, u32[]{:S(2)}) collective-permute-start(bf16[528,256]{1,0:T(8,128)(2,1)S(1)} %get-tuple-element.40), channel_id=1, source_target_pairs={{0,1},{1,0},{2,3},{3,2},{4,5},{5,4},{6,7},{7,6},{8,9},{9,8},{10,11... | collective-permute-start | bytes 811016 | tf_op jit(solution)/shard_map/ppermute | solution.py:196
  17.1 8.1 %collective-permute-start.8 = (bf16[528,256]{1,0:T(8,128)(2,1)S(1)}, bf16[528,256]{1,0:T(8,128)(2,1)S(1)}, u32[]{:S(2)}, u32[]{:S(2)}) collective-permute-start(bf16[528,256]{1,0:T(8,128)(2,1)S(1)} %get-tuple-element.46), channel_id=1, source_target_pairs={{0,1},{1,0},{2,3},{3,2},{4,5},{5,4},{6,7},{7,6},{8,9},{9,8},{10,11... | collective-permute-start | bytes 811016 | tf_op jit(solution)/shard_map/ppermute | solution.py:196
  19.7 9.3 %collective-permute-start.10 = (bf16[528,256]{1,0:T(8,128)(2,1)S(1)}, bf16[528,256]{1,0:T(8,128)(2,1)S(1)}, u32[]{:S(2)}, u32[]{:S(2)}) collective-permute-start(bf16[528,256]{1,0:T(8,128)(2,1)S(1)} %add_convert_fusion.1.rest_0_), channel_id=1, source_target_pairs={{0,2},{1,3},{2,0},{3,1},{4,6},{5,7},{6,4},{7,5},{8,10},{9,11},{10,... | collective-permute-start | bytes 811016 | tf_op jit(solution)/shard_map/ppermute | solution.py:196
  21.5 14.2 %collective-permute-start.11 = (bf16[528,256]{1,0:T(8,128)(2,1)S(1)}, bf16[528,256]{1,0:T(8,128)(2,1)S(1)}, u32[]{:S(2)}, u32[]{:S(2)}) collective-permute-start(bf16[528,256]{1,0:T(8,128)(2,1)S(1)} %add_convert_fusion.3.rest_0_), channel_id=1, source_target_pairs={{0,6},{1,7},{2,4},{3,5},{4,2},{5,3},{6,0},{7,1},{8,14},{9,15},{10,... | collective-permute-start | bytes 811016 | tf_op jit(solution)/shard_map/ppermute | solution.py:211
  25.3 14.7 %collective-permute-start.9 = (bf16[528,256]{1,0:T(8,128)(2,1)S(1)}, bf16[528,256]{1,0:T(8,128)(2,1)S(1)}, u32[]{:S(2)}, u32[]{:S(2)}) collective-permute-start(bf16[528,256]{1,0:T(8,128)(2,1)S(1)} %add_convert_fusion), channel_id=1, source_target_pairs={{0,4},{4,0},{8,12},{12,8},{16,20},{20,16},{24,28},{28,24},{1,5},{5... | collective-permute-start | bytes 811016 | tf_op jit(solution)/shard_map/ppermute | solution.py:199
  25.6 39.2 %collective-permute-start.28 = (bf16[528,256]{1,0:T(8,128)(2,1)S(1)}, bf16[528,256]{1,0:T(8,128)(2,1)S(1)}, u32[]{:S(2)}, u32[]{:S(2)}) collective-permute-start(bf16[528,256]{1,0:T(8,128)(2,1)S(1)} %get-tuple-element.41.rest_0_), channel_id=1, source_target_pairs={{0,1},{1,0},{2,3},{3,2},{4,5},{5,4},{6,7},{7,6},{8,9},{9,8},{10,11... | collective-permute-start | bytes 811016 | tf_op jit(solution)/shard_map/ppermute | solution.py:196
  40.8 8.0 %collective-permute-start.12 = (bf16[144,256]{1,0:T(8,128)(2,1)S(1)}, bf16[144,256]{1,0:T(8,128)(2,1)S(1)}, u32[]{:S(2)}, u32[]{:S(2)}) collective-permute-start(bf16[144,256]{1,0:T(8,128)(2,1)S(1)} %get-tuple-element.53), channel_id=1, source_target_pairs={{0,8},{4,12},{8,0},{12,4},{16,24},{20,28},{24,16},{28,20},{1,9},{5... | collective-permute-start | bytes 221192 | tf_op jit(solution)/shard_map/ppermute | solution.py:199
  42.4 7.7 %collective-permute-start.13 = (bf16[144,256]{1,0:T(8,128)(2,1)S(1)}, bf16[144,256]{1,0:T(8,128)(2,1)S(1)}, u32[]{:S(2)}, u32[]{:S(2)}) collective-permute-start(bf16[144,256]{1,0:T(8,128)(2,1)S(1)} %get-tuple-element.54), channel_id=1, source_target_pairs={{0,16},{4,20},{8,24},{12,28},{16,0},{20,4},{24,8},{28,12},{1,17},{... | collective-permute-start | bytes 221192 | tf_op jit(solution)/shard_map/ppermute | solution.py:199
  45.0 6.3 %collective-permute-start.14 = (bf16[144,256]{1,0:T(8,128)(2,1)S(1)}, bf16[144,256]{1,0:T(8,128)(2,1)S(1)}, u32[]{:S(2)}, u32[]{:S(2)}) collective-permute-start(bf16[144,256]{1,0:T(8,128)(2,1)S(1)} %get-tuple-element.49.rest_0_), channel_id=1, source_target_pairs={{0,24},{4,28},{8,16},{12,20},{16,8},{20,12},{24,0},{28,4},{1,25},{... | collective-permute-start | bytes 221192 | tf_op jit(solution)/shard_map/ppermute | solution.py:199
  52.0 6.4 %collective-permute-start.15 = (bf16[128,256]{1,0:T(8,128)(2,1)S(1)}, bf16[128,256]{1,0:T(8,128)(2,1)S(1)}, u32[]{:S(2)}, u32[]{:S(2)}) collective-permute-start(bf16[128,256]{1,0:T(8,128)(2,1)S(1)} %get-tuple-element.58), channel_id=1, source_target_pairs={{0,8},{4,12},{8,0},{12,4},{16,24},{20,28},{24,16},{28,20},{1,9},{5... | collective-permute-start | bytes 196616 | tf_op jit(solution)/shard_map/ppermute | solution.py:199
  53.0 6.2 %collective-permute-start.16 = (bf16[128,256]{1,0:T(8,128)(2,1)S(1)}, bf16[128,256]{1,0:T(8,128)(2,1)S(1)}, u32[]{:S(2)}, u32[]{:S(2)}) collective-permute-start(bf16[128,256]{1,0:T(8,128)(2,1)S(1)} %get-tuple-element.59), channel_id=1, source_target_pairs={{0,16},{4,20},{8,24},{12,28},{16,0},{20,4},{24,8},{28,12},{1,17},{... | collective-permute-start | bytes 196616 | tf_op jit(solution)/shard_map/ppermute | solution.py:199
  54.7 6.1 %collective-permute-start.17 = (bf16[128,256]{1,0:T(8,128)(2,1)S(1)}, bf16[128,256]{1,0:T(8,128)(2,1)S(1)}, u32[]{:S(2)}, u32[]{:S(2)}) collective-permute-start(bf16[128,256]{1,0:T(8,128)(2,1)S(1)} %get-tuple-element.60.rest_0_), channel_id=1, source_target_pairs={{0,24},{4,28},{8,16},{12,20},{16,8},{20,12},{24,0},{28,4},{1,25},{... | collective-permute-start | bytes 196616 | tf_op jit(solution)/shard_map/ppermute | solution.py:199
  62.6 6.5 %collective-permute-start.24 = (bf16[528,256]{1,0:T(8,128)(2,1)S(1)}, bf16[528,256]{1,0:T(8,128)(2,1)S(1)}, u32[]{:S(2)}, u32[]{:S(2)}) collective-permute-start(bf16[528,256]{1,0:T(8,128)(2,1)S(1)} %get-tuple-element.68), channel_id=1, source_target_pairs={{0,4},{4,0},{8,12},{12,8},{16,20},{20,16},{24,28},{28,24},{1,5},{5... | collective-permute-start | bytes 811016 | tf_op jit(solution)/shard_map/ppermute | solution.py:199
  63.1 6.0 %collective-permute-start.26 = (bf16[528,256]{1,0:T(8,128)(2,1)S(1)}, bf16[528,256]{1,0:T(8,128)(2,1)S(1)}, u32[]{:S(2)}, u32[]{:S(2)}) collective-permute-start(bf16[528,256]{1,0:T(8,128)(2,1)S(1)} %get-tuple-element.45), channel_id=1, source_target_pairs={{0,1},{1,0},{2,3},{3,2},{4,5},{5,4},{6,7},{7,6},{8,9},{9,8},{10,11... | collective-permute-start | bytes 811016 | tf_op jit(solution)/shard_map/ppermute | solution.py:196
  63.1 9.3 %collective-permute-start.21 = (bf16[528,256]{1,0:T(8,128)(2,1)S(1)}, bf16[528,256]{1,0:T(8,128)(2,1)S(1)}, u32[]{:S(2)}, u32[]{:S(2)}) collective-permute-start(bf16[528,256]{1,0:T(8,128)(2,1)S(1)} %get-tuple-element.66), channel_id=1, source_target_pairs={{0,2},{1,3},{2,0},{3,1},{4,6},{5,7},{6,4},{7,5},{8,10},{9,11},{10,... | collective-permute-start | bytes 811016 | tf_op jit(solution)/shard_map/ppermute | solution.py:196
  64.6 7.8 %collective-permute-start.27 = (bf16[528,256]{1,0:T(8,128)(2,1)S(1)}, bf16[528,256]{1,0:T(8,128)(2,1)S(1)}, u32[]{:S(2)}, u32[]{:S(2)}) collective-permute-start(bf16[528,256]{1,0:T(8,128)(2,1)S(1)} %get-tuple-element.70.near), channel_id=1, source_target_pairs={{0,1},{1,0},{2,3},{3,2},{4,5},{5,4},{6,7},{7,6},{8,9},{9,8},{10,11... | collective-permute-start | bytes 811016 | tf_op jit(solution)/shard_map/ppermute | solution.py:196
  64.8 14.0 %collective-permute-start.18 = (bf16[528,256]{1,0:T(8,128)(2,1)S(1)}, bf16[528,256]{1,0:T(8,128)(2,1)S(1)}, u32[]{:S(2)}, u32[]{:S(2)}) collective-permute-start(bf16[528,256]{1,0:T(8,128)(2,1)S(1)} %get-tuple-element.64), channel_id=1, source_target_pairs={{0,6},{1,7},{2,4},{3,5},{4,2},{5,3},{6,0},{7,1},{8,14},{9,15},{10,... | collective-permute-start | bytes 811016 | tf_op jit(solution)/shard_map/ppermute | solution.py:211
  69.1 11.7 %collective-permute-start.25 = (bf16[528,256]{1,0:T(8,128)(2,1)S(1)}, bf16[528,256]{1,0:T(8,128)(2,1)S(1)}, u32[]{:S(2)}, u32[]{:S(2)}) collective-permute-start(bf16[528,256]{1,0:T(8,128)(2,1)S(1)} %collective-permute-done.24.near), channel_id=1, source_target_pairs={{0,1},{1,0},{2,3},{3,2},{4,5},{5,4},{6,7},{7,6},{8,9},{9,8},{10,11... | collective-permute-start | bytes 811016 | tf_op jit(solution)/shard_map/ppermute | solution.py:196
  69.1 13.8 %collective-permute-start.23 = (bf16[528,256]{1,0:T(8,128)(2,1)S(1)}, bf16[528,256]{1,0:T(8,128)(2,1)S(1)}, u32[]{:S(2)}, u32[]{:S(2)}) collective-permute-start(bf16[528,256]{1,0:T(8,128)(2,1)S(1)} %get-tuple-element.43), channel_id=1, source_target_pairs={{0,1},{1,0},{2,3},{3,2},{4,5},{5,4},{6,7},{7,6},{8,9},{9,8},{10,11... | collective-permute-start | bytes 811016 | tf_op jit(solution)/shard_map/ppermute | solution.py:196
  72.4 10.5 %collective-permute-start.22 = (bf16[528,256]{1,0:T(8,128)(2,1)S(1)}, bf16[528,256]{1,0:T(8,128)(2,1)S(1)}, u32[]{:S(2)}, u32[]{:S(2)}) collective-permute-start(bf16[528,256]{1,0:T(8,128)(2,1)S(1)} %collective-permute-done.21.near), channel_id=1, source_target_pairs={{0,1},{1,0},{2,3},{3,2},{4,5},{5,4},{6,7},{7,6},{8,9},{9,8},{10,11... | collective-permute-start | bytes 811016 | tf_op jit(solution)/shard_map/ppermute | solution.py:196
  72.4 12.5 %collective-permute-start.20 = (bf16[528,256]{1,0:T(8,128)(2,1)S(1)}, bf16[528,256]{1,0:T(8,128)(2,1)S(1)}, u32[]{:S(2)}, u32[]{:S(2)}) collective-permute-start(bf16[528,256]{1,0:T(8,128)(2,1)S(1)} %get-tuple-element.39), channel_id=1, source_target_pairs={{0,1},{1,0},{2,3},{3,2},{4,5},{5,4},{6,7},{7,6},{8,9},{9,8},{10,11... | collective-permute-start | bytes 811016 | tf_op jit(solution)/shard_map/ppermute | solution.py:196
  78.8 6.1 %collective-permute-start.19 = (bf16[528,256]{1,0:T(8,128)(2,1)S(1)}, bf16[528,256]{1,0:T(8,128)(2,1)S(1)}, u32[]{:S(2)}, u32[]{:S(2)}) collective-permute-start(bf16[528,256]{1,0:T(8,128)(2,1)S(1)} %collective-permute-done.18.near), channel_id=1, source_target_pairs={{0,1},{1,0},{2,3},{3,2},{4,5},{5,4},{6,7},{7,6},{8,9},{9,8},{10,11... | collective-permute-start | bytes 811016 | tf_op jit(solution)/shard_map/ppermute | solution.py:196
  (12 other events, 57.1 us)

commit v3 on v2

v3 whole, which is shorter than its diff:
```python
import functools
import math

import jax
import jax.numpy as jnp
from jax import lax
from jax.experimental import pallas as pl
from jax.experimental.pallas import tpu as pltpu
from jax.sharding import PartitionSpec as P

F32, BF16 = jnp.float32, jnp.bfloat16
LOG2E = math.log2(math.e)
TOTAL_ROWS = 16
VMEM = 12 * 1024 * 1024


def feature_map(x, w):
    size, count = x.shape[1], w.shape[0]
    c = size ** (-0.25)
    p = lax.dot_general(x, w, (((1,), (1,)), ((), ())), preferred_element_type=F32)
    wide = x.astype(F32)
    square = jnp.sum(wide * wide, axis=1, keepdims=True)
    r = lax.rsqrt(square / size + 1e-06)
    half = square * r * r * (0.5 * c * c * LOG2E) + 0.5 * math.log2(count)
    ww = w.astype(F32)
    ww = ww * ww
    high = ww.astype(BF16)
    low = (ww - high.astype(F32)).astype(BF16)
    ones = jnp.ones((16, size), BF16)
    nt = (((1,), (1,)), ((), ()))
    total = lax.dot_general(ones, high, nt, preferred_element_type=F32)
    total = total + lax.dot_general(ones, low, nt, preferred_element_type=F32)
    s = lax.rsqrt(total[:1] / size + 1e-06)
    return jnp.exp2(p * (r * (c * LOG2E)) * s - half).astype(BF16)


def position(nx, ny):
    head, seq = lax.axis_index("head"), lax.axis_index("seq")
    return head // 2, head % 2, seq % ny, seq // ny


def place_of(pos, key, nx, ny, core):
    flip = 1 if nx > 1 else 0
    part = pos[2] ^ key[1]
    return ((pos[0] ^ key[0] ^ flip) * 2 + (pos[1] ^ core)) * ny + part, part


def heads_of(pos, key, shape, f0, f1):
    nx, ny, group, size = shape
    for core, f in ((1, f1), (0, f0)):
        place, part = place_of(pos, key, nx, ny, core)
        first = 0 if f.shape[0] == group else part * group
        for h in range(group):
            start = pl.multiple_of((place * group + h) * size, size)
            yield (1 - core) * group + h, pl.ds(start, size), f, first + h


def states_kernel(key, shape, waits, k, v, f0, f1, phi, *sums):
    nx, ny, group, size = shape
    *others, mine = sums
    pos = position(nx, ny)
    heads = list(heads_of(pos, key, shape, f0, f1))
    totals = []
    for i, cols, f, at in heads:
        if i % group == 0:
            waits(i // group)
        ph = feature_map(k[:, cols], f[at])
        phi[i] = ph
        totals.append(jnp.sum(ph.astype(F32), axis=0, keepdims=True))
    waits(2)
    for i, cols, _, _ in heads:
        h, half = i % group, group // 2
        late = i < group and h >= half
        out = mine if i >= group else others[-1] if late else others[0]
        h = h - half if late else h
        st = lax.dot_general(
            v[:, cols], phi[i], (((0,), (0,)), ((), ())), preferred_element_type=F32
        )
        out[h * size : (h + 1) * size] = st.astype(BF16)
    pad = jnp.zeros((TOTAL_ROWS - group, totals[0].shape[1]), F32)
    others[-1][(group - group // 2) * size :] = jnp.concatenate([*totals[:group], pad], axis=0).astype(BF16)
    mine[group * size :] = jnp.concatenate([*totals[group:], pad], axis=0).astype(BF16)
    waits(3)


def first_kernel(key, shape, k_far, v_far, f_far, f1, *refs):
    nx, ny, group, size = shape
    *outs, k, v, f, sems = refs
    wide = group * size
    blocks = k.shape[1] // wide
    place = place_of(position(nx, ny), key, nx, ny, 0)[0]
    copies = [[], [], [], []]

    def fetch(stage, source, target, at):
        copy = pltpu.make_async_copy(source, target, sems.at[at])
        copy.start()
        copies[stage].append(copy)

    def fetch_block(stage, source, target, j, at):
        cols = pl.ds(pl.multiple_of((place ^ j) * wide, wide), wide)
        fetch(stage, source.at[:, cols], target.at[:, cols], at)

    fetch_block(0, k_far, k, ny, 1)
    fetch(1, f_far, f, 0)
    fetch_block(1, k_far, k, 0, 2)
    fetch_block(2, v_far, v, ny, blocks + 1)
    fetch_block(2, v_far, v, 0, blocks + 2)
    rest = [j for j in range(blocks) if j not in (0, ny)]
    for n, j in enumerate(rest):
        fetch_block(3, k_far, k, j, 3 + n)
        fetch_block(3, v_far, v, j, blocks + 3 + n)

    def waits(stage):
        for copy in copies[stage]:
            copy.wait()

    states_kernel(key, shape, waits, k, v, f, f1, *outs)


def second_kernel(key, shape, q_far, k, v, f0, f1, *refs):
    *outs, q, sem = refs
    copy = pltpu.make_async_copy(q_far, q, sem.at[0])
    copy.start()

    def waits(stage):
        if stage == 3:
            copy.wait()

    states_kernel(key, shape, waits, k, v, f0, f1, *outs)


def later_kernel(extra, key, shape, k, v, f0, f1, *refs):
    states_kernel(key, shape, lambda stage: None, k, v, f0, f1, *refs[extra:])


def inner_kernel(key, shape, q, v, f0, f1, phi_k, *rest):
    phi_q, inner, weights = rest[-3:]
    nx, ny, group, size = shape
    tokens = q.shape[0]
    heads = list(heads_of(position(nx, ny), key, shape, f0, f1))
    for i, cols, f, at in heads:
        phi_q[i] = feature_map(q[:, cols], f[at])
    row = lax.broadcasted_iota(jnp.int32, (tokens, tokens), 0)
    col = lax.broadcasted_iota(jnp.int32, (tokens, tokens), 1)
    mask = col <= row
    for i, _, _, _ in heads:
        sc = lax.dot_general(
            phi_q[i], phi_k[i], (((1,), (1,)), ((), ())), preferred_element_type=F32
        )
        weights[i] = jnp.where(mask, sc, 0.0).astype(BF16)
    ones = jnp.ones((tokens, size), BF16)
    for i, cols, _, _ in heads:
        inner[i] = jnp.dot(
            weights[i],
            jnp.concatenate([v[:, cols], ones], axis=1),
            preferred_element_type=F32,
        )


def output_kernel(jobs, shape, *refs):
    out, ready, sems = refs[-3:]
    nx, ny, group, size = shape
    pos = position(nx, ny)
    add = (pos[1] == 1).astype(F32)
    copies = []
    for n, (key, core) in enumerate(jobs):
        phi_q, inner, base, extra_a, extra_b = refs[5 * n : 5 * n + 5]
        count = phi_q.shape[-1]
        place = place_of(pos, key, nx, ny, core)[0]
        half = extra_a.shape[0]
        whole = half == base.shape[0]
        last = extra_a[group * size :] if whole else extra_b[group * size - half :]
        totals = base[group * size :].astype(F32) + add * last.astype(F32)
        for h in range(group):
            rows = slice(h * size, (h + 1) * size)
            if whole or h * size < half:
                extra = extra_a[rows]
            else:
                extra = extra_b[h * size - half : (h + 1) * size - half]
            st = (base[rows].astype(F32) + add * extra.astype(F32)).astype(BF16)
            tot = jnp.broadcast_to(totals[h : h + 1], (size, count)).astype(BF16)
            at = (1 - core) * group + h
            acc = inner[at] + lax.dot_general(
                phi_q[at],
                jnp.concatenate([st, tot], axis=0),
                (((1,), (1,)), ((), ())),
                preferred_element_type=F32,
            )
            ready[n, :, rows] = (acc[:, :size] / acc[:, size:]).astype(BF16)
        wide = group * size
        copy = pltpu.make_async_copy(
            ready.at[n],
            out.at[:, pl.ds(pl.multiple_of(place * wide, wide), wide)],
            sems.at[n],
        )
        copy.start()
        copies.append(copy)
    for copy in copies:
        copy.wait()


def tie_kernel(count, *refs):
    for a, out in zip(refs[:count], refs[-count:]):
        out[...] = a[...]


def chip_kernel(mine, *refs):
    *others, out = refs
    start = 0
    for other in others:
        rows = slice(start, start + other.shape[0])
        start = rows.stop
        out[rows] = (mine[rows].astype(F32) + other[...].astype(F32)).astype(BF16)


def plane_kernel(count, zrows, ny, *refs):
    held, z = refs[-1], position(1, ny)[3]
    pieces, outs = refs[:count], refs[-1 - (held.shape[0] - TOTAL_ROWS) // zrows : -1]
    total = pieces[0][...].astype(F32)
    for piece in pieces[1:]:
        total = total + piece[...].astype(F32)
    held[...] = total
    srows = len(outs) * zrows
    for j, out in enumerate(outs):
        start = pl.multiple_of((z ^ j) * zrows, zrows)
        out[:zrows] = held[pl.ds(start, zrows)].astype(BF16)
        out[zrows:] = held[srows:].astype(BF16)


def prefix_kernel(count, zrows, ny, *refs):
    heard, outs, totals = refs[:count], refs[-1 - count : -1], refs[-1]
    z = position(1, ny)[3]
    for j, out in enumerate(outs):
        total = jnp.zeros(out.shape, F32)
        for i, part in enumerate(heard):
            total = total + jnp.where((z ^ i) < (z ^ j), part[:zrows].astype(F32), 0.0)
        out[...] = total.astype(BF16)
    total = jnp.zeros(totals.shape, F32)
    for i, part in enumerate(heard):
        total = total + jnp.where((z ^ i) < z, part[zrows:].astype(F32), 0.0)
    totals[...] = total


def place_kernel(nx, ny, count, zrows, *refs):
    keys = [(dx, dy) for dx in range(nx) for dy in range(ny)]
    prefix, totals = refs[:count], refs[count]
    pieces, outs = refs[count + 1 : count + 1 + len(keys)], refs[-1 - len(keys) : -1]
    held = refs[-1]
    x, _, y, z = position(nx, ny)
    for j in range(count):
        start = pl.multiple_of((z ^ j) * zrows, zrows)
        held[pl.ds(start, zrows)] = prefix[j][...].astype(F32)
    held[count * zrows :] = totals[...]
    for (dx, dy), out in zip(keys, outs):
        target = (y ^ dy) * nx + (x ^ dx)
        total = held[...]
        for (ex, ey), piece in zip(keys, pieces):
            source = (y ^ ey) * nx + (x ^ ex)
            total = total + jnp.where(source < target, piece[...].astype(F32), 0.0)
        out[...] = total.astype(BF16)


def body(seqs, heads, queries, keys, values, features):
    tokens, width = queries.shape[1:]
    q, k, v = (a.reshape(tokens, width) for a in (queries, keys, values))
    own, count, size = features.shape
    cores = 2
    nx = heads // cores
    ny = nx if seqs % nx == 0 else 1
    nz = seqs // ny
    flip = 1 if nx > 1 else 0
    group = own // ny
    srows = group * size
    zrows = srows // nz
    rows = srows + TOTAL_ROWS
    plane = [(dx, dy) for dx in range(nx) for dy in range(ny)]

    y = position(nx, ny)[2]

    def head_swap(a, bits):
        return lax.ppermute(a, "head", [(i, i ^ bits) for i in range(heads)])

    def seq_swap(a, bits):
        return lax.ppermute(a, "seq", [(i, i ^ bits) for i in range(seqs)])

    def plane_swap(a, dx, dy):
        if dy == 0:
            return head_swap(a, dx * cores)
        if dx == 0:
            return seq_swap(a, dy)
        pairs = [
            (s * heads + h, (s ^ dy) * heads + (h ^ (dx * cores)))
            for s in range(seqs)
            for h in range(heads)
        ]
        return lax.ppermute(a, ("seq", "head"), pairs)

    anywhere = pl.BlockSpec(memory_space=pl.ANY)

    shape = (nx, ny, group, size)
    near = pl.BlockSpec(memory_space=pltpu.VMEM)
    far = pl.BlockSpec(memory_space=pltpu.HBM)

    def call(kernel, out, args, after=(), outs=near, scratch=(), alias={}, fars=()):
        held = [pltpu.with_memory_space_constraint(a, pltpu.VMEM) for a in args]
        there = [pltpu.with_memory_space_constraint(a, pltpu.HBM) for a in fars]
        if outs is near:
            out = jax.tree.map(lambda a: pltpu.VMEM(a.shape, a.dtype), out)
        return pl.pallas_call(
            kernel,
            out_shape=out,
            in_specs=[far] * len(there) + [near] * len(held) + [anywhere] * len(after),
            out_specs=jax.tree.map(lambda _: outs, out),
            scratch_shapes=scratch,
            input_output_aliases=alias,
            compiler_params=pltpu.CompilerParams(vmem_limit_bytes=VMEM),
        )(*there, *held, *after)

    def tie(arrays, after):
        kernel = functools.partial(tie_kernel, len(arrays))
        return call(kernel, [jax.ShapeDtypeStruct(a.shape, a.dtype) for a in arrays], arrays, [after])

    def per_head(a, b):
        return jax.ShapeDtypeStruct((cores * group, a, b), BF16)

    whole = jax.ShapeDtypeStruct((rows, count), BF16)

    dirs, phi_k, phi_w, piece, got, theirs = {}, {}, {}, {}, {}, {}
    near_k, near_q = [], []

    def states(key, after=()):
        half = jax.ShapeDtypeStruct((group // 2 * size, count), BF16)
        rest = jax.ShapeDtypeStruct((rows - half.shape[0], count), BF16)
        outs = [per_head(tokens, count), *([half, rest] if group > 1 else [rest]), whole]
        like = [jax.ShapeDtypeStruct(a.shape, BF16) for a in (k, v, features)]
        if not near_k:
            sems = pltpu.SemaphoreType.DMA((2 * (width // (group * size)) + 1,))
            phi_k[key], *sums, key_block, value_block, part = call(
                functools.partial(first_kernel, key, shape),
                outs + like,
                [near_dirs],
                fars=[k, v, features],
                scratch=[sems],
            )
            near_k.extend([key_block, value_block, part])
        elif not near_q:
            near_k_v_f = [near_k[0], near_k[1], near_k[2], near_dirs]
            phi_k[key], *sums, loaded = call(
                functools.partial(second_kernel, key, shape),
                [*outs, like[0]],
                near_k_v_f,
                fars=[q],
                scratch=[pltpu.SemaphoreType.DMA((1,))],
            )
            near_q.append(loaded)
        else:
            phi_k[key], *sums = call(
                functools.partial(later_kernel, len(after), key, shape),
                outs,
                [*near_k[:2], *directions(key)],
                after,
            )
        *other, mine = sums
        other = [head_swap(a, 1) for a in other]
        theirs[key] = [[other[0], other[-1]], [head_swap(mine, 1)] * 2]
        piece[key] = call(chip_kernel, whole, [mine, *other])
        got[key] = piece[key] if key == (0, 0) else plane_swap(piece[key], *key)
        return mine

    def directions(key):
        return dirs[key] if key[0] != flip else (near_k[2], near_dirs)

    def inner(key, after=()):
        phi_w[key] = call(
            functools.partial(inner_kernel, key, shape),
            [
                per_head(tokens, count),
                jax.ShapeDtypeStruct((cores * group, tokens, 2 * size), F32),
            ],
            [near_q[0], near_k[1], *directions(key), phi_k[key]],
            after,
            scratch=[pltpu.VMEM((cores * group, tokens, tokens), BF16)],
        )
        return phi_w[key][0]

    near_dirs = head_swap(features, 1)
    first = [(flip, dy) for dy in range(ny)]
    later = [(dx, dy) for dx in range(nx) for dy in reversed(range(ny)) if dx != flip]
    for key in first:
        states(key)
    for ox in range(1, nx):
        if ny == 2:
            part = lax.dynamic_slice_in_dim(features, (y ^ 1) * group, group, 0)
            (part,) = tie([head_swap(part, ox * cores)], phi_k[first[-1]])
            rest = seq_swap(part, 1)
            dirs[ox ^ flip, 1] = (part, head_swap(part, 1))
            dirs[ox ^ flip, 0] = (rest, head_swap(rest, 1))
        else:
            (full,) = tie([head_swap(features, ox * cores)], phi_k[first[-1]])
            full = (full, head_swap(full, 1))
            for dy in range(ny):
                dirs[ox ^ flip, dy] = full

    for i, key in enumerate(later):
        states(key, [piece[first[0]] if i == 0 else got[first[0]]])

    summed = call(
        functools.partial(plane_kernel, len(plane), zrows, ny),
        [jax.ShapeDtypeStruct((zrows + TOTAL_ROWS, count), BF16)] * nz,
        [got[key] for key in plane],
        scratch=[pltpu.VMEM((rows, count), F32)],
    )
    heard = [a if j == 0 else seq_swap(a, j * ny) for j, a in enumerate(summed)]
    done = [inner(key, [summed[-1]]) for key in [*first, *later[:-1]]]
    *prefix, totals = call(
        functools.partial(prefix_kernel, nz, zrows, ny),
        [jax.ShapeDtypeStruct((zrows, count), BF16)] * nz
        + [jax.ShapeDtypeStruct((TOTAL_ROWS, count), F32)],
        heard,
        done,
    )
    done = [inner(later[-1], [prefix[-1]])] if later else []
    prefix = [a if j == 0 else seq_swap(a, j * ny) for j, a in enumerate(prefix)]
    placed = call(
        functools.partial(place_kernel, nx, ny, nz, zrows),
        [whole] * len(plane),
        [*prefix, totals, *[got[key] for key in plane]],
        done,
        scratch=[pltpu.VMEM((rows, count), F32)],
    )

    result = {
        key: a if key == (0, 0) else plane_swap(a, *key) for key, a in zip(plane, placed)
    }
    batches = [[((0, 0), 0), ((0, 0), 1)]]
    batches += [[((0, dy), 0)] for dy in range(1, ny)]
    tied = len(batches)
    batches += [[((0, dy), 1)] for dy in range(1, ny)]
    for core in range(cores):
        for dx in range(1, nx):
            batches.append([((dx, dy), core) for dy in range(ny)])
    out = None
    for i, jobs in enumerate(batches):
        args = []
        if i == tied:
            keys = [key for key in plane if key[0]]
            result.update(zip(keys, tie([result[key] for key in keys], out)))
        for key, core in jobs:
            base = head_swap(result[key], 1) if core else result[key]
            args += [*phi_w[key], base, *theirs[key][core]]
        out = call(
            functools.partial(output_kernel, jobs, shape),
            jax.ShapeDtypeStruct((tokens, width), BF16),
            args,
            [] if out is None else [out],
            anywhere,
            [
                pltpu.VMEM((len(jobs), tokens, group * size), BF16),
                pltpu.SemaphoreType.DMA((len(jobs),)),
            ],
            {} if out is None else {len(args): 0},
        )
    return out.reshape(queries.shape)


def solution(mesh):
    token = P(None, ("seq", "head"), None)
    return jax.shard_map(
        functools.partial(body, mesh.shape["seq"], mesh.shape["head"]),
        mesh=mesh,
        in_specs=(token, token, token, P("head", None, None)),
        out_specs=token,
        check_vma=False,
    )
```

time: 87.4 us -> 79.6 us (0.911)
  Pallas kernels: 26.7 us -> 21.4 us
  local copies, waits for them, and re-layouts: 5.22 us -> 2.56 us
  starting transfers between devices: 23.4 us -> 25.5 us
  waiting for transfers between devices: 31 us -> 29.5 us
    pallas_call x15 -> x22, Pallas kernels: 26.7 us -> 21.4 us  [call(): pl.pallas_call(kernel, out_shape=out, in_specs=[far] * len(there) + [near...]
    ppermute x2, waiting for transfers between devices: 12.6 us -> 8.29 us  [plane_swap(): return lax.ppermute(a, ('seq', 'head'), pairs)]
    unnamed x14 -> x2, local copies, waits for them, and re-layouts: 4.25 us -> 1.59 us
    ppermute x18 -> x22, waiting for transfers between devices: 4.35 us -> 5.99 us  [head_swap(): return lax.ppermute(a, 'head', [(i, i ^ bits) for i in range(heads)])]
    ppermute x9, starting transfers between devices: 11.5 us -> 12.9 us  [seq_swap(): return lax.ppermute(a, 'seq', [(i, i ^ bits) for i in range(seqs)])]
    ppermute x9, waiting for transfers between devices: 14.1 us -> 15.2 us  [seq_swap(): return lax.ppermute(a, 'seq', [(i, i ^ bits) for i in range(seqs)])]
    ppermute x18 -> x22, starting transfers between devices: 8.79 us -> 9.44 us  [head_swap(): return lax.ppermute(a, 'head', [(i, i ^ bits) for i in range(heads)])]
  transfers between devices with their start and end apart: 29 -> 33, of which waited for: 12 -> 13; matrix products, arithmetic and copies ran while one was open for 2% -> 1% of each run, Pallas kernels for 28% -> 25%
where the time goes in v3:
time: 79.6 us; the launch traced here: 79.4 us
  waiting for transfers between devices  29.5 us (37%)
  starting transfers between devices  25.5 us (32%)
  Pallas kernels  21.4 us (27%)
  local copies, waits for them, and re-layouts  2.56 us (3%)
    pallas_call x22, Pallas kernels, call(): pl.pallas_call(kernel, out_shape=out, in_specs=[far] * len(there) + [near...  21.4 us
    ppermute x9, waiting for transfers between devices, seq_swap(): return lax.ppermute(a, 'seq', [(i, i ^ bits) for i in range(seqs)])  15.2 us
    ppermute x9, starting transfers between devices, seq_swap(): return lax.ppermute(a, 'seq', [(i, i ^ bits) for i in range(seqs)])  12.9 us
    ppermute x22, starting transfers between devices, head_swap(): return lax.ppermute(a, 'head', [(i, i ^ bits) for i in range(heads)])  9.44 us
    ppermute x2, waiting for transfers between devices, plane_swap(): return lax.ppermute(a, ('seq', 'head'), pairs)  8.29 us
    ppermute x22, waiting for transfers between devices, head_swap(): return lax.ppermute(a, 'head', [(i, i ^ bits) for i in range(heads)])  5.99 us
    ppermute x2, starting transfers between devices, plane_swap(): return lax.ppermute(a, ('seq', 'head'), pairs)  3.21 us
  transfers between devices with their start and end apart: 33, of which 13 were waited for; matrix products, arithmetic and copies ran while one was open for 1% of the time, Pallas kernels for 25%

profile of v3, /device:TPU:0, one launch (start us, length us, event | category | flops | bytes accessed | tf_op | source)
XLA Modules:
  0.0 79.4 jit_solution(7089010210925302490)
XLA Ops:
  1.4 2.6 %collective-permute-start.1 = (bf16[4,256,128]{2,1,0:T(8,128)(2,1)S(1)}, bf16[4,256,128]{2,1,0:T(8,128)(2,1)S(1)}, u32[]{:S(2)}, u32[]{:S(2)}) collective-permute-start(bf16[4,256,128]{2,1,0:T(8,128)(2,1)S(1)} %constant_dynamic-slice_fusion), channel_id=1, source_target_pairs={{0,2},{1,3},{2,0},{3,1},{4,6},{5,7},{6,4},{7,5},{8,10},{9,11},{10,... | collective-permute-start | bytes 786440 | tf_op jit(solution)/shard_map/ppermute | solution.py:281
  4.0 2.7 %shard_map.46 = (bf16[8,256,256]{2,1,0:T(8,128)(2,1)S(1)}, bf16[256,256]{1,0:T(8,128)(2,1)S(1)}, bf16[272,256]{1,0:T(8,128)(2,1)S(1)}, bf16[528,256]{1,0:T(8,128...) custom-call(bf16[256,4096]{1,0:T(8,128)(2,1)} %bitcast.5, ...), custom_call_target="tpu_custom_call" | custom-call | tf_op jit(solution)/shard_map/pallas_call | solution.py:309
  6.7 1.6 %shard_map.47 = (bf16[8,256,256]{2,1,0:T(8,128)(2,1)S(1)}, bf16[256,256]{1,0:T(8,128)(2,1)S(1)}, bf16[272,256]{1,0:T(8,128)(2,1)S(1)}, bf16[528,256]{1,0:T(8,128)(2,1)S(1)}, bf16[256,4096]{1,0:T(8,128)(2,1)S(1)}) custom-call(bf16[256,4096]{1,0:T(8,128)(2,1)} %bitcast.4, bf16[256,4096]{1,0:T(8,128)(2,1)S(1)} %get-tuple-element.48.k, ...), custom_call_target="tpu_custom_call" | custom-call | tf_op jit(solution)/shard_map/pallas_call | solution.py:309
  8.3 2.6 %collective-permute-done.1.refs_0_ = bf16[4,256,128]{2,1,0:T(8,128)(2,1)S(1)} collective-permute-done((bf16[4,256,128]{2,1,0:T(8,128)(2,1)S(1)}, bf16[4,256,128]{2,1,0:T(8,128)(2,1)S(1)}, u32[]{:S(2)}, u32[]{:S(2)}) %collective-permute-start.1) | collective-permute-done | bytes 262176 | tf_op jit(solution)/shard_map/ppermute | solution.py:281
  11.1 1.8 %collective-permute-start.2 = (bf16[4,256,128]{2,1,0:T(8,128)(2,1)S(1)}, bf16[4,256,128]{2,1,0:T(8,128)(2,1)S(1)}, u32[]{:S(2)}, u32[]{:S(2)}) collective-permute-start(bf16[4,256,128]{2,1,0:T(8,128)(2,1)S(1)} %shard_map.48.f0), channel_id=1, source_target_pairs={{0,4},{4,0},{8,12},{12,8},{16,20},{20,16},{24,28},{28,24},{1,5},{5... | collective-permute-start | bytes 786440 | tf_op jit(solution)/shard_map/ppermute | solution.py:284
  14.8 1.6 %collective-permute-start.6 = (bf16[528,256]{1,0:T(8,128)(2,1)S(1)}, bf16[528,256]{1,0:T(8,128)(2,1)S(1)}, u32[]{:S(2)}, u32[]{:S(2)}) collective-permute-start(bf16[528,256]{1,0:T(8,128)(2,1)S(1)} %shard_map.49.refs_0_), channel_id=1, source_target_pairs={{0,2},{1,3},{2,0},{3,1},{4,6},{5,7},{6,4},{7,5},{8,10},{9,11},{10,... | collective-permute-start | bytes 811016 | tf_op jit(solution)/shard_map/ppermute | solution.py:281
  17.9 1.9 %collective-permute-done.2.f0 = bf16[4,256,128]{2,1,0:T(8,128)(2,1)S(1)} collective-permute-done((bf16[4,256,128]{2,1,0:T(8,128)(2,1)S(1)}, bf16[4,256,128]{2,1,0:T(8,128)(2,1)S(1)}, u32[]{:S(2)}, u32[]{:S(2)}) %collective-permute-start.2) | collective-permute-done | bytes 262176 | tf_op jit(solution)/shard_map/ppermute | solution.py:284
  20.4 2.8 %collective-permute-start.15 = (bf16[528,256]{1,0:T(8,128)(2,1)S(1)}, bf16[528,256]{1,0:T(8,128)(2,1)S(1)}, u32[]{:S(2)}, u32[]{:S(2)}) collective-permute-start(bf16[528,256]{1,0:T(8,128)(2,1)S(1)} %shard_map.54), channel_id=1, source_target_pairs={{0,6},{1,7},{2,4},{3,5},{4,2},{5,3},{6,0},{7,1},{8,14},{9,15},{10,... | collective-permute-start | bytes 811016 | tf_op jit(solution)/shard_map/ppermute | solution.py:296
  27.0 2.9 %collective-permute-done.15.refs_3_.refs_8_ = bf16[528,256]{1,0:T(8,128)(2,1)S(1)} collective-permute-done((bf16[528,256]{1,0:T(8,128)(2,1)S(1)}, bf16[528,256]{1,0:T(8,128)(2,1)S(1)}, u32[]{:S(2)}, u32[]{:S(2)}) %collective-permute-start.15) | collective-permute-done | bytes 270368 | tf_op jit(solution)/shard_map/ppermute | solution.py:296
  29.9 5.7 %collective-permute-done.12.refs_1_.refs_6_ = bf16[528,256]{1,0:T(8,128)(2,1)S(1)} collective-permute-done((bf16[528,256]{1,0:T(8,128)(2,1)S(1)}, bf16[528,256]{1,0:T(8,128)(2,1)S(1)}, u32[]{:S(2)}, u32[]{:S(2)}) %collective-permute-start.12) | collective-permute-done | bytes 270368 | tf_op jit(solution)/shard_map/ppermute | solution.py:284
  35.8 1.8 %collective-permute-start.16 = (bf16[144,256]{1,0:T(8,128)(2,1)S(1)}, bf16[144,256]{1,0:T(8,128)(2,1)S(1)}, u32[]{:S(2)}, u32[]{:S(2)}) collective-permute-start(bf16[144,256]{1,0:T(8,128)(2,1)S(1)} %get-tuple-element.70), channel_id=1, source_target_pairs={{0,8},{4,12},{8,0},{12,4},{16,24},{20,28},{24,16},{28,20},{1,9},{5... | collective-permute-start | bytes 221192 | tf_op jit(solution)/shard_map/ppermute | solution.py:284
  37.6 2.6 %collective-permute-start.17 = (bf16[144,256]{1,0:T(8,128)(2,1)S(1)}, bf16[144,256]{1,0:T(8,128)(2,1)S(1)}, u32[]{:S(2)}, u32[]{:S(2)}) collective-permute-start(bf16[144,256]{1,0:T(8,128)(2,1)S(1)} %get-tuple-element.71), channel_id=1, source_target_pairs={{0,16},{4,20},{8,24},{12,28},{16,0},{20,4},{24,8},{28,12},{1,17},{... | collective-permute-start | bytes 221192 | tf_op jit(solution)/shard_map/ppermute | solution.py:284
  40.3 1.5 %shard_map.57 = (bf16[8,256,256]{2,1,0:T(8,128)(2,1)S(1)}, f32[8,256,256]{2,1,0:T(8,128)S(1)}) custom-call(bf16[256,4096]{1,0:T(8,128)(2,1)S(1)} %get-tuple-element.51.q, bf16[256,4096]{1,0:T(8,128)(2,1)S(1)} %get-tuple-element.49.v, bf16[8,256,128]{2,1,0:T(8,128)(2,1)S(1)} %get-tuple-element.50.f0, bf16[8,256,128]{2,1,0:T(8,128)(2,1)S(1)} %collective-permute-done.f1, ...), custom_call_target="tpu_custom_call" | custom-call | tf_op jit(solution)/shard_map/pallas_call | solution.py:309
  41.8 1.5 %shard_map.58 = (bf16[8,256,256]{2,1,0:T(8,128)(2,1)S(1)}, f32[8,256,256]{2,1,0:T(8,128)S(1)}) custom-call(bf16[256,4096]{1,0:T(8,128)(2,1)S(1)} %get-tuple-element.51.q, bf16[256,4096]{1,0:T(8,128)(2,1)S(1)} %get-tuple-element.49.v, bf16[4,256,128]{2,1,0:T(8,128)(2,1)S(1)} %shard_map.48.f0, bf16[4,256,128]{2,1,0:T(8,128)(2,1)S(1)} %collective-permute-done.9.f1, ...), custom_call_target="tpu_custom_call" | custom-call | tf_op jit(solution)/shard_map/pallas_call | solution.py:309
  43.3 1.7 %shard_map.56 = (bf16[8,256,256]{2,1,0:T(8,128)(2,1)S(1)}, f32[8,256,256]{2,1,0:T(8,128)S(1)}) custom-call(bf16[256,4096]{1,0:T(8,128)(2,1)S(1)} %get-tuple-element.51.q, bf16[256,4096]{1,0:T(8,128)(2,1)S(1)} %get-tuple-element.49.v, bf16[8,256,128]{2,1,0:T(8,128)(2,1)S(1)} %get-tuple-element.50.f0, bf16[8,256,128]{2,1,0:T(8,128)(2,1)S(1)} %collective-permute-done.f1, ...), custom_call_target="tpu_custom_call" | custom-call | tf_op jit(solution)/shard_map/pallas_call | solution.py:309
  48.1 1.6 %collective-permute-start.20 = (bf16[128,256]{1,0:T(8,128)(2,1)S(1)}, bf16[128,256]{1,0:T(8,128)(2,1)S(1)}, u32[]{:S(2)}, u32[]{:S(2)}) collective-permute-start(bf16[128,256]{1,0:T(8,128)(2,1)S(1)} %get-tuple-element.77), channel_id=1, source_target_pairs={{0,16},{4,20},{8,24},{12,28},{16,0},{20,4},{24,8},{28,12},{1,17},{... | collective-permute-start | bytes 196616 | tf_op jit(solution)/shard_map/ppermute | solution.py:284
  51.1 1.5 %shard_map.60 = (bf16[8,256,256]{2,1,0:T(8,128)(2,1)S(1)}, f32[8,256,256]{2,1,0:T(8,128)S(1)}) custom-call(bf16[256,4096]{1,0:T(8,128)(2,1)S(1)} %get-tuple-element.51.q, bf16[256,4096]{1,0:T(8,128)(2,1)S(1)} %get-tuple-element.49.v, bf16[4,256,128]{2,1,0:T(8,128)(2,1)S(1)} %collective-permute-done.2.f0, bf16[4,256,128]{2,1,0:T(8,128)(2,1)S(1)} %collective-permute-done.3.f1, ...), custom_call_target="tpu_custom_call" | custom-call | tf_op jit(solution)/shard_map/pallas_call | solution.py:309
  52.7 2.0 %collective-permute-done.20.refs_2_ = bf16[128,256]{1,0:T(8,128)(2,1)S(1)} collective-permute-done((bf16[128,256]{1,0:T(8,128)(2,1)S(1)}, bf16[128,256]{1,0:T(8,128)(2,1)S(1)}, u32[]{:S(2)}, u32[]{:S(2)}) %collective-permute-start.20) | collective-permute-done | bytes 65568 | tf_op jit(solution)/shard_map/ppermute | solution.py:284
  57.2 1.6 %collective-permute-start.24 = (bf16[528,256]{1,0:T(8,128)(2,1)S(1)}, bf16[528,256]{1,0:T(8,128)(2,1)S(1)}, u32[]{:S(2)}, u32[]{:S(2)}) collective-permute-start(bf16[528,256]{1,0:T(8,128)(2,1)S(1)} %get-tuple-element.85), channel_id=1, source_target_pairs={{0,4},{4,0},{8,12},{12,8},{16,20},{20,16},{24,28},{28,24},{1,5},{5... | collective-permute-start | bytes 811016 | tf_op jit(solution)/shard_map/ppermute | solution.py:284
  58.7 1.5 %collective-permute-start.22 = (bf16[528,256]{1,0:T(8,128)(2,1)S(1)}, bf16[528,256]{1,0:T(8,128)(2,1)S(1)}, u32[]{:S(2)}, u32[]{:S(2)}) collective-permute-start(bf16[528,256]{1,0:T(8,128)(2,1)S(1)} %get-tuple-element.82), channel_id=1, source_target_pairs={{0,2},{1,3},{2,0},{3,1},{4,6},{5,7},{6,4},{7,5},{8,10},{9,11},{10,... | collective-permute-start | bytes 811016 | tf_op jit(solution)/shard_map/ppermute | solution.py:281
  60.7 3.0 %collective-permute-done.24.refs_2_ = bf16[528,256]{1,0:T(8,128)(2,1)S(1)} collective-permute-done((bf16[528,256]{1,0:T(8,128)(2,1)S(1)}, bf16[528,256]{1,0:T(8,128)(2,1)S(1)}, u32[]{:S(2)}, u32[]{:S(2)}) %collective-permute-start.24) | collective-permute-done | bytes 270368 | tf_op jit(solution)/shard_map/ppermute | solution.py:284
  66.5 1.5 %collective-permute-done.22.refs_0_ = bf16[528,256]{1,0:T(8,128)(2,1)S(1)} collective-permute-done((bf16[528,256]{1,0:T(8,128)(2,1)S(1)}, bf16[528,256]{1,0:T(8,128)(2,1)S(1)}, u32[]{:S(2)}, u32[]{:S(2)}) %collective-permute-start.22) | collective-permute-done | bytes 270368 | tf_op jit(solution)/shard_map/ppermute | solution.py:281
  68.0 5.3 %collective-permute-done.23.refs_1_ = bf16[528,256]{1,0:T(8,128)(2,1)S(1)} collective-permute-done((bf16[528,256]{1,0:T(8,128)(2,1)S(1)}, bf16[528,256]{1,0:T(8,128)(2,1)S(1)}, u32[]{:S(2)}, u32[]{:S(2)}) %collective-permute-start.23) | collective-permute-done | bytes 270368 | tf_op jit(solution)/shard_map/ppermute | solution.py:296
  73.4 1.6 %copy-done = bf16[256,4096]{1,0:T(8,128)(2,1)S(1)} copy-done((bf16[256,4096]{1,0:T(8,128)(2,1)S(1)}, bf16[256,4096]{1,0:T(8,128)(2,1)}, u32[]{:S(2)}) %copy-start) | copy-done | bytes 2097176
  (67 shorter events, 24.1 us)
Async XLA Ops:
  1.4 9.5 %collective-permute-start.1 = (bf16[4,256,128]{2,1,0:T(8,128)(2,1)S(1)}, bf16[4,256,128]{2,1,0:T(8,128)(2,1)S(1)}, u32[]{:S(2)}, u32[]{:S(2)}) collective-permute-start(bf16[4,256,128]{2,1,0:T(8,128)(2,1)S(1)} %constant_dynamic-slice_fusion), channel_id=1, source_target_pairs={{0,2},{1,3},{2,0},{3,1},{4,6},{5,7},{6,4},{7,5},{8,10},{9,11},{10,... | collective-permute-start | bytes 786440 | tf_op jit(solution)/shard_map/ppermute | solution.py:281
  11.0 5.4 %collective-permute-start.9 = (bf16[4,256,128]{2,1,0:T(8,128)(2,1)S(1)}, bf16[4,256,128]{2,1,0:T(8,128)(2,1)S(1)}, u32[]{:S(2)}, u32[]{:S(2)}) collective-permute-start(bf16[4,256,128]{2,1,0:T(8,128)(2,1)S(1)} %shard_map.48.f0), channel_id=1, source_target_pairs={{0,1},{1,0},{2,3},{3,2},{4,5},{5,4},{6,7},{7,6},{8,9},{9,8},{10,11... | collective-permute-start | bytes 786440 | tf_op jit(solution)/shard_map/ppermute | solution.py:281
  11.1 8.7 %collective-permute-start.2 = (bf16[4,256,128]{2,1,0:T(8,128)(2,1)S(1)}, bf16[4,256,128]{2,1,0:T(8,128)(2,1)S(1)}, u32[]{:S(2)}, u32[]{:S(2)}) collective-permute-start(bf16[4,256,128]{2,1,0:T(8,128)(2,1)S(1)} %shard_map.48.f0), channel_id=1, source_target_pairs={{0,4},{4,0},{8,12},{12,8},{16,20},{20,16},{24,28},{28,24},{1,5},{5... | collective-permute-start | bytes 786440 | tf_op jit(solution)/shard_map/ppermute | solution.py:284
  13.4 6.4 %collective-permute-start.13 = (bf16[256,256]{1,0:T(8,128)(2,1)S(1)}, bf16[256,256]{1,0:T(8,128)(2,1)S(1)}, u32[]{:S(2)}, u32[]{:S(2)}) collective-permute-start(bf16[256,256]{1,0:T(8,128)(2,1)S(1)} %get-tuple-element.64), channel_id=1, source_target_pairs={{0,1},{1,0},{2,3},{3,2},{4,5},{5,4},{6,7},{7,6},{8,9},{9,8},{10,11... | collective-permute-start | bytes 393224 | tf_op jit(solution)/shard_map/ppermute | solution.py:281
  14.4 5.9 %collective-permute-start.14 = (bf16[272,256]{1,0:T(8,128)(2,1)S(1)}, bf16[272,256]{1,0:T(8,128)(2,1)S(1)}, u32[]{:S(2)}, u32[]{:S(2)}) collective-permute-start(bf16[272,256]{1,0:T(8,128)(2,1)S(1)} %get-tuple-element.65), channel_id=1, source_target_pairs={{0,1},{1,0},{2,3},{3,2},{4,5},{5,4},{6,7},{7,6},{8,9},{9,8},{10,11... | collective-permute-start | bytes 417800 | tf_op jit(solution)/shard_map/ppermute | solution.py:281
  14.8 9.0 %collective-permute-start.6 = (bf16[528,256]{1,0:T(8,128)(2,1)S(1)}, bf16[528,256]{1,0:T(8,128)(2,1)S(1)}, u32[]{:S(2)}, u32[]{:S(2)}) collective-permute-start(bf16[528,256]{1,0:T(8,128)(2,1)S(1)} %shard_map.49.refs_0_), channel_id=1, source_target_pairs={{0,2},{1,3},{2,0},{3,1},{4,6},{5,7},{6,4},{7,5},{8,10},{9,11},{10,... | collective-permute-start | bytes 811016 | tf_op jit(solution)/shard_map/ppermute | solution.py:281
  17.9 5.3 %collective-permute-start.11 = (bf16[272,256]{1,0:T(8,128)(2,1)S(1)}, bf16[272,256]{1,0:T(8,128)(2,1)S(1)}, u32[]{:S(2)}, u32[]{:S(2)}) collective-permute-start(bf16[272,256]{1,0:T(8,128)(2,1)S(1)} %get-tuple-element.62), channel_id=1, source_target_pairs={{0,1},{1,0},{2,3},{3,2},{4,5},{5,4},{6,7},{7,6},{8,9},{9,8},{10,11... | collective-permute-start | bytes 417800 | tf_op jit(solution)/shard_map/ppermute | solution.py:281
  20.4 9.5 %collective-permute-start.15 = (bf16[528,256]{1,0:T(8,128)(2,1)S(1)}, bf16[528,256]{1,0:T(8,128)(2,1)S(1)}, u32[]{:S(2)}, u32[]{:S(2)}) collective-permute-start(bf16[528,256]{1,0:T(8,128)(2,1)S(1)} %shard_map.54), channel_id=1, source_target_pairs={{0,6},{1,7},{2,4},{3,5},{4,2},{5,3},{6,0},{7,1},{8,14},{9,15},{10,... | collective-permute-start | bytes 811016 | tf_op jit(solution)/shard_map/ppermute | solution.py:296
  23.2 12.4 %collective-permute-start.12 = (bf16[528,256]{1,0:T(8,128)(2,1)S(1)}, bf16[528,256]{1,0:T(8,128)(2,1)S(1)}, u32[]{:S(2)}, u32[]{:S(2)}) collective-permute-start(bf16[528,256]{1,0:T(8,128)(2,1)S(1)} %shard_map.53), channel_id=1, source_target_pairs={{0,4},{4,0},{8,12},{12,8},{16,20},{20,16},{24,28},{28,24},{1,5},{5... | collective-permute-start | bytes 811016 | tf_op jit(solution)/shard_map/ppermute | solution.py:284
  25.8 34.9 %collective-permute-start.26 = (bf16[528,256]{1,0:T(8,128)(2,1)S(1)}, bf16[528,256]{1,0:T(8,128)(2,1)S(1)}, u32[]{:S(2)}, u32[]{:S(2)}) collective-permute-start(bf16[528,256]{1,0:T(8,128)(2,1)S(1)} %get-tuple-element.57.mine), channel_id=1, source_target_pairs={{0,1},{1,0},{2,3},{3,2},{4,5},{5,4},{6,7},{7,6},{8,9},{9,8},{10,11... | collective-permute-start | bytes 811016 | tf_op jit(solution)/shard_map/ppermute | solution.py:281
  35.8 9.2 %collective-permute-start.16 = (bf16[144,256]{1,0:T(8,128)(2,1)S(1)}, bf16[144,256]{1,0:T(8,128)(2,1)S(1)}, u32[]{:S(2)}, u32[]{:S(2)}) collective-permute-start(bf16[144,256]{1,0:T(8,128)(2,1)S(1)} %get-tuple-element.70), channel_id=1, source_target_pairs={{0,8},{4,12},{8,0},{12,4},{16,24},{20,28},{24,16},{28,20},{1,9},{5... | collective-permute-start | bytes 221192 | tf_op jit(solution)/shard_map/ppermute | solution.py:284
  37.6 8.0 %collective-permute-start.17 = (bf16[144,256]{1,0:T(8,128)(2,1)S(1)}, bf16[144,256]{1,0:T(8,128)(2,1)S(1)}, u32[]{:S(2)}, u32[]{:S(2)}) collective-permute-start(bf16[144,256]{1,0:T(8,128)(2,1)S(1)} %get-tuple-element.71), channel_id=1, source_target_pairs={{0,16},{4,20},{8,24},{12,28},{16,0},{20,4},{24,8},{28,12},{1,17},{... | collective-permute-start | bytes 221192 | tf_op jit(solution)/shard_map/ppermute | solution.py:284
  40.2 6.3 %collective-permute-start.18 = (bf16[144,256]{1,0:T(8,128)(2,1)S(1)}, bf16[144,256]{1,0:T(8,128)(2,1)S(1)}, u32[]{:S(2)}, u32[]{:S(2)}) collective-permute-start(bf16[144,256]{1,0:T(8,128)(2,1)S(1)} %get-tuple-element.66.rest_0_), channel_id=1, source_target_pairs={{0,24},{4,28},{8,16},{12,20},{16,8},{20,12},{24,0},{28,4},{1,25},{... | collective-permute-start | bytes 221192 | tf_op jit(solution)/shard_map/ppermute | solution.py:284
  46.7 6.0 %collective-permute-start.19 = (bf16[128,256]{1,0:T(8,128)(2,1)S(1)}, bf16[128,256]{1,0:T(8,128)(2,1)S(1)}, u32[]{:S(2)}, u32[]{:S(2)}) collective-permute-start(bf16[128,256]{1,0:T(8,128)(2,1)S(1)} %get-tuple-element.76), channel_id=1, source_target_pairs={{0,8},{4,12},{8,0},{12,4},{16,24},{20,28},{24,16},{28,20},{1,9},{5... | collective-permute-start | bytes 196616 | tf_op jit(solution)/shard_map/ppermute | solution.py:284
  48.1 6.6 %collective-permute-start.20 = (bf16[128,256]{1,0:T(8,128)(2,1)S(1)}, bf16[128,256]{1,0:T(8,128)(2,1)S(1)}, u32[]{:S(2)}, u32[]{:S(2)}) collective-permute-start(bf16[128,256]{1,0:T(8,128)(2,1)S(1)} %get-tuple-element.77), channel_id=1, source_target_pairs={{0,16},{4,20},{8,24},{12,28},{16,0},{20,4},{24,8},{28,12},{1,17},{... | collective-permute-start | bytes 196616 | tf_op jit(solution)/shard_map/ppermute | solution.py:284
  49.7 6.2 %collective-permute-start.21 = (bf16[128,256]{1,0:T(8,128)(2,1)S(1)}, bf16[128,256]{1,0:T(8,128)(2,1)S(1)}, u32[]{:S(2)}, u32[]{:S(2)}) collective-permute-start(bf16[128,256]{1,0:T(8,128)(2,1)S(1)} %get-tuple-element.78.rest_0_), channel_id=1, source_target_pairs={{0,24},{4,28},{8,16},{12,20},{16,8},{20,12},{24,0},{28,4},{1,25},{... | collective-permute-start | bytes 196616 | tf_op jit(solution)/shard_map/ppermute | solution.py:284
  57.2 6.5 %collective-permute-start.24 = (bf16[528,256]{1,0:T(8,128)(2,1)S(1)}, bf16[528,256]{1,0:T(8,128)(2,1)S(1)}, u32[]{:S(2)}, u32[]{:S(2)}) collective-permute-start(bf16[528,256]{1,0:T(8,128)(2,1)S(1)} %get-tuple-element.85), channel_id=1, source_target_pairs={{0,4},{4,0},{8,12},{12,8},{16,20},{20,16},{24,28},{28,24},{1,5},{5... | collective-permute-start | bytes 811016 | tf_op jit(solution)/shard_map/ppermute | solution.py:284
  58.7 4.9 %collective-permute-start.25 = (bf16[528,256]{1,0:T(8,128)(2,1)S(1)}, bf16[528,256]{1,0:T(8,128)(2,1)S(1)}, u32[]{:S(2)}, u32[]{:S(2)}) collective-permute-start(bf16[528,256]{1,0:T(8,128)(2,1)S(1)} %get-tuple-element.87.refs_2_), channel_id=1, source_target_pairs={{0,1},{1,0},{2,3},{3,2},{4,5},{5,4},{6,7},{7,6},{8,9},{9,8},{10,11... | collective-permute-start | bytes 811016 | tf_op jit(solution)/shard_map/ppermute | solution.py:281
  58.7 9.3 %collective-permute-start.22 = (bf16[528,256]{1,0:T(8,128)(2,1)S(1)}, bf16[528,256]{1,0:T(8,128)(2,1)S(1)}, u32[]{:S(2)}, u32[]{:S(2)}) collective-permute-start(bf16[528,256]{1,0:T(8,128)(2,1)S(1)} %get-tuple-element.82), channel_id=1, source_target_pairs={{0,2},{1,3},{2,0},{3,1},{4,6},{5,7},{6,4},{7,5},{8,10},{9,11},{10,... | collective-permute-start | bytes 811016 | tf_op jit(solution)/shard_map/ppermute | solution.py:281
  60.3 13.1 %collective-permute-start.23 = (bf16[528,256]{1,0:T(8,128)(2,1)S(1)}, bf16[528,256]{1,0:T(8,128)(2,1)S(1)}, u32[]{:S(2)}, u32[]{:S(2)}) collective-permute-start(bf16[528,256]{1,0:T(8,128)(2,1)S(1)} %get-tuple-element.83), channel_id=1, source_target_pairs={{0,6},{1,7},{2,4},{3,5},{4,2},{5,3},{6,0},{7,1},{8,14},{9,15},{10,... | collective-permute-start | bytes 811016 | tf_op jit(solution)/shard_map/ppermute | solution.py:296
  60.7 14.4 %collective-permute-start.32 = (bf16[528,256]{1,0:T(8,128)(2,1)S(1)}, bf16[528,256]{1,0:T(8,128)(2,1)S(1)}, u32[]{:S(2)}, u32[]{:S(2)}) collective-permute-start(bf16[528,256]{1,0:T(8,128)(2,1)S(1)} %get-tuple-element.60.mine), channel_id=1, source_target_pairs={{0,1},{1,0},{2,3},{3,2},{4,5},{5,4},{6,7},{7,6},{8,9},{9,8},{10,11... | collective-permute-start | bytes 811016 | tf_op jit(solution)/shard_map/ppermute | solution.py:281
  63.7 14.3 %collective-permute-start.28 = (bf16[528,256]{1,0:T(8,128)(2,1)S(1)}, bf16[528,256]{1,0:T(8,128)(2,1)S(1)}, u32[]{:S(2)}, u32[]{:S(2)}) collective-permute-start(bf16[528,256]{1,0:T(8,128)(2,1)S(1)} %get-tuple-element.54.mine), channel_id=1, source_target_pairs={{0,1},{1,0},{2,3},{3,2},{4,5},{5,4},{6,7},{7,6},{8,9},{9,8},{10,11... | collective-permute-start | bytes 811016 | tf_op jit(solution)/shard_map/ppermute | solution.py:281
  63.7 11.9 %collective-permute-start.31 = (bf16[528,256]{1,0:T(8,128)(2,1)S(1)}, bf16[528,256]{1,0:T(8,128)(2,1)S(1)}, u32[]{:S(2)}, u32[]{:S(2)}) collective-permute-start(bf16[528,256]{1,0:T(8,128)(2,1)S(1)} %collective-permute-done.24.refs_2_), channel_id=1, source_target_pairs={{0,1},{1,0},{2,3},{3,2},{4,5},{5,4},{6,7},{7,6},{8,9},{9,8},{10,11... | collective-permute-start | bytes 811016 | tf_op jit(solution)/shard_map/ppermute | solution.py:281
  68.0 9.9 %collective-permute-start.30 = (bf16[528,256]{1,0:T(8,128)(2,1)S(1)}, bf16[528,256]{1,0:T(8,128)(2,1)S(1)}, u32[]{:S(2)}, u32[]{:S(2)}) collective-permute-start(bf16[528,256]{1,0:T(8,128)(2,1)S(1)} %get-tuple-element.63.mine), channel_id=1, source_target_pairs={{0,1},{1,0},{2,3},{3,2},{4,5},{5,4},{6,7},{7,6},{8,9},{9,8},{10,11... | collective-permute-start | bytes 811016 | tf_op jit(solution)/shard_map/ppermute | solution.py:281
  (10 other events, 25.1 us)

commit v4 on v3

--- a/solution.py
+++ b/solution.py
@@ -11,7 +11,7 @@
 F32, BF16 = jnp.float32, jnp.bfloat16
 LOG2E = math.log2(math.e)
 TOTAL_ROWS = 16
-VMEM = 12 * 1024 * 1024
+VMEM = 6 * 1024 * 1024
 
 
 def feature_map(x, w):
@@ -45,21 +45,25 @@
     return ((pos[0] ^ key[0] ^ flip) * 2 + (pos[1] ^ core)) * ny + part, part
 
 
-def heads_of(pos, key, shape, f0, f1):
+def heads_of(pos, key, shape, f0, *f1):
     nx, ny, group, size = shape
-    for core, f in ((1, f1), (0, f0)):
+    for core, fs in ((1, f1), (0, [f0])):
         place, part = place_of(pos, key, nx, ny, core)
-        first = 0 if f.shape[0] == group else part * group
+        held = sum(f.shape[0] for f in fs)
+        first = 0 if held == group else part * group
         for h in range(group):
             start = pl.multiple_of((place * group + h) * size, size)
-            yield (1 - core) * group + h, pl.ds(start, size), f, first + h
-
-
-def states_kernel(key, shape, waits, k, v, f0, f1, phi, *sums):
+            f, at = fs[0], first + h
+            if len(fs) > 1:
+                f, at = fs[h // fs[0].shape[0]], h % fs[0].shape[0]
+            yield (1 - core) * group + h, pl.ds(start, size), f, at
+
+
+def states_kernel(key, shape, waits, k, v, fs, phi, *sums):
     nx, ny, group, size = shape
     *others, mine = sums
     pos = position(nx, ny)
-    heads = list(heads_of(pos, key, shape, f0, f1))
+    heads = list(heads_of(pos, key, shape, *fs))
     totals = []
     for i, cols, f, at in heads:
         if i % group == 0:
@@ -114,7 +118,7 @@
         for copy in copies[stage]:
             copy.wait()
 
-    states_kernel(key, shape, waits, k, v, f, f1, *outs)
+    states_kernel(key, shape, waits, k, v, [f, f1], *outs)
 
 
 def second_kernel(key, shape, q_far, k, v, f0, f1, *refs):
@@ -126,18 +130,19 @@
         if stage == 3:
             copy.wait()
 
-    states_kernel(key, shape, waits, k, v, f0, f1, *outs)
-
-
-def later_kernel(extra, key, shape, k, v, f0, f1, *refs):
-    states_kernel(key, shape, lambda stage: None, k, v, f0, f1, *refs[extra:])
-
-
-def inner_kernel(key, shape, q, v, f0, f1, phi_k, *rest):
+    states_kernel(key, shape, waits, k, v, [f0, f1], *outs)
+
+
+def later_kernel(count, extra, key, shape, k, v, *refs):
+    fs, outs = refs[:count], refs[count + extra :]
+    states_kernel(key, shape, lambda stage: None, k, v, fs, *outs)
+
+
+def inner_kernel(count, key, shape, q, v, phi_k, *rest):
     phi_q, inner, weights = rest[-3:]
     nx, ny, group, size = shape
     tokens = q.shape[0]
-    heads = list(heads_of(position(nx, ny), key, shape, f0, f1))
+    heads = list(heads_of(position(nx, ny), key, shape, *rest[:count]))
     for i, cols, f, at in heads:
         phi_q[i] = feature_map(q[:, cols], f[at])
     row = lax.broadcasted_iota(jnp.int32, (tokens, tokens), 0)
@@ -157,8 +162,8 @@
         )
 
 
-def output_kernel(jobs, shape, *refs):
-    out, ready, sems = refs[-3:]
+def output_kernel(jobs, shape, extra, *refs):
+    out, *marks, ready, sems = refs[5 * len(jobs) + extra :]
     nx, ny, group, size = shape
     pos = position(nx, ny)
     add = (pos[1] == 1).astype(F32)
@@ -195,6 +200,8 @@
         )
         copy.start()
         copies.append(copy)
+    for mark in marks:
+        mark[...] = jnp.zeros(mark.shape, F32)
     for copy in copies:
         copy.wait()
 
@@ -211,6 +218,20 @@
         rows = slice(start, start + other.shape[0])
         start = rows.stop
         out[rows] = (mine[rows].astype(F32) + other[...].astype(F32)).astype(BF16)
+
+
+def row_kernel(nx, ny, *refs):
+    pieces, out, before = refs[:nx], refs[nx], refs[nx + 1 :]
+    x = position(nx, ny)[0]
+    total = pieces[0][...].astype(F32)
+    for piece in pieces[1:]:
+        total = total + piece[...].astype(F32)
+    out[...] = total.astype(BF16)
+    for n, out in enumerate(before):
+        total = jnp.zeros(out.shape, F32)
+        for ex, piece in enumerate(pieces):
+            total = total + jnp.where((x ^ ex) < n + 1, piece[...].astype(F32), 0.0)
+        out[...] = total.astype(BF16)
 
 
 def plane_kernel(count, zrows, ny, *refs):
@@ -228,7 +249,7 @@
 
 
 def prefix_kernel(count, zrows, ny, *refs):
-    heard, outs, totals = refs[:count], refs[-1 - count : -1], refs[-1]
+    heard, outs, totals = refs[count - 1 :: -1], refs[-1 - count : -1], refs[-1]
     z = position(1, ny)[3]
     for j, out in enumerate(outs):
         total = jnp.zeros(out.shape, F32)
@@ -243,8 +264,9 @@
 
 def place_kernel(nx, ny, count, zrows, *refs):
     keys = [(dx, dy) for dx in range(nx) for dy in range(ny)]
-    prefix, totals = refs[:count], refs[count]
-    pieces, outs = refs[count + 1 : count + 1 + len(keys)], refs[-1 - len(keys) : -1]
+    prefix, totals = refs[count - 1 :: -1], refs[count]
+    row_sums = refs[count + 1 : count + 1 + ny]
+    before, outs = refs[count + 1 + ny :], refs[-1 - len(keys) : -1]
     held = refs[-1]
     x, _, y, z = position(nx, ny)
     for j in range(count):
@@ -252,11 +274,12 @@
         held[pl.ds(start, zrows)] = prefix[j][...].astype(F32)
     held[count * zrows :] = totals[...]
     for (dx, dy), out in zip(keys, outs):
-        target = (y ^ dy) * nx + (x ^ dx)
         total = held[...]
-        for (ex, ey), piece in zip(keys, pieces):
-            source = (y ^ ey) * nx + (x ^ ex)
-            total = total + jnp.where(source < target, piece[...].astype(F32), 0.0)
+        for ey, row_sum in enumerate(row_sums):
+            total = total + jnp.where((y ^ ey) < (y ^ dy), row_sum[...].astype(F32), 0.0)
+        for n in range(nx - 1):
+            part = before[dy * (nx - 1) + n][...].astype(F32)
+            total = total + jnp.where((x ^ dx) == n + 1, part, 0.0)
         out[...] = total.astype(BF16)
 
 
@@ -275,7 +298,6 @@
     rows = srows + TOTAL_ROWS
     plane = [(dx, dy) for dx in range(nx) for dy in range(ny)]
 
-    y = position(nx, ny)[2]
 
     def head_swap(a, bits):
         return lax.ppermute(a, "head", [(i, i ^ bits) for i in range(heads)])
@@ -310,7 +332,7 @@
             kernel,
             out_shape=out,
             in_specs=[far] * len(there) + [near] * len(held) + [anywhere] * len(after),
-            out_specs=jax.tree.map(lambda _: outs, out),
+            out_specs=jax.tree.map(lambda _: outs, out) if outs is near else outs,
             scratch_shapes=scratch,
             input_output_aliases=alias,
             compiler_params=pltpu.CompilerParams(vmem_limit_bytes=VMEM),
@@ -318,7 +340,7 @@
 
     def tie(arrays, after):
         kernel = functools.partial(tie_kernel, len(arrays))
-        return call(kernel, [jax.ShapeDtypeStruct(a.shape, a.dtype) for a in arrays], arrays, [after])
+        return call(kernel, [jax.ShapeDtypeStruct(a.shape, a.dtype) for a in arrays], arrays, after)
 
     def per_head(a, b):
         return jax.ShapeDtypeStruct((cores * group, a, b), BF16)
@@ -355,7 +377,7 @@
             near_q.append(loaded)
         else:
             phi_k[key], *sums = call(
-                functools.partial(later_kernel, len(after), key, shape),
+                functools.partial(later_kernel, len(directions(key)), len(after), key, shape),
                 outs,
                 [*near_k[:2], *directions(key)],
                 after,
@@ -364,7 +386,7 @@
         other = [head_swap(a, 1) for a in other]
         theirs[key] = [[other[0], other[-1]], [head_swap(mine, 1)] * 2]
         piece[key] = call(chip_kernel, whole, [mine, *other])
-        got[key] = piece[key] if key == (0, 0) else plane_swap(piece[key], *key)
+        got[key] = head_swap(piece[key], key[0] * cores) if key[0] else piece[key]
         return mine
 
     def directions(key):
@@ -372,65 +394,87 @@
 
     def inner(key, after=()):
         phi_w[key] = call(
-            functools.partial(inner_kernel, key, shape),
+            functools.partial(inner_kernel, len(directions(key)), key, shape),
             [
                 per_head(tokens, count),
                 jax.ShapeDtypeStruct((cores * group, tokens, 2 * size), F32),
             ],
-            [near_q[0], near_k[1], *directions(key), phi_k[key]],
+            [near_q[0], near_k[1], phi_k[key], *directions(key)],
             after,
             scratch=[pltpu.VMEM((cores * group, tokens, tokens), BF16)],
         )
         return phi_w[key][0]
 
     near_dirs = head_swap(features, 1)
-    first = [(flip, dy) for dy in range(ny)]
+    first = [(flip, dy) for dy in reversed(range(ny))]
     later = [(dx, dy) for dx in range(nx) for dy in reversed(range(ny)) if dx != flip]
     for key in first:
         states(key)
+    ready = [piece[first[0]], phi_k[first[-1]]]
     for ox in range(1, nx):
         if ny == 2:
-            part = lax.dynamic_slice_in_dim(features, (y ^ 1) * group, group, 0)
-            (part,) = tie([head_swap(part, ox * cores)], phi_k[first[-1]])
+            part = lax.dynamic_slice_in_dim(features, (position(nx, ny)[2] ^ 1) * group, group, 0)
+            (part,) = tie([head_swap(part, ox * cores)], ready)
             rest = seq_swap(part, 1)
             dirs[ox ^ flip, 1] = (part, head_swap(part, 1))
             dirs[ox ^ flip, 0] = (rest, head_swap(rest, 1))
         else:
-            (full,) = tie([head_swap(features, ox * cores)], phi_k[first[-1]])
+            (full,) = tie([head_swap(features, ox * cores)], ready)
             full = (full, head_swap(full, 1))
             for dy in range(ny):
                 dirs[ox ^ flip, dy] = full
-
-    for i, key in enumerate(later):
-        states(key, [piece[first[0]] if i == 0 else got[first[0]]])
-
+    for key in later:
+        states(key, [piece[first[0]]])
+
+    rows_of, before = {}, {}
+    for dy in reversed(range(ny)):
+        sums, *before[dy] = call(
+            functools.partial(row_kernel, nx, ny),
+            [whole] * nx,
+            [got[dx, dy] for dx in range(nx)],
+        )
+        rows_of[dy] = seq_swap(sums, dy) if dy else sums
     summed = call(
-        functools.partial(plane_kernel, len(plane), zrows, ny),
+        functools.partial(plane_kernel, ny, zrows, ny),
         [jax.ShapeDtypeStruct((zrows + TOTAL_ROWS, count), BF16)] * nz,
-        [got[key] for key in plane],
+        [rows_of[dy] for dy in range(ny)],
         scratch=[pltpu.VMEM((rows, count), F32)],
     )
-    heard = [a if j == 0 else seq_swap(a, j * ny) for j, a in enumerate(summed)]
+
+    def exchange(parts):
+        heard = [seq_swap(parts[j], j * ny) for j in reversed(range(1, nz))]
+        return [parts[0], *reversed(heard)]
+
+    heard = exchange(summed)
     done = [inner(key, [summed[-1]]) for key in [*first, *later[:-1]]]
+    for dy in range(1, ny):
+        before[dy] = [seq_swap(a, dy) for a in tie(before[dy], [summed[0]])] if nx > 1 else []
     *prefix, totals = call(
         functools.partial(prefix_kernel, nz, zrows, ny),
         [jax.ShapeDtypeStruct((zrows, count), BF16)] * nz
         + [jax.ShapeDtypeStruct((TOTAL_ROWS, count), F32)],
-        heard,
-        done,
+        heard[::-1],
+        done + [a for dy in range(1, ny) for a in before[dy]],
     )
     done = [inner(later[-1], [prefix[-1]])] if later else []
-    prefix = [a if j == 0 else seq_swap(a, j * ny) for j, a in enumerate(prefix)]
+    prefix = exchange(prefix)
     placed = call(
         functools.partial(place_kernel, nx, ny, nz, zrows),
         [whole] * len(plane),
-        [*prefix, totals, *[got[key] for key in plane]],
+        [
+            *prefix[::-1],
+            totals,
+            *[rows_of[dy] for dy in range(ny)],
+            *[a for dy in range(ny) for a in before[dy]],
+        ],
         done,
         scratch=[pltpu.VMEM((rows, count), F32)],
     )
 
+    placed = dict(zip(plane, placed))
     result = {
-        key: a if key == (0, 0) else plane_swap(a, *key) for key, a in zip(plane, placed)
+        key: plane_swap(placed[key], *key) if any(key) else placed[key]
+        for key in reversed(plane)
     }
     batches = [[((0, 0), 0), ((0, 0), 1)]]
     batches += [[((0, dy), 0)] for dy in range(1, ny)]
@@ -444,16 +488,17 @@
         args = []
         if i == tied:
             keys = [key for key in plane if key[0]]
-            result.update(zip(keys, tie([result[key] for key in keys], out)))
+            result.update(zip(keys, tie([result[key] for key in keys], mark)))
         for key, core in jobs:
             base = head_swap(result[key], 1) if core else result[key]
             args += [*phi_w[key], base, *theirs[key][core]]
-        out = call(
-            functools.partial(output_kernel, jobs, shape),
-            jax.ShapeDtypeStruct((tokens, width), BF16),
+        marked = [pltpu.VMEM((8, 128), F32)] if i == tied - 1 else []
+        out, *mark = call(
+            functools.partial(output_kernel, jobs, shape, int(i > 0)),
+            [jax.ShapeDtypeStruct((tokens, width), BF16), *marked],
             args,
             [] if out is None else [out],
-            anywhere,
+            [anywhere] + [near] * len(marked),
             [
                 pltpu.VMEM((len(jobs), tokens, group * size), BF16),
                 pltpu.SemaphoreType.DMA((len(jobs),)),

time: 79.6 us -> 73.8 us (0.927)
  waiting for transfers between devices: 29.5 us -> 23.9 us
  starting transfers between devices: 25.5 us -> 27.1 us
  local copies, waits for them, and re-layouts: 2.56 us -> 0.97 us
    ppermute x9 -> x10, waiting for transfers between devices: 15.2 us -> 12.6 us  [seq_swap(): return lax.ppermute(a, 'seq', [(i, i ^ bits) for i in range(seqs)])]
    ppermute x2 -> x1, waiting for transfers between devices: 8.29 us -> 6.36 us  [plane_swap(): return lax.ppermute(a, ('seq', 'head'), pairs)]
    ppermute x22 -> x23, starting transfers between devices: 9.44 us -> 11.2 us  [head_swap(): return lax.ppermute(a, 'head', [(i, i ^ bits) for i in range(heads)])]
    ppermute x2 -> x1, starting transfers between devices: 3.21 us -> 1.5 us  [plane_swap(): return lax.ppermute(a, ('seq', 'head'), pairs)]
    unnamed x2 -> x0, local copies, waits for them, and re-layouts: 1.59 us -> none
    ppermute x9 -> x10, starting transfers between devices: 12.9 us -> 14.4 us  [seq_swap(): return lax.ppermute(a, 'seq', [(i, i ^ bits) for i in range(seqs)])]
    ppermute x22 -> x23, waiting for transfers between devices: 5.99 us -> 4.96 us  [head_swap(): return lax.ppermute(a, 'head', [(i, i ^ bits) for i in range(heads)])]
    pallas_call x22 -> x25, Pallas kernels: 21.4 us -> 21.3 us  [call(): pl.pallas_call(kernel, out_shape=out, in_specs=[far] * len(there) + [near...]
  transfers between devices with their start and end apart: 33 -> 34, of which waited for: 13 -> 12; matrix products, arithmetic and copies ran while one was open for 1% -> 1% of each run, Pallas kernels for 25% -> 27%
where the time goes in v4:
time: 73.8 us; the launch traced here: 73.6 us
  starting transfers between devices  27.1 us (37%)
  waiting for transfers between devices  23.9 us (32%)
  Pallas kernels  21.3 us (29%)
  local copies, waits for them, and re-layouts  0.97 us (1%)
    pallas_call x25, Pallas kernels, call(): pl.pallas_call(kernel, out_shape=out, in_specs=[far] * len(there) + [near...  21.3 us
    ppermute x10, starting transfers between devices, seq_swap(): return lax.ppermute(a, 'seq', [(i, i ^ bits) for i in range(seqs)])  14.4 us
    ppermute x10, waiting for transfers between devices, seq_swap(): return lax.ppermute(a, 'seq', [(i, i ^ bits) for i in range(seqs)])  12.6 us
    ppermute x23, starting transfers between devices, head_swap(): return lax.ppermute(a, 'head', [(i, i ^ bits) for i in range(heads)])  11.2 us
    ppermute x1, waiting for transfers between devices, plane_swap(): return lax.ppermute(a, ('seq', 'head'), pairs)  6.36 us
    ppermute x23, waiting for transfers between devices, head_swap(): return lax.ppermute(a, 'head', [(i, i ^ bits) for i in range(heads)])  4.96 us
    ppermute x1, starting transfers between devices, plane_swap(): return lax.ppermute(a, ('seq', 'head'), pairs)  1.5 us
  transfers between devices with their start and end apart: 34, of which 12 were waited for; matrix products, arithmetic and copies ran while one was open for 1% of the time, Pallas kernels for 27%

profile of v4, /device:TPU:0, one launch (start us, length us, event | category | flops | bytes accessed | tf_op | source)
XLA Modules:
  0.0 73.6 jit_solution(2158890789143637971)
XLA Ops:
  1.4 2.6 %collective-permute-start.1 = (bf16[4,256,128]{2,1,0:T(8,128)(2,1)S(1)}, bf16[4,256,128]{2,1,0:T(8,128)(2,1)S(1)}, u32[]{:S(2)}, u32[]{:S(2)}) collective-permute-start(bf16[4,256,128]{2,1,0:T(8,128)(2,1)S(1)} %constant_dynamic-slice_fusion), channel_id=1, source_target_pairs={{0,2},{1,3},{2,0},{3,1},{4,6},{5,7},{6,4},{7,5},{8,10},{9,11},{10,... | collective-permute-start | bytes 786440 | tf_op jit(solution)/shard_map/ppermute | solution.py:303
  4.0 2.7 %shard_map.46 = (bf16[8,256,256]{2,1,0:T(8,128)(2,1)S(1)}, bf16[256,256]{1,0:T(8,128)(2,1)S(1)}, bf16[272,256]{1,0:T(8,128)(2,1)S(1)}, bf16[528,256]{1,0:T(8,128...) custom-call(bf16[256,4096]{1,0:T(8,128)(2,1)} %bitcast.5, ...), custom_call_target="tpu_custom_call" | custom-call | tf_op jit(solution)/shard_map/pallas_call | solution.py:331
  7.2 1.6 %shard_map.47 = (bf16[8,256,256]{2,1,0:T(8,128)(2,1)S(1)}, bf16[256,256]{1,0:T(8,128)(2,1)S(1)}, bf16[272,256]{1,0:T(8,128)(2,1)S(1)}, bf16[528,256]{1,0:T(8,128)(2,1)S(1)}, bf16[256,4096]{1,0:T(8,128)(2,1)S(1)}) custom-call(bf16[256,4096]{1,0:T(8,128)(2,1)} %bitcast.4, bf16[256,4096]{1,0:T(8,128)(2,1)S(1)} %get-tuple-element.54.k, ...), custom_call_target="tpu_custom_call" | custom-call | tf_op jit(solution)/shard_map/pallas_call | solution.py:331
  9.0 2.0 %collective-permute-done.1.refs_0_ = bf16[4,256,128]{2,1,0:T(8,128)(2,1)S(1)} collective-permute-done((bf16[4,256,128]{2,1,0:T(8,128)(2,1)S(1)}, bf16[4,256,128]{2,1,0:T(8,128)(2,1)S(1)}, u32[]{:S(2)}, u32[]{:S(2)}) %collective-permute-start.1) | collective-permute-done | bytes 262176 | tf_op jit(solution)/shard_map/ppermute | solution.py:303
  11.1 1.8 %collective-permute-start.4 = (bf16[4,256,128]{2,1,0:T(8,128)(2,1)S(1)}, bf16[4,256,128]{2,1,0:T(8,128)(2,1)S(1)}, u32[]{:S(2)}, u32[]{:S(2)}) collective-permute-start(bf16[4,256,128]{2,1,0:T(8,128)(2,1)S(1)} %shard_map.49.refs_0_.rest_0_), channel_id=1, source_target_pairs={{0,4},{4,0},{8,12},{12,8},{16,20},{20,16},{24,28},{28,24},{1,5},{5... | collective-permute-start | bytes 786440 | tf_op jit(solution)/shard_map/ppermute | solution.py:306
  12.9 1.5 %collective-permute-start.14 = (bf16[528,256]{1,0:T(8,128)(2,1)S(1)}, bf16[528,256]{1,0:T(8,128)(2,1)S(1)}, u32[]{:S(2)}, u32[]{:S(2)}) collective-permute-start(bf16[528,256]{1,0:T(8,128)(2,1)S(1)} %shard_map.48.refs_1_.refs_2_), channel_id=1, source_target_pairs={{0,2},{1,3},{2,0},{3,1},{4,6},{5,7},{6,4},{7,5},{8,10},{9,11},{10,... | collective-permute-start | bytes 811016 | tf_op jit(solution)/shard_map/ppermute | solution.py:303
  16.5 3.3 %collective-permute-done.4.refs_0_.rest_0_ = bf16[4,256,128]{2,1,0:T(8,128)(2,1)S(1)} collective-permute-done((bf16[4,256,128]{2,1,0:T(8,128)(2,1)S(1)}, bf16[4,256,128]{2,1,0:T(8,128)(2,1)S(1)}, u32[]{:S(2)}, u32[]{:S(2)}) %collective-permute-start.4) | collective-permute-done | bytes 262176 | tf_op jit(solution)/shard_map/ppermute | solution.py:306
  20.4 1.8 %collective-permute-start.10 = (bf16[528,256]{1,0:T(8,128)(2,1)S(1)}, bf16[528,256]{1,0:T(8,128)(2,1)S(1)}, u32[]{:S(2)}, u32[]{:S(2)}) collective-permute-start(bf16[528,256]{1,0:T(8,128)(2,1)S(1)} %shard_map.52), channel_id=1, source_target_pairs={{0,2},{1,3},{2,0},{3,1},{4,6},{5,7},{6,4},{7,5},{8,10},{9,11},{10,... | collective-permute-start | bytes 811016 | tf_op jit(solution)/shard_map/ppermute | solution.py:303
  22.4 1.6 %collective-permute-start.15 = (bf16[528,256]{1,0:T(8,128)(2,1)S(1)}, bf16[528,256]{1,0:T(8,128)(2,1)S(1)}, u32[]{:S(2)}, u32[]{:S(2)}) collective-permute-start(bf16[528,256]{1,0:T(8,128)(2,1)S(1)} %get-tuple-element.72), channel_id=1, source_target_pairs={{0,4},{4,0},{8,12},{12,8},{16,20},{20,16},{24,28},{28,24},{1,5},{5... | collective-permute-start | bytes 811016 | tf_op jit(solution)/shard_map/ppermute | solution.py:306
  27.2 1.7 %collective-permute-done.10.refs_1_ = bf16[528,256]{1,0:T(8,128)(2,1)S(1)} collective-permute-done((bf16[528,256]{1,0:T(8,128)(2,1)S(1)}, bf16[528,256]{1,0:T(8,128)(2,1)S(1)}, u32[]{:S(2)}, u32[]{:S(2)}) %collective-permute-start.10) | collective-permute-done | bytes 270368 | tf_op jit(solution)/shard_map/ppermute | solution.py:303
  29.0 1.6 %collective-permute-done.15.refs_1_.refs_6_ = bf16[528,256]{1,0:T(8,128)(2,1)S(1)} collective-permute-done((bf16[528,256]{1,0:T(8,128)(2,1)S(1)}, bf16[528,256]{1,0:T(8,128)(2,1)S(1)}, u32[]{:S(2)}, u32[]{:S(2)}) %collective-permute-start.15) | collective-permute-done | bytes 270368 | tf_op jit(solution)/shard_map/ppermute | solution.py:306
  30.8 1.6 %collective-permute-start.19 = (bf16[528,256]{1,0:T(8,128)(2,1)S(1)}, bf16[528,256]{1,0:T(8,128)(2,1)S(1)}, u32[]{:S(2)}, u32[]{:S(2)}) collective-permute-start(bf16[528,256]{1,0:T(8,128)(2,1)S(1)} %shard_map.61), channel_id=1, source_target_pairs={{0,4},{4,0},{8,12},{12,8},{16,20},{20,16},{24,28},{28,24},{1,5},{5... | collective-permute-start | bytes 811016 | tf_op jit(solution)/shard_map/ppermute | solution.py:306
  32.3 2.6 %collective-permute-start.17 = (bf16[144,256]{1,0:T(8,128)(2,1)S(1)}, bf16[144,256]{1,0:T(8,128)(2,1)S(1)}, u32[]{:S(2)}, u32[]{:S(2)}) collective-permute-start(bf16[144,256]{1,0:T(8,128)(2,1)S(1)} %get-tuple-element.76), channel_id=1, source_target_pairs={{0,16},{4,20},{8,24},{12,28},{16,0},{20,4},{24,8},{28,12},{1,17},{... | collective-permute-start | bytes 221192 | tf_op jit(solution)/shard_map/ppermute | solution.py:306
  34.9 1.6 %collective-permute-start.18 = (bf16[144,256]{1,0:T(8,128)(2,1)S(1)}, bf16[144,256]{1,0:T(8,128)(2,1)S(1)}, u32[]{:S(2)}, u32[]{:S(2)}) collective-permute-start(bf16[144,256]{1,0:T(8,128)(2,1)S(1)} %get-tuple-element.77), channel_id=1, source_target_pairs={{0,8},{4,12},{8,0},{12,4},{16,24},{20,28},{24,16},{28,20},{1,9},{5... | collective-permute-start | bytes 221192 | tf_op jit(solution)/shard_map/ppermute | solution.py:306
  36.7 1.5 %shard_map.58 = (bf16[8,256,256]{2,1,0:T(8,128)(2,1)S(1)}, f32[8,256,256]{2,1,0:T(8,128)S(1)}) custom-call(bf16[256,4096]{1,0:T(8,128)(2,1)S(1)} %get-tuple-element.57.q, bf16[256,4096]{1,0:T(8,128)(2,1)S(1)} %get-tuple-element.55.v, bf16[8,256,256]{2,1,0:T(8,128)(2,1)S(1)} %get-tuple-element.58.refs_2_.phi_k, ...), custom_call_target="tpu_custom_call" | custom-call | tf_op jit(solution)/shard_map/pallas_call | solution.py:331
  38.3 1.5 %shard_map.60 = (bf16[8,256,256]{2,1,0:T(8,128)(2,1)S(1)}, f32[8,256,256]{2,1,0:T(8,128)S(1)}) custom-call(bf16[256,4096]{1,0:T(8,128)(2,1)S(1)} %get-tuple-element.57.q, bf16[256,4096]{1,0:T(8,128)(2,1)S(1)} %get-tuple-element.55.v, bf16[8,256,256]{2,1,0:T(8,128)(2,1)S(1)} %get-tuple-element.81.phi_k, bf16[4,256,128]{2,1,0:T(8,128)(2,1)S(1)} %shard_map.49.refs_0_.rest_0_, ...), custom_call_target="tpu_custom_call" | custom-call | tf_op jit(solution)/shard_map/pallas_call | solution.py:331
  39.8 1.7 %shard_map.59 = (bf16[8,256,256]{2,1,0:T(8,128)(2,1)S(1)}, f32[8,256,256]{2,1,0:T(8,128)S(1)}) custom-call(bf16[256,4096]{1,0:T(8,128)(2,1)S(1)} %get-tuple-element.57.q, bf16[256,4096]{1,0:T(8,128)(2,1)S(1)} %get-tuple-element.55.v, bf16[8,256,256]{2,1,0:T(8,128)(2,1)S(1)} %get-tuple-element.79.phi_k, ...), custom_call_target="tpu_custom_call" | custom-call | tf_op jit(solution)/shard_map/pallas_call | solution.py:331
  42.8 2.7 %collective-permute-start.21 = (bf16[128,256]{1,0:T(8,128)(2,1)S(1)}, bf16[128,256]{1,0:T(8,128)(2,1)S(1)}, u32[]{:S(2)}, u32[]{:S(2)}) collective-permute-start(bf16[128,256]{1,0:T(8,128)(2,1)S(1)} %get-tuple-element.85), channel_id=1, source_target_pairs={{0,16},{4,20},{8,24},{12,28},{16,0},{20,4},{24,8},{28,12},{1,17},{... | collective-permute-start | bytes 196616 | tf_op jit(solution)/shard_map/ppermute | solution.py:306
  47.3 1.5 %shard_map.63 = (bf16[8,256,256]{2,1,0:T(8,128)(2,1)S(1)}, f32[8,256,256]{2,1,0:T(8,128)S(1)}) custom-call(bf16[256,4096]{1,0:T(8,128)(2,1)S(1)} %get-tuple-element.57.q, bf16[256,4096]{1,0:T(8,128)(2,1)S(1)} %get-tuple-element.55.v, bf16[8,256,256]{2,1,0:T(8,128)(2,1)S(1)} %get-tuple-element.90.phi_k, ...), custom_call_target="tpu_custom_call" | custom-call | tf_op jit(solution)/shard_map/pallas_call | solution.py:331
  49.3 1.6 %collective-permute-done.22.refs_2_ = bf16[128,256]{1,0:T(8,128)(2,1)S(1)} collective-permute-done((bf16[128,256]{1,0:T(8,128)(2,1)S(1)}, bf16[128,256]{1,0:T(8,128)(2,1)S(1)}, u32[]{:S(2)}, u32[]{:S(2)}) %collective-permute-start.22) | collective-permute-done | bytes 65568 | tf_op jit(solution)/shard_map/ppermute | solution.py:306
  53.6 1.5 %collective-permute-start.23 = (bf16[528,256]{1,0:T(8,128)(2,1)S(1)}, bf16[528,256]{1,0:T(8,128)(2,1)S(1)}, u32[]{:S(2)}, u32[]{:S(2)}) collective-permute-start(bf16[528,256]{1,0:T(8,128)(2,1)S(1)} %get-tuple-element.92), channel_id=1, source_target_pairs={{0,2},{1,3},{2,0},{3,1},{4,6},{5,7},{6,4},{7,5},{8,10},{9,11},{10,... | collective-permute-start | bytes 811016 | tf_op jit(solution)/shard_map/ppermute | solution.py:303
  55.0 1.5 %collective-permute-start.24 = (bf16[528,256]{1,0:T(8,128)(2,1)S(1)}, bf16[528,256]{1,0:T(8,128)(2,1)S(1)}, u32[]{:S(2)}, u32[]{:S(2)}) collective-permute-start(bf16[528,256]{1,0:T(8,128)(2,1)S(1)} %get-tuple-element.93), channel_id=1, source_target_pairs={{0,6},{1,7},{2,4},{3,5},{4,2},{5,3},{6,0},{7,1},{8,14},{9,15},{10,... | collective-permute-start | bytes 811016 | tf_op jit(solution)/shard_map/ppermute | solution.py:318
  56.5 3.2 %collective-permute-done.25.refs_2_ = bf16[528,256]{1,0:T(8,128)(2,1)S(1)} collective-permute-done((bf16[528,256]{1,0:T(8,128)(2,1)S(1)}, bf16[528,256]{1,0:T(8,128)(2,1)S(1)}, u32[]{:S(2)}, u32[]{:S(2)}) %collective-permute-start.25) | collective-permute-done | bytes 270368 | tf_op jit(solution)/shard_map/ppermute | solution.py:306
  62.8 6.4 %collective-permute-done.24.refs_1_ = bf16[528,256]{1,0:T(8,128)(2,1)S(1)} collective-permute-done((bf16[528,256]{1,0:T(8,128)(2,1)S(1)}, bf16[528,256]{1,0:T(8,128)(2,1)S(1)}, u32[]{:S(2)}, u32[]{:S(2)}) %collective-permute-start.24) | collective-permute-done | bytes 270368 | tf_op jit(solution)/shard_map/ppermute | solution.py:318
  (70 shorter events, 22.2 us)
Async XLA Ops:
  1.4 9.5 %collective-permute-start.1 = (bf16[4,256,128]{2,1,0:T(8,128)(2,1)S(1)}, bf16[4,256,128]{2,1,0:T(8,128)(2,1)S(1)}, u32[]{:S(2)}, u32[]{:S(2)}) collective-permute-start(bf16[4,256,128]{2,1,0:T(8,128)(2,1)S(1)} %constant_dynamic-slice_fusion), channel_id=1, source_target_pairs={{0,2},{1,3},{2,0},{3,1},{4,6},{5,7},{6,4},{7,5},{8,10},{9,11},{10,... | collective-permute-start | bytes 786440 | tf_op jit(solution)/shard_map/ppermute | solution.py:303
  11.1 8.7 %collective-permute-start.4 = (bf16[4,256,128]{2,1,0:T(8,128)(2,1)S(1)}, bf16[4,256,128]{2,1,0:T(8,128)(2,1)S(1)}, u32[]{:S(2)}, u32[]{:S(2)}) collective-permute-start(bf16[4,256,128]{2,1,0:T(8,128)(2,1)S(1)} %shard_map.49.refs_0_.rest_0_), channel_id=1, source_target_pairs={{0,4},{4,0},{8,12},{12,8},{16,20},{20,16},{24,28},{28,24},{1,5},{5... | collective-permute-start | bytes 786440 | tf_op jit(solution)/shard_map/ppermute | solution.py:306
  12.9 9.4 %collective-permute-start.14 = (bf16[528,256]{1,0:T(8,128)(2,1)S(1)}, bf16[528,256]{1,0:T(8,128)(2,1)S(1)}, u32[]{:S(2)}, u32[]{:S(2)}) collective-permute-start(bf16[528,256]{1,0:T(8,128)(2,1)S(1)} %shard_map.48.refs_1_.refs_2_), channel_id=1, source_target_pairs={{0,2},{1,3},{2,0},{3,1},{4,6},{5,7},{6,4},{7,5},{8,10},{9,11},{10,... | collective-permute-start | bytes 811016 | tf_op jit(solution)/shard_map/ppermute | solution.py:303
  14.4 5.4 %collective-permute-start.8 = (bf16[256,256]{1,0:T(8,128)(2,1)S(1)}, bf16[256,256]{1,0:T(8,128)(2,1)S(1)}, u32[]{:S(2)}, u32[]{:S(2)}) collective-permute-start(bf16[256,256]{1,0:T(8,128)(2,1)S(1)} %get-tuple-element.66), channel_id=1, source_target_pairs={{0,1},{1,0},{2,3},{3,2},{4,5},{5,4},{6,7},{7,6},{8,9},{9,8},{10,11... | collective-permute-start | bytes 393224 | tf_op jit(solution)/shard_map/ppermute | solution.py:303
  14.4 5.9 %collective-permute-start.9 = (bf16[272,256]{1,0:T(8,128)(2,1)S(1)}, bf16[272,256]{1,0:T(8,128)(2,1)S(1)}, u32[]{:S(2)}, u32[]{:S(2)}) collective-permute-start(bf16[272,256]{1,0:T(8,128)(2,1)S(1)} %get-tuple-element.67), channel_id=1, source_target_pairs={{0,1},{1,0},{2,3},{3,2},{4,5},{5,4},{6,7},{7,6},{8,9},{9,8},{10,11... | collective-permute-start | bytes 417800 | tf_op jit(solution)/shard_map/ppermute | solution.py:303
  16.4 5.8 %collective-permute-start.13 = (bf16[272,256]{1,0:T(8,128)(2,1)S(1)}, bf16[272,256]{1,0:T(8,128)(2,1)S(1)}, u32[]{:S(2)}, u32[]{:S(2)}) collective-permute-start(bf16[272,256]{1,0:T(8,128)(2,1)S(1)} %get-tuple-element.71), channel_id=1, source_target_pairs={{0,1},{1,0},{2,3},{3,2},{4,5},{5,4},{6,7},{7,6},{8,9},{9,8},{10,11... | collective-permute-start | bytes 417800 | tf_op jit(solution)/shard_map/ppermute | solution.py:303
  20.4 8.5 %collective-permute-start.10 = (bf16[528,256]{1,0:T(8,128)(2,1)S(1)}, bf16[528,256]{1,0:T(8,128)(2,1)S(1)}, u32[]{:S(2)}, u32[]{:S(2)}) collective-permute-start(bf16[528,256]{1,0:T(8,128)(2,1)S(1)} %shard_map.52), channel_id=1, source_target_pairs={{0,2},{1,3},{2,0},{3,1},{4,6},{5,7},{6,4},{7,5},{8,10},{9,11},{10,... | collective-permute-start | bytes 811016 | tf_op jit(solution)/shard_map/ppermute | solution.py:303
  22.4 8.2 %collective-permute-start.15 = (bf16[528,256]{1,0:T(8,128)(2,1)S(1)}, bf16[528,256]{1,0:T(8,128)(2,1)S(1)}, u32[]{:S(2)}, u32[]{:S(2)}) collective-permute-start(bf16[528,256]{1,0:T(8,128)(2,1)S(1)} %get-tuple-element.72), channel_id=1, source_target_pairs={{0,4},{4,0},{8,12},{12,8},{16,20},{20,16},{24,28},{28,24},{1,5},{5... | collective-permute-start | bytes 811016 | tf_op jit(solution)/shard_map/ppermute | solution.py:306
  30.8 11.9 %collective-permute-start.19 = (bf16[528,256]{1,0:T(8,128)(2,1)S(1)}, bf16[528,256]{1,0:T(8,128)(2,1)S(1)}, u32[]{:S(2)}, u32[]{:S(2)}) collective-permute-start(bf16[528,256]{1,0:T(8,128)(2,1)S(1)} %shard_map.61), channel_id=1, source_target_pairs={{0,4},{4,0},{8,12},{12,8},{16,20},{20,16},{24,28},{28,24},{1,5},{5... | collective-permute-start | bytes 811016 | tf_op jit(solution)/shard_map/ppermute | solution.py:306
  32.3 24.2 %collective-permute-start.27 = (bf16[528,256]{1,0:T(8,128)(2,1)S(1)}, bf16[528,256]{1,0:T(8,128)(2,1)S(1)}, u32[]{:S(2)}, u32[]{:S(2)}) collective-permute-start(bf16[528,256]{1,0:T(8,128)(2,1)S(1)} %get-tuple-element.62.mine), channel_id=1, source_target_pairs={{0,1},{1,0},{2,3},{3,2},{4,5},{5,4},{6,7},{7,6},{8,9},{9,8},{10,11... | collective-permute-start | bytes 811016 | tf_op jit(solution)/shard_map/ppermute | solution.py:303
  32.3 9.1 %collective-permute-start.17 = (bf16[144,256]{1,0:T(8,128)(2,1)S(1)}, bf16[144,256]{1,0:T(8,128)(2,1)S(1)}, u32[]{:S(2)}, u32[]{:S(2)}) collective-permute-start(bf16[144,256]{1,0:T(8,128)(2,1)S(1)} %get-tuple-element.76), channel_id=1, source_target_pairs={{0,16},{4,20},{8,24},{12,28},{16,0},{20,4},{24,8},{28,12},{1,17},{... | collective-permute-start | bytes 221192 | tf_op jit(solution)/shard_map/ppermute | solution.py:306
  34.9 6.6 %collective-permute-start.18 = (bf16[144,256]{1,0:T(8,128)(2,1)S(1)}, bf16[144,256]{1,0:T(8,128)(2,1)S(1)}, u32[]{:S(2)}, u32[]{:S(2)}) collective-permute-start(bf16[144,256]{1,0:T(8,128)(2,1)S(1)} %get-tuple-element.77), channel_id=1, source_target_pairs={{0,8},{4,12},{8,0},{12,4},{16,24},{20,28},{24,16},{28,20},{1,9},{5... | collective-permute-start | bytes 221192 | tf_op jit(solution)/shard_map/ppermute | solution.py:306
  36.5 6.2 %collective-permute-start.16 = (bf16[144,256]{1,0:T(8,128)(2,1)S(1)}, bf16[144,256]{1,0:T(8,128)(2,1)S(1)}, u32[]{:S(2)}, u32[]{:S(2)}) collective-permute-start(bf16[144,256]{1,0:T(8,128)(2,1)S(1)} %get-tuple-element.73.rest_2_), channel_id=1, source_target_pairs={{0,24},{4,28},{8,16},{12,20},{16,8},{20,12},{24,0},{28,4},{1,25},{... | collective-permute-start | bytes 221192 | tf_op jit(solution)/shard_map/ppermute | solution.py:306
  42.8 6.5 %collective-permute-start.21 = (bf16[128,256]{1,0:T(8,128)(2,1)S(1)}, bf16[128,256]{1,0:T(8,128)(2,1)S(1)}, u32[]{:S(2)}, u32[]{:S(2)}) collective-permute-start(bf16[128,256]{1,0:T(8,128)(2,1)S(1)} %get-tuple-element.85), channel_id=1, source_target_pairs={{0,16},{4,20},{8,24},{12,28},{16,0},{20,4},{24,8},{28,12},{1,17},{... | collective-permute-start | bytes 196616 | tf_op jit(solution)/shard_map/ppermute | solution.py:306
  45.5 5.4 %collective-permute-start.22 = (bf16[128,256]{1,0:T(8,128)(2,1)S(1)}, bf16[128,256]{1,0:T(8,128)(2,1)S(1)}, u32[]{:S(2)}, u32[]{:S(2)}) collective-permute-start(bf16[128,256]{1,0:T(8,128)(2,1)S(1)} %get-tuple-element.86), channel_id=1, source_target_pairs={{0,8},{4,12},{8,0},{12,4},{16,24},{20,28},{24,16},{28,20},{1,9},{5... | collective-permute-start | bytes 196616 | tf_op jit(solution)/shard_map/ppermute | solution.py:306
  45.9 6.1 %collective-permute-start.20 = (bf16[128,256]{1,0:T(8,128)(2,1)S(1)}, bf16[128,256]{1,0:T(8,128)(2,1)S(1)}, u32[]{:S(2)}, u32[]{:S(2)}) collective-permute-start(bf16[128,256]{1,0:T(8,128)(2,1)S(1)} %get-tuple-element.84.rest_2_), channel_id=1, source_target_pairs={{0,24},{4,28},{8,16},{12,20},{16,8},{20,12},{24,0},{28,4},{1,25},{... | collective-permute-start | bytes 196616 | tf_op jit(solution)/shard_map/ppermute | solution.py:306
  53.0 6.8 %collective-permute-start.25 = (bf16[528,256]{1,0:T(8,128)(2,1)S(1)}, bf16[528,256]{1,0:T(8,128)(2,1)S(1)}, u32[]{:S(2)}, u32[]{:S(2)}) collective-permute-start(bf16[528,256]{1,0:T(8,128)(2,1)S(1)} %get-tuple-element.95), channel_id=1, source_target_pairs={{0,4},{4,0},{8,12},{12,8},{16,20},{20,16},{24,28},{28,24},{1,5},{5... | collective-permute-start | bytes 811016 | tf_op jit(solution)/shard_map/ppermute | solution.py:306
  53.5 6.2 %collective-permute-start.26 = (bf16[528,256]{1,0:T(8,128)(2,1)S(1)}, bf16[528,256]{1,0:T(8,128)(2,1)S(1)}, u32[]{:S(2)}, u32[]{:S(2)}) collective-permute-start(bf16[528,256]{1,0:T(8,128)(2,1)S(1)} %get-tuple-element.97.refs_2_), channel_id=1, source_target_pairs={{0,1},{1,0},{2,3},{3,2},{4,5},{5,4},{6,7},{7,6},{8,9},{9,8},{10,11... | collective-permute-start | bytes 811016 | tf_op jit(solution)/shard_map/ppermute | solution.py:303
  53.6 9.3 %collective-permute-start.23 = (bf16[528,256]{1,0:T(8,128)(2,1)S(1)}, bf16[528,256]{1,0:T(8,128)(2,1)S(1)}, u32[]{:S(2)}, u32[]{:S(2)}) collective-permute-start(bf16[528,256]{1,0:T(8,128)(2,1)S(1)} %get-tuple-element.92), channel_id=1, source_target_pairs={{0,2},{1,3},{2,0},{3,1},{4,6},{5,7},{6,4},{7,5},{8,10},{9,11},{10,... | collective-permute-start | bytes 811016 | tf_op jit(solution)/shard_map/ppermute | solution.py:303
  55.0 14.2 %collective-permute-start.24 = (bf16[528,256]{1,0:T(8,128)(2,1)S(1)}, bf16[528,256]{1,0:T(8,128)(2,1)S(1)}, u32[]{:S(2)}, u32[]{:S(2)}) collective-permute-start(bf16[528,256]{1,0:T(8,128)(2,1)S(1)} %get-tuple-element.93), channel_id=1, source_target_pairs={{0,6},{1,7},{2,4},{3,5},{4,2},{5,3},{6,0},{7,1},{8,14},{9,15},{10,... | collective-permute-start | bytes 811016 | tf_op jit(solution)/shard_map/ppermute | solution.py:318
  56.5 12.8 %collective-permute-start.33 = (bf16[528,256]{1,0:T(8,128)(2,1)S(1)}, bf16[528,256]{1,0:T(8,128)(2,1)S(1)}, u32[]{:S(2)}, u32[]{:S(2)}) collective-permute-start(bf16[528,256]{1,0:T(8,128)(2,1)S(1)} %get-tuple-element.69.mine), channel_id=1, source_target_pairs={{0,1},{1,0},{2,3},{3,2},{4,5},{5,4},{6,7},{7,6},{8,9},{9,8},{10,11... | collective-permute-start | bytes 811016 | tf_op jit(solution)/shard_map/ppermute | solution.py:303
  59.8 12.4 %collective-permute-start.31 = (bf16[528,256]{1,0:T(8,128)(2,1)S(1)}, bf16[528,256]{1,0:T(8,128)(2,1)S(1)}, u32[]{:S(2)}, u32[]{:S(2)}) collective-permute-start(bf16[528,256]{1,0:T(8,128)(2,1)S(1)} %get-tuple-element.59.mine), channel_id=1, source_target_pairs={{0,1},{1,0},{2,3},{3,2},{4,5},{5,4},{6,7},{7,6},{8,9},{9,8},{10,11... | collective-permute-start | bytes 811016 | tf_op jit(solution)/shard_map/ppermute | solution.py:303
  59.8 10.1 %collective-permute-start.32 = (bf16[528,256]{1,0:T(8,128)(2,1)S(1)}, bf16[528,256]{1,0:T(8,128)(2,1)S(1)}, u32[]{:S(2)}, u32[]{:S(2)}) collective-permute-start(bf16[528,256]{1,0:T(8,128)(2,1)S(1)} %collective-permute-done.25.refs_2_), channel_id=1, source_target_pairs={{0,1},{1,0},{2,3},{3,2},{4,5},{5,4},{6,7},{7,6},{8,9},{9,8},{10,11... | collective-permute-start | bytes 811016 | tf_op jit(solution)/shard_map/ppermute | solution.py:303
  62.8 9.3 %collective-permute-start.29 = (bf16[528,256]{1,0:T(8,128)(2,1)S(1)}, bf16[528,256]{1,0:T(8,128)(2,1)S(1)}, u32[]{:S(2)}, u32[]{:S(2)}) collective-permute-start(bf16[528,256]{1,0:T(8,128)(2,1)S(1)} %get-tuple-element.65.mine), channel_id=1, source_target_pairs={{0,1},{1,0},{2,3},{3,2},{4,5},{5,4},{6,7},{7,6},{8,9},{9,8},{10,11... | collective-permute-start | bytes 811016 | tf_op jit(solution)/shard_map/ppermute | solution.py:303
  (10 other events, 27.6 us)

commit v5 on v4

--- a/solution.py
+++ b/solution.py
@@ -73,16 +73,15 @@
         totals.append(jnp.sum(ph.astype(F32), axis=0, keepdims=True))
     waits(2)
     for i, cols, _, _ in heads:
-        h, half = i % group, group // 2
-        late = i < group and h >= half
-        out = mine if i >= group else others[-1] if late else others[0]
-        h = h - half if late else h
+        h, out, each = i % group, mine, group // len(others)
+        if i < group:
+            h, out = h % each, others[h // each]
         st = lax.dot_general(
             v[:, cols], phi[i], (((0,), (0,)), ((), ())), preferred_element_type=F32
         )
         out[h * size : (h + 1) * size] = st.astype(BF16)
     pad = jnp.zeros((TOTAL_ROWS - group, totals[0].shape[1]), F32)
-    others[-1][(group - group // 2) * size :] = jnp.concatenate([*totals[:group], pad], axis=0).astype(BF16)
+    others[-1][group // len(others) * size :] = jnp.concatenate([*totals[:group], pad], axis=0).astype(BF16)
     mine[group * size :] = jnp.concatenate([*totals[group:], pad], axis=0).astype(BF16)
     waits(3)
 
@@ -162,26 +161,26 @@
         )
 
 
-def output_kernel(jobs, shape, extra, *refs):
-    out, *marks, ready, sems = refs[5 * len(jobs) + extra :]
+def output_kernel(jobs, counts, shape, extra, *refs):
+    jobs_refs, at = [], 0
+    for count in counts:
+        jobs_refs.append(refs[at : at + count])
+        at += count
+    out, *marks, ready, sems = refs[at + extra :]
     nx, ny, group, size = shape
     pos = position(nx, ny)
     add = (pos[1] == 1).astype(F32)
     copies = []
     for n, (key, core) in enumerate(jobs):
-        phi_q, inner, base, extra_a, extra_b = refs[5 * n : 5 * n + 5]
+        phi_q, inner, base, *extras = jobs_refs[n]
         count = phi_q.shape[-1]
         place = place_of(pos, key, nx, ny, core)[0]
-        half = extra_a.shape[0]
-        whole = half == base.shape[0]
-        last = extra_a[group * size :] if whole else extra_b[group * size - half :]
+        each = group // len(extras)
+        last = extras[-1][each * size :]
         totals = base[group * size :].astype(F32) + add * last.astype(F32)
         for h in range(group):
             rows = slice(h * size, (h + 1) * size)
-            if whole or h * size < half:
-                extra = extra_a[rows]
-            else:
-                extra = extra_b[h * size - half : (h + 1) * size - half]
+            extra = extras[h // each][h % each * size : (h % each + 1) * size]
             st = (base[rows].astype(F32) + add * extra.astype(F32)).astype(BF16)
             tot = jnp.broadcast_to(totals[h : h + 1], (size, count)).astype(BF16)
             at = (1 - core) * group + h
@@ -220,18 +219,12 @@
         out[rows] = (mine[rows].astype(F32) + other[...].astype(F32)).astype(BF16)
 
 
-def row_kernel(nx, ny, *refs):
-    pieces, out, before = refs[:nx], refs[nx], refs[nx + 1 :]
-    x = position(nx, ny)[0]
+def row_kernel(*refs):
+    *pieces, out = refs
     total = pieces[0][...].astype(F32)
     for piece in pieces[1:]:
         total = total + piece[...].astype(F32)
     out[...] = total.astype(BF16)
-    for n, out in enumerate(before):
-        total = jnp.zeros(out.shape, F32)
-        for ex, piece in enumerate(pieces):
-            total = total + jnp.where((x ^ ex) < n + 1, piece[...].astype(F32), 0.0)
-        out[...] = total.astype(BF16)
 
 
 def plane_kernel(count, zrows, ny, *refs):
@@ -262,24 +255,30 @@
     totals[...] = total
 
 
-def place_kernel(nx, ny, count, zrows, *refs):
-    keys = [(dx, dy) for dx in range(nx) for dy in range(ny)]
+def rows_kernel(ny, count, zrows, *refs):
     prefix, totals = refs[count - 1 :: -1], refs[count]
-    row_sums = refs[count + 1 : count + 1 + ny]
-    before, outs = refs[count + 1 + ny :], refs[-1 - len(keys) : -1]
-    held = refs[-1]
-    x, _, y, z = position(nx, ny)
+    row_sums, outs, held = refs[count + 1 : count + 1 + ny], refs[-1 - ny : -1], refs[-1]
+    _, _, y, z = position(1, ny)
     for j in range(count):
         start = pl.multiple_of((z ^ j) * zrows, zrows)
         held[pl.ds(start, zrows)] = prefix[j][...].astype(F32)
     held[count * zrows :] = totals[...]
-    for (dx, dy), out in zip(keys, outs):
+    for dy, out in enumerate(outs):
         total = held[...]
         for ey, row_sum in enumerate(row_sums):
-            total = total + jnp.where((y ^ ey) < (y ^ dy), row_sum[...].astype(F32), 0.0)
-        for n in range(nx - 1):
-            part = before[dy * (nx - 1) + n][...].astype(F32)
-            total = total + jnp.where((x ^ dx) == n + 1, part, 0.0)
+            if ey != dy:
+                total = total + jnp.where((y ^ ey) < (y ^ dy), row_sum[...].astype(F32), 0.0)
+        out[...] = total.astype(out.dtype)
+
+
+def columns_kernel(nx, ny, base, *refs):
+    pieces, outs = refs[:nx], refs[nx:]
+    x = position(nx, ny)[0]
+    for dx, out in enumerate(outs):
+        total = base[...].astype(F32)
+        for ex, piece in enumerate(pieces):
+            if ex != dx:
+                total = total + jnp.where((x ^ ex) < (x ^ dx), piece[...].astype(F32), 0.0)
         out[...] = total.astype(BF16)
 
 
@@ -351,9 +350,11 @@
     near_k, near_q = [], []
 
     def states(key, after=()):
-        half = jax.ShapeDtypeStruct((group // 2 * size, count), BF16)
-        rest = jax.ShapeDtypeStruct((rows - half.shape[0], count), BF16)
-        outs = [per_head(tokens, count), *([half, rest] if group > 1 else [rest]), whole]
+        cuts = group if key == later[0] else min(group, 2)
+        cut = [group // cuts * size] * cuts
+        cut[-1] += TOTAL_ROWS
+        cut = [jax.ShapeDtypeStruct((n, count), BF16) for n in cut]
+        outs = [per_head(tokens, count), *cut, whole]
         like = [jax.ShapeDtypeStruct(a.shape, BF16) for a in (k, v, features)]
         if not near_k:
             sems = pltpu.SemaphoreType.DMA((2 * (width // (group * size)) + 1,))
@@ -384,7 +385,7 @@
             )
         *other, mine = sums
         other = [head_swap(a, 1) for a in other]
-        theirs[key] = [[other[0], other[-1]], [head_swap(mine, 1)] * 2]
+        theirs[key] = [other, [head_swap(mine, 1)]]
         piece[key] = call(chip_kernel, whole, [mine, *other])
         got[key] = head_swap(piece[key], key[0] * cores) if key[0] else piece[key]
         return mine
@@ -417,22 +418,21 @@
             (part,) = tie([head_swap(part, ox * cores)], ready)
             rest = seq_swap(part, 1)
             dirs[ox ^ flip, 1] = (part, head_swap(part, 1))
-            dirs[ox ^ flip, 0] = (rest, head_swap(rest, 1))
+            dirs[ox ^ flip, 0] = (rest,)
         else:
             (full,) = tie([head_swap(features, ox * cores)], ready)
             full = (full, head_swap(full, 1))
             for dy in range(ny):
                 dirs[ox ^ flip, dy] = full
     for key in later:
-        states(key, [piece[first[0]]])
-
-    rows_of, before = {}, {}
+        if key != later[0] and ny == 2:
+            (rest,) = tie([dirs[key][0]], [piece[later[0]]])
+            dirs[key] = (rest, head_swap(rest, 1))
+        states(key, [piece[key] for key in first])
+
+    rows_of = {}
     for dy in reversed(range(ny)):
-        sums, *before[dy] = call(
-            functools.partial(row_kernel, nx, ny),
-            [whole] * nx,
-            [got[dx, dy] for dx in range(nx)],
-        )
+        sums = call(row_kernel, whole, [got[dx, dy] for dx in range(nx)])
         rows_of[dy] = seq_swap(sums, dy) if dy else sums
     summed = call(
         functools.partial(plane_kernel, ny, zrows, ny),
@@ -447,54 +447,52 @@
 
     heard = exchange(summed)
     done = [inner(key, [summed[-1]]) for key in [*first, *later[:-1]]]
-    for dy in range(1, ny):
-        before[dy] = [seq_swap(a, dy) for a in tie(before[dy], [summed[0]])] if nx > 1 else []
     *prefix, totals = call(
         functools.partial(prefix_kernel, nz, zrows, ny),
         [jax.ShapeDtypeStruct((zrows, count), BF16)] * nz
         + [jax.ShapeDtypeStruct((TOTAL_ROWS, count), F32)],
         heard[::-1],
-        done + [a for dy in range(1, ny) for a in before[dy]],
+        done,
     )
     done = [inner(later[-1], [prefix[-1]])] if later else []
     prefix = exchange(prefix)
-    placed = call(
-        functools.partial(place_kernel, nx, ny, nz, zrows),
-        [whole] * len(plane),
-        [
-            *prefix[::-1],
-            totals,
-            *[rows_of[dy] for dy in range(ny)],
-            *[a for dy in range(ny) for a in before[dy]],
-        ],
+    bases = call(
+        functools.partial(rows_kernel, ny, nz, zrows),
+        [jax.ShapeDtypeStruct((rows, count), BF16 if dy else F32) for dy in range(ny)],
+        [*prefix[::-1], totals, *[rows_of[dy] for dy in range(ny)]],
         done,
         scratch=[pltpu.VMEM((rows, count), F32)],
     )
-
-    placed = dict(zip(plane, placed))
-    result = {
-        key: plane_swap(placed[key], *key) if any(key) else placed[key]
-        for key in reversed(plane)
-    }
-    batches = [[((0, 0), 0), ((0, 0), 1)]]
-    batches += [[((0, dy), 0)] for dy in range(1, ny)]
+    result = {}
+    for dy, base in enumerate(bases):
+        placed = call(
+            functools.partial(columns_kernel, nx, ny),
+            [whole] * nx,
+            [seq_swap(base, dy) if dy else base, *[got[dx, dy] for dx in range(nx)]],
+        )
+        for dx, a in enumerate(placed):
+            result[dx, dy] = head_swap(a, dx * cores) if dx else a
+
+    late = [key for key in plane if all(key)]
+    soon = [key for key in plane if not key[0]]
+    batches = [[(key, 0), (key, 1)] for key in soon]
     tied = len(batches)
-    batches += [[((0, dy), 1)] for dy in range(1, ny)]
-    for core in range(cores):
-        for dx in range(1, nx):
-            batches.append([((dx, dy), core) for dy in range(ny)])
+    batches += [[(key, 0) for key in late]] if late else []
+    batches += [[(key, 0), (key, 1)] for key in plane if key not in late + soon]
+    batches += [[(key, 1) for key in late]] if late else []
     out = None
     for i, jobs in enumerate(batches):
         args = []
         if i == tied:
-            keys = [key for key in plane if key[0]]
-            result.update(zip(keys, tie([result[key] for key in keys], mark)))
+            result.update(zip(late, tie([result[key] for key in late], mark)))
+        counts = []
         for key, core in jobs:
             base = head_swap(result[key], 1) if core else result[key]
             args += [*phi_w[key], base, *theirs[key][core]]
+            counts.append(3 + len(theirs[key][core]))
         marked = [pltpu.VMEM((8, 128), F32)] if i == tied - 1 else []
         out, *mark = call(
-            functools.partial(output_kernel, jobs, shape, int(i > 0)),
+            functools.partial(output_kernel, jobs, counts, shape, int(i > 0)),
             [jax.ShapeDtypeStruct((tokens, width), BF16), *marked],
             args,
             [] if out is None else [out],

time: 73.8 us -> 71.9 us (0.974)
  starting transfers between devices: 27.1 us -> 25.3 us
    ppermute x23 -> x26, waiting for transfers between devices: 4.96 us -> 13.7 us  [head_swap(): return lax.ppermute(a, 'head', [(i, i ^ bits) for i in range(heads)])]
    ppermute x1 -> x0, waiting for transfers between devices: 6.36 us -> none  [plane_swap(): return lax.ppermute(a, ('seq', 'head'), pairs)]
    ppermute x10 -> x9, waiting for transfers between devices: 12.6 us -> 10.7 us  [seq_swap(): return lax.ppermute(a, 'seq', [(i, i ^ bits) for i in range(seqs)])]
    ppermute x1 -> x0, starting transfers between devices: 1.5 us -> none  [plane_swap(): return lax.ppermute(a, ('seq', 'head'), pairs)]
    pallas_call x25 -> x27, Pallas kernels: 21.3 us -> 20.6 us  [call(): pl.pallas_call(kernel, out_shape=out, in_specs=[far] * len(there) + [near...]
    ppermute x10 -> x9, starting transfers between devices: 14.4 us -> 13.8 us  [seq_swap(): return lax.ppermute(a, 'seq', [(i, i ^ bits) for i in range(seqs)])]
    ppermute x23 -> x26, starting transfers between devices: 11.2 us -> 11.5 us  [head_swap(): return lax.ppermute(a, 'head', [(i, i ^ bits) for i in range(heads)])]
  transfers between devices with their start and end apart: 34 -> 35, of which waited for: 12 -> 15; matrix products, arithmetic and copies ran while one was open for 1% -> 1% of each run, Pallas kernels for 27% -> 27%
where the time goes in v5:
time: 71.9 us; the launch traced here: 71.7 us
  starting transfers between devices  25.3 us (35%)
  waiting for transfers between devices  24.4 us (34%)
  Pallas kernels  20.6 us (29%)
  local copies, waits for them, and re-layouts  0.97 us (1%)
    pallas_call x27, Pallas kernels, call(): pl.pallas_call(kernel, out_shape=out, in_specs=[far] * len(there) + [near...  20.6 us
    ppermute x9, starting transfers between devices, seq_swap(): return lax.ppermute(a, 'seq', [(i, i ^ bits) for i in range(seqs)])  13.8 us
    ppermute x26, waiting for transfers between devices, head_swap(): return lax.ppermute(a, 'head', [(i, i ^ bits) for i in range(heads)])  13.7 us
    ppermute x26, starting transfers between devices, head_swap(): return lax.ppermute(a, 'head', [(i, i ^ bits) for i in range(heads)])  11.5 us
    ppermute x9, waiting for transfers between devices, seq_swap(): return lax.ppermute(a, 'seq', [(i, i ^ bits) for i in range(seqs)])  10.7 us
  transfers between devices with their start and end apart: 35, of which 15 were waited for; matrix products, arithmetic and copies ran while one was open for 1% of the time, Pallas kernels for 27%

profile of v5, /device:TPU:0, one launch (start us, length us, event | category | flops | bytes accessed | tf_op | source)
XLA Modules:
  0.0 71.7 jit_solution(16179938663653257861)
XLA Ops:
  1.4 2.6 %collective-permute-start.1 = (bf16[4,256,128]{2,1,0:T(8,128)(2,1)S(1)}, bf16[4,256,128]{2,1,0:T(8,128)(2,1)S(1)}, u32[]{:S(2)}, u32[]{:S(2)}) collective-permute-start(bf16[4,256,128]{2,1,0:T(8,128)(2,1)S(1)} %constant_dynamic-slice_fusion), channel_id=1, source_target_pairs={{0,2},{1,3},{2,0},{3,1},{4,6},{5,7},{6,4},{7,5},{8,10},{9,11},{10,... | collective-permute-start | bytes 786440 | tf_op jit(solution)/shard_map/ppermute | solution.py:302
  4.0 2.7 %shard_map.46 = (bf16[8,256,256]{2,1,0:T(8,128)(2,1)S(1)}, bf16[256,256]{1,0:T(8,128)(2,1)S(1)}, bf16[272,256]{1,0:T(8,128)(2,1)S(1)}, bf16[528,256]{1,0:T(8,128...) custom-call(bf16[256,4096]{1,0:T(8,128)(2,1)} %bitcast.5, ...), custom_call_target="tpu_custom_call" | custom-call | tf_op jit(solution)/shard_map/pallas_call | solution.py:330
  7.3 1.6 %shard_map.47 = (bf16[8,256,256]{2,1,0:T(8,128)(2,1)S(1)}, bf16[256,256]{1,0:T(8,128)(2,1)S(1)}, bf16[272,256]{1,0:T(8,128)(2,1)S(1)}, bf16[528,256]{1,0:T(8,128)(2,1)S(1)}, bf16[256,4096]{1,0:T(8,128)(2,1)S(1)}) custom-call(bf16[256,4096]{1,0:T(8,128)(2,1)} %bitcast.4, bf16[256,4096]{1,0:T(8,128)(2,1)S(1)} %get-tuple-element.52.k, ...), custom_call_target="tpu_custom_call" | custom-call | tf_op jit(solution)/shard_map/pallas_call | solution.py:330
  9.0 2.0 %collective-permute-done.1.refs_0_ = bf16[4,256,128]{2,1,0:T(8,128)(2,1)S(1)} collective-permute-done((bf16[4,256,128]{2,1,0:T(8,128)(2,1)S(1)}, bf16[4,256,128]{2,1,0:T(8,128)(2,1)S(1)}, u32[]{:S(2)}, u32[]{:S(2)}) %collective-permute-start.1) | collective-permute-done | bytes 262176 | tf_op jit(solution)/shard_map/ppermute | solution.py:302
  11.6 1.8 %collective-permute-start.4 = (bf16[4,256,128]{2,1,0:T(8,128)(2,1)S(1)}, bf16[4,256,128]{2,1,0:T(8,128)(2,1)S(1)}, u32[]{:S(2)}, u32[]{:S(2)}) collective-permute-start(bf16[4,256,128]{2,1,0:T(8,128)(2,1)S(1)} %shard_map.49.refs_0_.rest_0_), channel_id=1, source_target_pairs={{0,4},{4,0},{8,12},{12,8},{16,20},{20,16},{24,28},{28,24},{1,5},{5... | collective-permute-start | bytes 786440 | tf_op jit(solution)/shard_map/ppermute | solution.py:305
  13.4 1.5 %collective-permute-start.16 = (bf16[528,256]{1,0:T(8,128)(2,1)S(1)}, bf16[528,256]{1,0:T(8,128)(2,1)S(1)}, u32[]{:S(2)}, u32[]{:S(2)}) collective-permute-start(bf16[528,256]{1,0:T(8,128)(2,1)S(1)} %shard_map.48.refs_1_.refs_2_), channel_id=1, source_target_pairs={{0,2},{1,3},{2,0},{3,1},{4,6},{5,7},{6,4},{7,5},{8,10},{9,11},{10,... | collective-permute-start | bytes 811016 | tf_op jit(solution)/shard_map/ppermute | solution.py:302
  15.0 1.5 %shard_map.51 = (bf16[8,256,256]{2,1,0:T(8,128)(2,1)S(1)}, bf16[128,256]{1,0:T(8,128)(2,1)S(1)}, bf16[128,256]{1,0:T(8,128)(2,1)S(1)}, bf16[128,256]{1,0:T(8,128...) custom-call(bf16[256,4096]{1,0:T(8,128)(2,1)S(1)} %get-tuple-element.52.k, ...), custom_call_target="tpu_custom_call" | custom-call | tf_op jit(solution)/shard_map/pallas_call | solution.py:330
  20.4 1.8 %collective-permute-start.15 = (bf16[528,256]{1,0:T(8,128)(2,1)S(1)}, bf16[528,256]{1,0:T(8,128)(2,1)S(1)}, u32[]{:S(2)}, u32[]{:S(2)}) collective-permute-start(bf16[528,256]{1,0:T(8,128)(2,1)S(1)} %shard_map.50.refs_3_), channel_id=1, source_target_pairs={{0,2},{1,3},{2,0},{3,1},{4,6},{5,7},{6,4},{7,5},{8,10},{9,11},{10,... | collective-permute-start | bytes 811016 | tf_op jit(solution)/shard_map/ppermute | solution.py:302
  22.3 1.6 %collective-permute-start.17 = (bf16[528,256]{1,0:T(8,128)(2,1)S(1)}, bf16[528,256]{1,0:T(8,128)(2,1)S(1)}, u32[]{:S(2)}, u32[]{:S(2)}) collective-permute-start(bf16[528,256]{1,0:T(8,128)(2,1)S(1)} %shard_map.57), channel_id=1, source_target_pairs={{0,4},{4,0},{8,12},{12,8},{16,20},{20,16},{24,28},{28,24},{1,5},{5... | collective-permute-start | bytes 811016 | tf_op jit(solution)/shard_map/ppermute | solution.py:305
  27.0 2.3 %collective-permute-done.15.refs_1_ = bf16[528,256]{1,0:T(8,128)(2,1)S(1)} collective-permute-done((bf16[528,256]{1,0:T(8,128)(2,1)S(1)}, bf16[528,256]{1,0:T(8,128)(2,1)S(1)}, u32[]{:S(2)}, u32[]{:S(2)}) %collective-permute-start.15) | collective-permute-done | bytes 270368 | tf_op jit(solution)/shard_map/ppermute | solution.py:302
  29.4 1.5 %collective-permute-done.17.refs_1_.refs_6_ = bf16[528,256]{1,0:T(8,128)(2,1)S(1)} collective-permute-done((bf16[528,256]{1,0:T(8,128)(2,1)S(1)}, bf16[528,256]{1,0:T(8,128)(2,1)S(1)}, u32[]{:S(2)}, u32[]{:S(2)}) %collective-permute-start.17) | collective-permute-done | bytes 270368 | tf_op jit(solution)/shard_map/ppermute | solution.py:305
  31.0 2.7 %collective-permute-start.19 = (bf16[144,256]{1,0:T(8,128)(2,1)S(1)}, bf16[144,256]{1,0:T(8,128)(2,1)S(1)}, u32[]{:S(2)}, u32[]{:S(2)}) collective-permute-start(bf16[144,256]{1,0:T(8,128)(2,1)S(1)} %get-tuple-element.75), channel_id=1, source_target_pairs={{0,16},{4,20},{8,24},{12,28},{16,0},{20,4},{24,8},{28,12},{1,17},{... | collective-permute-start | bytes 221192 | tf_op jit(solution)/shard_map/ppermute | solution.py:305
  33.7 1.6 %collective-permute-start.20 = (bf16[144,256]{1,0:T(8,128)(2,1)S(1)}, bf16[144,256]{1,0:T(8,128)(2,1)S(1)}, u32[]{:S(2)}, u32[]{:S(2)}) collective-permute-start(bf16[144,256]{1,0:T(8,128)(2,1)S(1)} %get-tuple-element.76), channel_id=1, source_target_pairs={{0,8},{4,12},{8,0},{12,4},{16,24},{20,28},{24,16},{28,20},{1,9},{5... | collective-permute-start | bytes 221192 | tf_op jit(solution)/shard_map/ppermute | solution.py:305
  35.5 1.5 %shard_map.60 = (bf16[8,256,256]{2,1,0:T(8,128)(2,1)S(1)}, f32[8,256,256]{2,1,0:T(8,128)S(1)}) custom-call(bf16[256,4096]{1,0:T(8,128)(2,1)S(1)} %get-tuple-element.55.q, bf16[256,4096]{1,0:T(8,128)(2,1)S(1)} %get-tuple-element.53.v, bf16[8,256,256]{2,1,0:T(8,128)(2,1)S(1)} %get-tuple-element.60.refs_2_.phi_k, ...), custom_call_target="tpu_custom_call" | custom-call | tf_op jit(solution)/shard_map/pallas_call | solution.py:330
  37.0 1.5 %shard_map.61 = (bf16[8,256,256]{2,1,0:T(8,128)(2,1)S(1)}, f32[8,256,256]{2,1,0:T(8,128)S(1)}) custom-call(bf16[256,4096]{1,0:T(8,128)(2,1)S(1)} %get-tuple-element.55.q, bf16[256,4096]{1,0:T(8,128)(2,1)S(1)} %get-tuple-element.53.v, bf16[8,256,256]{2,1,0:T(8,128)(2,1)S(1)} %get-tuple-element.79.phi_k, bf16[4,256,128]{2,1,0:T(8,128)(2,1)S(1)} %shard_map.49.refs_0_.rest_0_, ...), custom_call_target="tpu_custom_call" | custom-call | tf_op jit(solution)/shard_map/pallas_call | solution.py:330
  38.5 1.7 %shard_map.59 = (bf16[8,256,256]{2,1,0:T(8,128)(2,1)S(1)}, f32[8,256,256]{2,1,0:T(8,128)S(1)}) custom-call(bf16[256,4096]{1,0:T(8,128)(2,1)S(1)} %get-tuple-element.55.q, bf16[256,4096]{1,0:T(8,128)(2,1)S(1)} %get-tuple-element.53.v, bf16[8,256,256]{2,1,0:T(8,128)(2,1)S(1)} %get-tuple-element.56.phi_k, ...), custom_call_target="tpu_custom_call" | custom-call | tf_op jit(solution)/shard_map/pallas_call | solution.py:330
  41.6 1.5 %collective-permute-start.22 = (bf16[128,256]{1,0:T(8,128)(2,1)S(1)}, bf16[128,256]{1,0:T(8,128)(2,1)S(1)}, u32[]{:S(2)}, u32[]{:S(2)}) collective-permute-start(bf16[128,256]{1,0:T(8,128)(2,1)S(1)} %get-tuple-element.82), channel_id=1, source_target_pairs={{0,16},{4,20},{8,24},{12,28},{16,0},{20,4},{24,8},{28,12},{1,17},{... | collective-permute-start | bytes 196616 | tf_op jit(solution)/shard_map/ppermute | solution.py:305
  43.0 1.6 %collective-permute-start.23 = (bf16[128,256]{1,0:T(8,128)(2,1)S(1)}, bf16[128,256]{1,0:T(8,128)(2,1)S(1)}, u32[]{:S(2)}, u32[]{:S(2)}) collective-permute-start(bf16[128,256]{1,0:T(8,128)(2,1)S(1)} %get-tuple-element.83), channel_id=1, source_target_pairs={{0,8},{4,12},{8,0},{12,4},{16,24},{20,28},{24,16},{28,20},{1,9},{5... | collective-permute-start | bytes 196616 | tf_op jit(solution)/shard_map/ppermute | solution.py:305
  46.0 1.5 %shard_map.63 = (bf16[8,256,256]{2,1,0:T(8,128)(2,1)S(1)}, f32[8,256,256]{2,1,0:T(8,128)S(1)}) custom-call(bf16[256,4096]{1,0:T(8,128)(2,1)S(1)} %get-tuple-element.55.q, bf16[256,4096]{1,0:T(8,128)(2,1)S(1)} %get-tuple-element.53.v, bf16[8,256,256]{2,1,0:T(8,128)(2,1)S(1)} %get-tuple-element.86.phi_k, bf16[4,256,128]{2,1,0:T(8,128)(2,1)S(1)} %shard_map.53.refs_0_.rest_0_, ...), custom_call_target="tpu_custom_call" | custom-call | tf_op jit(solution)/shard_map/pallas_call | solution.py:330
  48.6 2.1 %collective-permute-done.21.refs_0_ = bf16[128,256]{1,0:T(8,128)(2,1)S(1)} collective-permute-done((bf16[128,256]{1,0:T(8,128)(2,1)S(1)}, bf16[128,256]{1,0:T(8,128)(2,1)S(1)}, u32[]{:S(2)}, u32[]{:S(2)}) %collective-permute-start.21) | collective-permute-done | bytes 65568 | tf_op jit(solution)/shard_map/ppermute | solution.py:305
  51.0 1.6 %collective-permute-start.24 = (bf16[528,256]{1,0:T(8,128)(2,1)S(1)}, bf16[528,256]{1,0:T(8,128)(2,1)S(1)}, u32[]{:S(2)}, u32[]{:S(2)}) collective-permute-start(bf16[528,256]{1,0:T(8,128)(2,1)S(1)} %get-tuple-element.88), channel_id=1, source_target_pairs={{0,4},{4,0},{8,12},{12,8},{16,20},{20,16},{24,28},{28,24},{1,5},{5... | collective-permute-start | bytes 811016 | tf_op jit(solution)/shard_map/ppermute | solution.py:305
  53.9 3.6 %collective-permute-done.24.base = bf16[528,256]{1,0:T(8,128)(2,1)S(1)} collective-permute-done((bf16[528,256]{1,0:T(8,128)(2,1)S(1)}, bf16[528,256]{1,0:T(8,128)(2,1)S(1)}, u32[]{:S(2)}, u32[]{:S(2)}) %collective-permute-start.24) | collective-permute-done | bytes 270368 | tf_op jit(solution)/shard_map/ppermute | solution.py:305
  60.2 2.5 %collective-permute-done.32.refs_2_ = bf16[528,256]{1,0:T(8,128)(2,1)S(1)} collective-permute-done((bf16[528,256]{1,0:T(8,128)(2,1)S(1)}, bf16[528,256]{1,0:T(8,128)(2,1)S(1)}, u32[]{:S(2)}, u32[]{:S(2)}) %collective-permute-start.32) | collective-permute-done | bytes 270368 | tf_op jit(solution)/shard_map/ppermute | solution.py:302
  63.9 4.1 %collective-permute-done.25.refs_0_ = bf16[528,256]{1,0:T(8,128)(2,1)S(1)} collective-permute-done((bf16[528,256]{1,0:T(8,128)(2,1)S(1)}, bf16[528,256]{1,0:T(8,128)(2,1)S(1)}, u32[]{:S(2)}, u32[]{:S(2)}) %collective-permute-start.25) | collective-permute-done | bytes 270368 | tf_op jit(solution)/shard_map/ppermute | solution.py:302
  (74 shorter events, 23.1 us)
Async XLA Ops:
  0.0 4.0 %collective-permute-start = (bf16[8,256,128]{2,1,0:T(8,128)(2,1)}, bf16[8,256,128]{2,1,0:T(8,128)(2,1)S(1)}, u32[]{:S(2)}, u32[]{:S(2)}) collective-permute-start(bf16[8,256,128]{2,1,0:T(8,128)(2,1)} %f_far.1), channel_id=1, source_target_pairs={{0,1},{1,0},{2,3},{3,2},{4,5},{5,4},{6,7},{7,6},{8,9},{9,8},{10,11... | collective-permute-start | bytes 1572872 | tf_op jit(solution)/shard_map/ppermute | solution.py:302
  1.4 9.5 %collective-permute-start.1 = (bf16[4,256,128]{2,1,0:T(8,128)(2,1)S(1)}, bf16[4,256,128]{2,1,0:T(8,128)(2,1)S(1)}, u32[]{:S(2)}, u32[]{:S(2)}) collective-permute-start(bf16[4,256,128]{2,1,0:T(8,128)(2,1)S(1)} %constant_dynamic-slice_fusion), channel_id=1, source_target_pairs={{0,2},{1,3},{2,0},{3,1},{4,6},{5,7},{6,4},{7,5},{8,10},{9,11},{10,... | collective-permute-start | bytes 786440 | tf_op jit(solution)/shard_map/ppermute | solution.py:302
  11.0 4.0 %collective-permute-start.5 = (bf16[4,256,128]{2,1,0:T(8,128)(2,1)S(1)}, bf16[4,256,128]{2,1,0:T(8,128)(2,1)S(1)}, u32[]{:S(2)}, u32[]{:S(2)}) collective-permute-start(bf16[4,256,128]{2,1,0:T(8,128)(2,1)S(1)} %shard_map.49.refs_0_.rest_0_), channel_id=1, source_target_pairs={{0,1},{1,0},{2,3},{3,2},{4,5},{5,4},{6,7},{7,6},{8,9},{9,8},{10,11... | collective-permute-start | bytes 786440 | tf_op jit(solution)/shard_map/ppermute | solution.py:302
  11.1 3.8 %collective-permute-start.7 = (bf16[272,256]{1,0:T(8,128)(2,1)S(1)}, bf16[272,256]{1,0:T(8,128)(2,1)S(1)}, u32[]{:S(2)}, u32[]{:S(2)}) collective-permute-start(bf16[272,256]{1,0:T(8,128)(2,1)S(1)} %get-tuple-element.63), channel_id=1, source_target_pairs={{0,1},{1,0},{2,3},{3,2},{4,5},{5,4},{6,7},{7,6},{8,9},{9,8},{10,11... | collective-permute-start | bytes 417800 | tf_op jit(solution)/shard_map/ppermute | solution.py:302
  11.6 8.7 %collective-permute-start.4 = (bf16[4,256,128]{2,1,0:T(8,128)(2,1)S(1)}, bf16[4,256,128]{2,1,0:T(8,128)(2,1)S(1)}, u32[]{:S(2)}, u32[]{:S(2)}) collective-permute-start(bf16[4,256,128]{2,1,0:T(8,128)(2,1)S(1)} %shard_map.49.refs_0_.rest_0_), channel_id=1, source_target_pairs={{0,4},{4,0},{8,12},{12,8},{16,20},{20,16},{24,28},{28,24},{1,5},{5... | collective-permute-start | bytes 786440 | tf_op jit(solution)/shard_map/ppermute | solution.py:305
  13.4 8.8 %collective-permute-start.16 = (bf16[528,256]{1,0:T(8,128)(2,1)S(1)}, bf16[528,256]{1,0:T(8,128)(2,1)S(1)}, u32[]{:S(2)}, u32[]{:S(2)}) collective-permute-start(bf16[528,256]{1,0:T(8,128)(2,1)S(1)} %shard_map.48.refs_1_.refs_2_), channel_id=1, source_target_pairs={{0,2},{1,3},{2,0},{3,1},{4,6},{5,7},{6,4},{7,5},{8,10},{9,11},{10,... | collective-permute-start | bytes 811016 | tf_op jit(solution)/shard_map/ppermute | solution.py:302
  20.4 8.9 %collective-permute-start.15 = (bf16[528,256]{1,0:T(8,128)(2,1)S(1)}, bf16[528,256]{1,0:T(8,128)(2,1)S(1)}, u32[]{:S(2)}, u32[]{:S(2)}) collective-permute-start(bf16[528,256]{1,0:T(8,128)(2,1)S(1)} %shard_map.50.refs_3_), channel_id=1, source_target_pairs={{0,2},{1,3},{2,0},{3,1},{4,6},{5,7},{6,4},{7,5},{8,10},{9,11},{10,... | collective-permute-start | bytes 811016 | tf_op jit(solution)/shard_map/ppermute | solution.py:302
  22.3 8.6 %collective-permute-start.17 = (bf16[528,256]{1,0:T(8,128)(2,1)S(1)}, bf16[528,256]{1,0:T(8,128)(2,1)S(1)}, u32[]{:S(2)}, u32[]{:S(2)}) collective-permute-start(bf16[528,256]{1,0:T(8,128)(2,1)S(1)} %shard_map.57), channel_id=1, source_target_pairs={{0,4},{4,0},{8,12},{12,8},{16,20},{20,16},{24,28},{28,24},{1,5},{5... | collective-permute-start | bytes 811016 | tf_op jit(solution)/shard_map/ppermute | solution.py:305
  31.0 9.2 %collective-permute-start.19 = (bf16[144,256]{1,0:T(8,128)(2,1)S(1)}, bf16[144,256]{1,0:T(8,128)(2,1)S(1)}, u32[]{:S(2)}, u32[]{:S(2)}) collective-permute-start(bf16[144,256]{1,0:T(8,128)(2,1)S(1)} %get-tuple-element.75), channel_id=1, source_target_pairs={{0,16},{4,20},{8,24},{12,28},{16,0},{20,4},{24,8},{28,12},{1,17},{... | collective-permute-start | bytes 221192 | tf_op jit(solution)/shard_map/ppermute | solution.py:305
  33.7 6.6 %collective-permute-start.20 = (bf16[144,256]{1,0:T(8,128)(2,1)S(1)}, bf16[144,256]{1,0:T(8,128)(2,1)S(1)}, u32[]{:S(2)}, u32[]{:S(2)}) collective-permute-start(bf16[144,256]{1,0:T(8,128)(2,1)S(1)} %get-tuple-element.76), channel_id=1, source_target_pairs={{0,8},{4,12},{8,0},{12,4},{16,24},{20,28},{24,16},{28,20},{1,9},{5... | collective-permute-start | bytes 221192 | tf_op jit(solution)/shard_map/ppermute | solution.py:305
  35.2 6.2 %collective-permute-start.18 = (bf16[144,256]{1,0:T(8,128)(2,1)S(1)}, bf16[144,256]{1,0:T(8,128)(2,1)S(1)}, u32[]{:S(2)}, u32[]{:S(2)}) collective-permute-start(bf16[144,256]{1,0:T(8,128)(2,1)S(1)} %get-tuple-element.72.rest_2_), channel_id=1, source_target_pairs={{0,24},{4,28},{8,16},{12,20},{16,8},{20,12},{24,0},{28,4},{1,25},{... | collective-permute-start | bytes 221192 | tf_op jit(solution)/shard_map/ppermute | solution.py:305
  41.6 6.7 %collective-permute-start.22 = (bf16[128,256]{1,0:T(8,128)(2,1)S(1)}, bf16[128,256]{1,0:T(8,128)(2,1)S(1)}, u32[]{:S(2)}, u32[]{:S(2)}) collective-permute-start(bf16[128,256]{1,0:T(8,128)(2,1)S(1)} %get-tuple-element.82), channel_id=1, source_target_pairs={{0,16},{4,20},{8,24},{12,28},{16,0},{20,4},{24,8},{28,12},{1,17},{... | collective-permute-start | bytes 196616 | tf_op jit(solution)/shard_map/ppermute | solution.py:305
  43.0 5.6 %collective-permute-start.23 = (bf16[128,256]{1,0:T(8,128)(2,1)S(1)}, bf16[128,256]{1,0:T(8,128)(2,1)S(1)}, u32[]{:S(2)}, u32[]{:S(2)}) collective-permute-start(bf16[128,256]{1,0:T(8,128)(2,1)S(1)} %get-tuple-element.83), channel_id=1, source_target_pairs={{0,8},{4,12},{8,0},{12,4},{16,24},{20,28},{24,16},{28,20},{1,9},{5... | collective-permute-start | bytes 196616 | tf_op jit(solution)/shard_map/ppermute | solution.py:305
  44.7 6.1 %collective-permute-start.21 = (bf16[128,256]{1,0:T(8,128)(2,1)S(1)}, bf16[128,256]{1,0:T(8,128)(2,1)S(1)}, u32[]{:S(2)}, u32[]{:S(2)}) collective-permute-start(bf16[128,256]{1,0:T(8,128)(2,1)S(1)} %get-tuple-element.81.rest_2_), channel_id=1, source_target_pairs={{0,24},{4,28},{8,16},{12,20},{16,8},{20,12},{24,0},{28,4},{1,25},{... | collective-permute-start | bytes 196616 | tf_op jit(solution)/shard_map/ppermute | solution.py:305
  51.0 6.5 %collective-permute-start.24 = (bf16[528,256]{1,0:T(8,128)(2,1)S(1)}, bf16[528,256]{1,0:T(8,128)(2,1)S(1)}, u32[]{:S(2)}, u32[]{:S(2)}) collective-permute-start(bf16[528,256]{1,0:T(8,128)(2,1)S(1)} %get-tuple-element.88), channel_id=1, source_target_pairs={{0,4},{4,0},{8,12},{12,8},{16,20},{20,16},{24,28},{28,24},{1,5},{5... | collective-permute-start | bytes 811016 | tf_op jit(solution)/shard_map/ppermute | solution.py:305
  52.6 5.2 %collective-permute-start.29 = (bf16[528,256]{1,0:T(8,128)(2,1)S(1)}, bf16[528,256]{1,0:T(8,128)(2,1)S(1)}, u32[]{:S(2)}, u32[]{:S(2)}) collective-permute-start(bf16[528,256]{1,0:T(8,128)(2,1)S(1)} %get-tuple-element.69.mine), channel_id=1, source_target_pairs={{0,1},{1,0},{2,3},{3,2},{4,5},{5,4},{6,7},{7,6},{8,9},{9,8},{10,11... | collective-permute-start | bytes 811016 | tf_op jit(solution)/shard_map/ppermute | solution.py:302
  52.7 5.7 %collective-permute-start.28 = (bf16[528,256]{1,0:T(8,128)(2,1)S(1)}, bf16[528,256]{1,0:T(8,128)(2,1)S(1)}, u32[]{:S(2)}, u32[]{:S(2)}) collective-permute-start(bf16[528,256]{1,0:T(8,128)(2,1)S(1)} %get-tuple-element.94.refs_2_), channel_id=1, source_target_pairs={{0,1},{1,0},{2,3},{3,2},{4,5},{5,4},{6,7},{7,6},{8,9},{9,8},{10,11... | collective-permute-start | bytes 811016 | tf_op jit(solution)/shard_map/ppermute | solution.py:302
  53.3 6.5 %collective-permute-start.27 = (bf16[528,256]{1,0:T(8,128)(2,1)S(1)}, bf16[528,256]{1,0:T(8,128)(2,1)S(1)}, u32[]{:S(2)}, u32[]{:S(2)}) collective-permute-start(bf16[528,256]{1,0:T(8,128)(2,1)S(1)} %get-tuple-element.64.mine), channel_id=1, source_target_pairs={{0,1},{1,0},{2,3},{3,2},{4,5},{5,4},{6,7},{7,6},{8,9},{9,8},{10,11... | collective-permute-start | bytes 811016 | tf_op jit(solution)/shard_map/ppermute | solution.py:302
  53.4 9.3 %collective-permute-start.32 = (bf16[528,256]{1,0:T(8,128)(2,1)S(1)}, bf16[528,256]{1,0:T(8,128)(2,1)S(1)}, u32[]{:S(2)}, u32[]{:S(2)}) collective-permute-start(bf16[528,256]{1,0:T(8,128)(2,1)S(1)} %get-tuple-element.97), channel_id=1, source_target_pairs={{0,2},{1,3},{2,0},{3,1},{4,6},{5,7},{6,4},{7,5},{8,10},{9,11},{10,... | collective-permute-start | bytes 811016 | tf_op jit(solution)/shard_map/ppermute | solution.py:302
  57.7 5.0 %collective-permute-start.26 = (bf16[528,256]{1,0:T(8,128)(2,1)S(1)}, bf16[528,256]{1,0:T(8,128)(2,1)S(1)}, u32[]{:S(2)}, u32[]{:S(2)}) collective-permute-start(bf16[528,256]{1,0:T(8,128)(2,1)S(1)} %get-tuple-element.91.refs_2_), channel_id=1, source_target_pairs={{0,1},{1,0},{2,3},{3,2},{4,5},{5,4},{6,7},{7,6},{8,9},{9,8},{10,11... | collective-permute-start | bytes 811016 | tf_op jit(solution)/shard_map/ppermute | solution.py:302
  57.8 10.2 %collective-permute-start.25 = (bf16[528,256]{1,0:T(8,128)(2,1)S(1)}, bf16[528,256]{1,0:T(8,128)(2,1)S(1)}, u32[]{:S(2)}, u32[]{:S(2)}) collective-permute-start(bf16[528,256]{1,0:T(8,128)(2,1)S(1)} %get-tuple-element.89), channel_id=1, source_target_pairs={{0,2},{1,3},{2,0},{3,1},{4,6},{5,7},{6,4},{7,5},{8,10},{9,11},{10,... | collective-permute-start | bytes 811016 | tf_op jit(solution)/shard_map/ppermute | solution.py:302
  58.4 12.1 %collective-permute-start.31 = (bf16[528,256]{1,0:T(8,128)(2,1)S(1)}, bf16[528,256]{1,0:T(8,128)(2,1)S(1)}, u32[]{:S(2)}, u32[]{:S(2)}) collective-permute-start(bf16[528,256]{1,0:T(8,128)(2,1)S(1)} %get-tuple-element.57.mine), channel_id=1, source_target_pairs={{0,1},{1,0},{2,3},{3,2},{4,5},{5,4},{6,7},{7,6},{8,9},{9,8},{10,11... | collective-permute-start | bytes 811016 | tf_op jit(solution)/shard_map/ppermute | solution.py:302
  59.8 9.4 %collective-permute-start.34 = (bf16[528,256]{1,0:T(8,128)(2,1)S(1)}, bf16[528,256]{1,0:T(8,128)(2,1)S(1)}, u32[]{:S(2)}, u32[]{:S(2)}) collective-permute-start(bf16[528,256]{1,0:T(8,128)(2,1)S(1)} %get-tuple-element.61.mine), channel_id=1, source_target_pairs={{0,1},{1,0},{2,3},{3,2},{4,5},{5,4},{6,7},{7,6},{8,9},{9,8},{10,11... | collective-permute-start | bytes 811016 | tf_op jit(solution)/shard_map/ppermute | solution.py:302
  62.6 6.6 %collective-permute-start.33 = (bf16[528,256]{1,0:T(8,128)(2,1)S(1)}, bf16[528,256]{1,0:T(8,128)(2,1)S(1)}, u32[]{:S(2)}, u32[]{:S(2)}) collective-permute-start(bf16[528,256]{1,0:T(8,128)(2,1)S(1)} %collective-permute-done.32.refs_2_), channel_id=1, source_target_pairs={{0,1},{1,0},{2,3},{3,2},{4,5},{5,4},{6,7},{7,6},{8,9},{9,8},{10,11... | collective-permute-start | bytes 811016 | tf_op jit(solution)/shard_map/ppermute | solution.py:302
  (11 other events, 22.9 us)

commit v6 on v5

--- a/solution.py
+++ b/solution.py
@@ -175,13 +175,16 @@
         phi_q, inner, base, *extras = jobs_refs[n]
         count = phi_q.shape[-1]
         place = place_of(pos, key, nx, ny, core)[0]
-        each = group // len(extras)
-        last = extras[-1][each * size :]
-        totals = base[group * size :].astype(F32) + add * last.astype(F32)
+        each = group // max(len(extras), 1)
+        totals = base[group * size :].astype(F32)
+        if extras:
+            totals = totals + add * extras[-1][each * size :].astype(F32)
         for h in range(group):
             rows = slice(h * size, (h + 1) * size)
-            extra = extras[h // each][h % each * size : (h % each + 1) * size]
-            st = (base[rows].astype(F32) + add * extra.astype(F32)).astype(BF16)
+            st = base[rows]
+            if extras:
+                extra = extras[h // each][h % each * size : (h % each + 1) * size]
+                st = (st.astype(F32) + add * extra.astype(F32)).astype(BF16)
             tot = jnp.broadcast_to(totals[h : h + 1], (size, count)).astype(BF16)
             at = (1 - core) * group + h
             acc = inner[at] + lax.dot_general(
@@ -191,18 +194,21 @@
                 preferred_element_type=F32,
             )
             ready[n, :, rows] = (acc[:, :size] / acc[:, size:]).astype(BF16)
-        wide = group * size
-        copy = pltpu.make_async_copy(
-            ready.at[n],
-            out.at[:, pl.ds(pl.multiple_of(place * wide, wide), wide)],
-            sems.at[n],
-        )
-        copy.start()
-        copies.append(copy)
+            start = pl.multiple_of((place * group + h) * size, size)
+            copy = pltpu.make_async_copy(
+                ready.at[n, :, rows], out.at[:, pl.ds(start, size)], sems.at[n, h]
+            )
+            copy.start()
+            copies.append(copy)
     for mark in marks:
         mark[...] = jnp.zeros(mark.shape, F32)
     for copy in copies:
         copy.wait()
+
+
+def far_kernel(shape, base, mine, *refs):
+    add = (position(*shape[:2])[1] == 0).astype(F32)
+    refs[-1][...] = (base[...].astype(F32) + add * mine[...].astype(F32)).astype(BF16)
 
 
 def tie_kernel(count, *refs):
@@ -347,7 +353,7 @@
     whole = jax.ShapeDtypeStruct((rows, count), BF16)
 
     dirs, phi_k, phi_w, piece, got, theirs = {}, {}, {}, {}, {}, {}
-    near_k, near_q = [], []
+    near_k, near_q, own_sums = [], [], {}
 
     def states(key, after=()):
         cuts = group if key == later[0] else min(group, 2)
@@ -385,7 +391,7 @@
             )
         *other, mine = sums
         other = [head_swap(a, 1) for a in other]
-        theirs[key] = [other, [head_swap(mine, 1)]]
+        theirs[key], own_sums[key] = other, mine
         piece[key] = call(chip_kernel, whole, [mine, *other])
         got[key] = head_swap(piece[key], key[0] * cores) if key[0] else piece[key]
         return mine
@@ -411,7 +417,7 @@
     later = [(dx, dy) for dx in range(nx) for dy in reversed(range(ny)) if dx != flip]
     for key in first:
         states(key)
-    ready = [piece[first[0]], phi_k[first[-1]]]
+    ready = [piece[first[0]], piece[first[-1]]]
     for ox in range(1, nx):
         if ny == 2:
             part = lax.dynamic_slice_in_dim(features, (position(nx, ny)[2] ^ 1) * group, group, 0)
@@ -428,7 +434,7 @@
         if key != later[0] and ny == 2:
             (rest,) = tie([dirs[key][0]], [piece[later[0]]])
             dirs[key] = (rest, head_swap(rest, 1))
-        states(key, [piece[key] for key in first])
+        states(key, [piece[first[0]]])
 
     rows_of = {}
     for dy in reversed(range(ny)):
@@ -474,24 +480,26 @@
             result[dx, dy] = head_swap(a, dx * cores) if dx else a
 
     late = [key for key in plane if all(key)]
-    soon = [key for key in plane if not key[0]]
-    batches = [[(key, 0), (key, 1)] for key in soon]
+    middle = [key for key in plane if key[0] and not key[1]]
+    batches = [[(key, 0), (key, 1)] for key in plane if not key[0]]
+    batches += [[(key, 0) for key in middle]] if middle else []
     tied = len(batches)
-    batches += [[(key, 0) for key in late]] if late else []
-    batches += [[(key, 0), (key, 1)] for key in plane if key not in late + soon]
+    batches += [[(key, 1) for key in middle] + [(key, 0) for key in late]] if middle else []
     batches += [[(key, 1) for key in late]] if late else []
-    out = None
+    out, mark = None, []
     for i, jobs in enumerate(batches):
         args = []
-        if i == tied:
-            result.update(zip(late, tie([result[key] for key in late], mark)))
         counts = []
         for key, core in jobs:
-            base = head_swap(result[key], 1) if core else result[key]
-            args += [*phi_w[key], base, *theirs[key][core]]
-            counts.append(3 + len(theirs[key][core]))
+            base, extras = result[key], theirs[key]
+            if core:
+                kernel = functools.partial(far_kernel, shape)
+                base = call(kernel, whole, [base, own_sums[key]], mark if key in late else [])
+                base, extras = head_swap(base, 1), []
+            args += [*phi_w[key], base, *extras]
+            counts.append(3 + len(extras))
         marked = [pltpu.VMEM((8, 128), F32)] if i == tied - 1 else []
-        out, *mark = call(
+        out, *marks = call(
             functools.partial(output_kernel, jobs, counts, shape, int(i > 0)),
             [jax.ShapeDtypeStruct((tokens, width), BF16), *marked],
             args,
@@ -499,10 +507,11 @@
             [anywhere] + [near] * len(marked),
             [
                 pltpu.VMEM((len(jobs), tokens, group * size), BF16),
-                pltpu.SemaphoreType.DMA((len(jobs),)),
+                pltpu.SemaphoreType.DMA((len(jobs), group)),
             ],
             {} if out is None else {len(args): 0},
         )
+        mark = marks or mark
     return out.reshape(queries.shape)
 
 

time: 71.9 us -> 69.3 us (0.964)
  waiting for transfers between devices: 24.4 us -> 22.6 us
  starting transfers between devices: 25.3 us -> 24.3 us
    ppermute x26 -> x22, waiting for transfers between devices: 13.7 us -> 11.3 us  [head_swap(): return lax.ppermute(a, 'head', [(i, i ^ bits) for i in range(heads)])]
    ppermute x26 -> x22, starting transfers between devices: 11.5 us -> 10.4 us  [head_swap(): return lax.ppermute(a, 'head', [(i, i ^ bits) for i in range(heads)])]
    pallas_call x27 -> x30, Pallas kernels: 20.6 us -> 20.8 us  [call(): pl.pallas_call(kernel, out_shape=out, in_specs=[far] * len(there) + [near...]
  transfers between devices with their start and end apart: 35 -> 31, of which waited for: 15 -> 18; matrix products, arithmetic and copies ran while one was open for 1% -> 1% of each run, Pallas kernels for 27% -> 28%
where the time goes in v6:
time: 69.3 us; the launch traced here: 69.1 us
  starting transfers between devices  24.3 us (35%)
  waiting for transfers between devices  22.6 us (33%)
  Pallas kernels  20.8 us (30%)
  local copies, waits for them, and re-layouts  0.97 us (1%)
    pallas_call x30, Pallas kernels, call(): pl.pallas_call(kernel, out_shape=out, in_specs=[far] * len(there) + [near...  20.8 us
    ppermute x9, starting transfers between devices, seq_swap(): return lax.ppermute(a, 'seq', [(i, i ^ bits) for i in range(seqs)])  13.9 us
    ppermute x22, waiting for transfers between devices, head_swap(): return lax.ppermute(a, 'head', [(i, i ^ bits) for i in range(heads)])  11.3 us
    ppermute x9, waiting for transfers between devices, seq_swap(): return lax.ppermute(a, 'seq', [(i, i ^ bits) for i in range(seqs)])  11.3 us
    ppermute x22, starting transfers between devices, head_swap(): return lax.ppermute(a, 'head', [(i, i ^ bits) for i in range(heads)])  10.4 us
  transfers between devices with their start and end apart: 31, of which 18 were waited for; matrix products, arithmetic and copies ran while one was open for 1% of the time, Pallas kernels for 28%

profile of v6, /device:TPU:0, one launch (start us, length us, event | category | flops | bytes accessed | tf_op | source)
XLA Modules:
  0.0 69.1 jit_solution(12458817193758452116)
XLA Ops:
  1.4 2.6 %collective-permute-start.1 = (bf16[4,256,128]{2,1,0:T(8,128)(2,1)S(1)}, bf16[4,256,128]{2,1,0:T(8,128)(2,1)S(1)}, u32[]{:S(2)}, u32[]{:S(2)}) collective-permute-start(bf16[4,256,128]{2,1,0:T(8,128)(2,1)S(1)} %constant_dynamic-slice_fusion), channel_id=1, source_target_pairs={{0,2},{1,3},{2,0},{3,1},{4,6},{5,7},{6,4},{7,5},{8,10},{9,11},{10,... | collective-permute-start | bytes 786440 | tf_op jit(solution)/shard_map/ppermute | solution.py:308
  4.0 2.7 %shard_map.46 = (bf16[8,256,256]{2,1,0:T(8,128)(2,1)S(1)}, bf16[256,256]{1,0:T(8,128)(2,1)S(1)}, bf16[272,256]{1,0:T(8,128)(2,1)S(1)}, bf16[528,256]{1,0:T(8,128...) custom-call(bf16[256,4096]{1,0:T(8,128)(2,1)} %bitcast.5, ...), custom_call_target="tpu_custom_call" | custom-call | tf_op jit(solution)/shard_map/pallas_call | solution.py:336
  7.0 1.6 %shard_map.47 = (bf16[8,256,256]{2,1,0:T(8,128)(2,1)S(1)}, bf16[256,256]{1,0:T(8,128)(2,1)S(1)}, bf16[272,256]{1,0:T(8,128)(2,1)S(1)}, bf16[528,256]{1,0:T(8,128)(2,1)S(1)}, bf16[256,4096]{1,0:T(8,128)(2,1)S(1)}) custom-call(bf16[256,4096]{1,0:T(8,128)(2,1)} %bitcast.4, bf16[256,4096]{1,0:T(8,128)(2,1)S(1)} %get-tuple-element.52.k, ...), custom_call_target="tpu_custom_call" | custom-call | tf_op jit(solution)/shard_map/pallas_call | solution.py:336
  11.1 1.8 %collective-permute-start.6 = (bf16[4,256,128]{2,1,0:T(8,128)(2,1)S(1)}, bf16[4,256,128]{2,1,0:T(8,128)(2,1)S(1)}, u32[]{:S(2)}, u32[]{:S(2)}) collective-permute-start(bf16[4,256,128]{2,1,0:T(8,128)(2,1)S(1)} %shard_map.50.refs_0_.rest_0_), channel_id=1, source_target_pairs={{0,4},{4,0},{8,12},{12,8},{16,20},{20,16},{24,28},{28,24},{1,5},{5... | collective-permute-start | bytes 786440 | tf_op jit(solution)/shard_map/ppermute | solution.py:311
  12.9 1.5 %collective-permute-start.16 = (bf16[528,256]{1,0:T(8,128)(2,1)S(1)}, bf16[528,256]{1,0:T(8,128)(2,1)S(1)}, u32[]{:S(2)}, u32[]{:S(2)}) collective-permute-start(bf16[528,256]{1,0:T(8,128)(2,1)S(1)} %shard_map.48.refs_1_.refs_2_), channel_id=1, source_target_pairs={{0,2},{1,3},{2,0},{3,1},{4,6},{5,7},{6,4},{7,5},{8,10},{9,11},{10,... | collective-permute-start | bytes 811016 | tf_op jit(solution)/shard_map/ppermute | solution.py:308
  14.4 1.4 %shard_map.51 = (bf16[8,256,256]{2,1,0:T(8,128)(2,1)S(1)}, bf16[128,256]{1,0:T(8,128)(2,1)S(1)}, bf16[128,256]{1,0:T(8,128)(2,1)S(1)}, bf16[128,256]{1,0:T(8,128...) custom-call(bf16[256,4096]{1,0:T(8,128)(2,1)S(1)} %get-tuple-element.52.k, ...), custom_call_target="tpu_custom_call" | custom-call | tf_op jit(solution)/shard_map/pallas_call | solution.py:336
  19.9 1.8 %collective-permute-start.15 = (bf16[528,256]{1,0:T(8,128)(2,1)S(1)}, bf16[528,256]{1,0:T(8,128)(2,1)S(1)}, u32[]{:S(2)}, u32[]{:S(2)}) collective-permute-start(bf16[528,256]{1,0:T(8,128)(2,1)S(1)} %shard_map.49.refs_2_), channel_id=1, source_target_pairs={{0,2},{1,3},{2,0},{3,1},{4,6},{5,7},{6,4},{7,5},{8,10},{9,11},{10,... | collective-permute-start | bytes 811016 | tf_op jit(solution)/shard_map/ppermute | solution.py:308
  21.8 1.6 %collective-permute-start.17 = (bf16[528,256]{1,0:T(8,128)(2,1)S(1)}, bf16[528,256]{1,0:T(8,128)(2,1)S(1)}, u32[]{:S(2)}, u32[]{:S(2)}) collective-permute-start(bf16[528,256]{1,0:T(8,128)(2,1)S(1)} %shard_map.57), channel_id=1, source_target_pairs={{0,4},{4,0},{8,12},{12,8},{16,20},{20,16},{24,28},{28,24},{1,5},{5... | collective-permute-start | bytes 811016 | tf_op jit(solution)/shard_map/ppermute | solution.py:311
  23.3 1.4 %shard_map.54 = (bf16[8,256,256]{2,1,0:T(8,128)(2,1)S(1)}, bf16[256,256]{1,0:T(8,128)(2,1)S(1)}, bf16[272,256]{1,0:T(8,128)(2,1)S(1)}, bf16[528,256]{1,0:T(8,128)(2,1)S(1)}) custom-call(bf16[256,4096]{1,0:T(8,128)(2,1)S(1)} %get-tuple-element.52.k, bf16[256,4096]{1,0:T(8,128)(2,1)S(1)} %get-tuple-element.53.v, ...), custom_call_target="tpu_custom_call" | custom-call | tf_op jit(solution)/shard_map/pallas_call | solution.py:336
  26.5 2.3 %collective-permute-done.15.refs_1_ = bf16[528,256]{1,0:T(8,128)(2,1)S(1)} collective-permute-done((bf16[528,256]{1,0:T(8,128)(2,1)S(1)}, bf16[528,256]{1,0:T(8,128)(2,1)S(1)}, u32[]{:S(2)}, u32[]{:S(2)}) %collective-permute-start.15) | collective-permute-done | bytes 270368 | tf_op jit(solution)/shard_map/ppermute | solution.py:308
  28.9 1.5 %collective-permute-done.17.refs_1_.refs_6_ = bf16[528,256]{1,0:T(8,128)(2,1)S(1)} collective-permute-done((bf16[528,256]{1,0:T(8,128)(2,1)S(1)}, bf16[528,256]{1,0:T(8,128)(2,1)S(1)}, u32[]{:S(2)}, u32[]{:S(2)}) %collective-permute-start.17) | collective-permute-done | bytes 270368 | tf_op jit(solution)/shard_map/ppermute | solution.py:311
  30.5 2.7 %collective-permute-start.19 = (bf16[144,256]{1,0:T(8,128)(2,1)S(1)}, bf16[144,256]{1,0:T(8,128)(2,1)S(1)}, u32[]{:S(2)}, u32[]{:S(2)}) collective-permute-start(bf16[144,256]{1,0:T(8,128)(2,1)S(1)} %get-tuple-element.74), channel_id=1, source_target_pairs={{0,16},{4,20},{8,24},{12,28},{16,0},{20,4},{24,8},{28,12},{1,17},{... | collective-permute-start | bytes 221192 | tf_op jit(solution)/shard_map/ppermute | solution.py:311
  33.1 1.6 %collective-permute-start.20 = (bf16[144,256]{1,0:T(8,128)(2,1)S(1)}, bf16[144,256]{1,0:T(8,128)(2,1)S(1)}, u32[]{:S(2)}, u32[]{:S(2)}) collective-permute-start(bf16[144,256]{1,0:T(8,128)(2,1)S(1)} %get-tuple-element.75), channel_id=1, source_target_pairs={{0,8},{4,12},{8,0},{12,4},{16,24},{20,28},{24,16},{28,20},{1,9},{5... | collective-permute-start | bytes 221192 | tf_op jit(solution)/shard_map/ppermute | solution.py:311
  34.9 1.5 %shard_map.61 = (bf16[8,256,256]{2,1,0:T(8,128)(2,1)S(1)}, f32[8,256,256]{2,1,0:T(8,128)S(1)}) custom-call(bf16[256,4096]{1,0:T(8,128)(2,1)S(1)} %get-tuple-element.55.q, bf16[256,4096]{1,0:T(8,128)(2,1)S(1)} %get-tuple-element.53.v, bf16[8,256,256]{2,1,0:T(8,128)(2,1)S(1)} %get-tuple-element.79.phi_k, bf16[4,256,128]{2,1,0:T(8,128)(2,1)S(1)} %shard_map.50.refs_0_.rest_0_, ...), custom_call_target="tpu_custom_call" | custom-call | tf_op jit(solution)/shard_map/pallas_call | solution.py:336
  36.4 1.5 %shard_map.60 = (bf16[8,256,256]{2,1,0:T(8,128)(2,1)S(1)}, f32[8,256,256]{2,1,0:T(8,128)S(1)}) custom-call(bf16[256,4096]{1,0:T(8,128)(2,1)S(1)} %get-tuple-element.55.q, bf16[256,4096]{1,0:T(8,128)(2,1)S(1)} %get-tuple-element.53.v, bf16[8,256,256]{2,1,0:T(8,128)(2,1)S(1)} %get-tuple-element.77.phi_k, ...), custom_call_target="tpu_custom_call" | custom-call | tf_op jit(solution)/shard_map/pallas_call | solution.py:336
  38.0 1.7 %shard_map.59 = (bf16[8,256,256]{2,1,0:T(8,128)(2,1)S(1)}, f32[8,256,256]{2,1,0:T(8,128)S(1)}) custom-call(bf16[256,4096]{1,0:T(8,128)(2,1)S(1)} %get-tuple-element.55.q, bf16[256,4096]{1,0:T(8,128)(2,1)S(1)} %get-tuple-element.53.v, bf16[8,256,256]{2,1,0:T(8,128)(2,1)S(1)} %get-tuple-element.56.phi_k, ...), custom_call_target="tpu_custom_call" | custom-call | tf_op jit(solution)/shard_map/pallas_call | solution.py:336
  41.1 1.5 %collective-permute-start.22 = (bf16[128,256]{1,0:T(8,128)(2,1)S(1)}, bf16[128,256]{1,0:T(8,128)(2,1)S(1)}, u32[]{:S(2)}, u32[]{:S(2)}) collective-permute-start(bf16[128,256]{1,0:T(8,128)(2,1)S(1)} %get-tuple-element.82), channel_id=1, source_target_pairs={{0,16},{4,20},{8,24},{12,28},{16,0},{20,4},{24,8},{28,12},{1,17},{... | collective-permute-start | bytes 196616 | tf_op jit(solution)/shard_map/ppermute | solution.py:311
  42.5 1.6 %collective-permute-start.23 = (bf16[128,256]{1,0:T(8,128)(2,1)S(1)}, bf16[128,256]{1,0:T(8,128)(2,1)S(1)}, u32[]{:S(2)}, u32[]{:S(2)}) collective-permute-start(bf16[128,256]{1,0:T(8,128)(2,1)S(1)} %get-tuple-element.83), channel_id=1, source_target_pairs={{0,8},{4,12},{8,0},{12,4},{16,24},{20,28},{24,16},{28,20},{1,9},{5... | collective-permute-start | bytes 196616 | tf_op jit(solution)/shard_map/ppermute | solution.py:311
  44.1 1.4 %collective-permute-start.21 = (bf16[128,256]{1,0:T(8,128)(2,1)S(1)}, bf16[128,256]{1,0:T(8,128)(2,1)S(1)}, u32[]{:S(2)}, u32[]{:S(2)}) collective-permute-start(bf16[128,256]{1,0:T(8,128)(2,1)S(1)} %get-tuple-element.81.rest_2_), channel_id=1, source_target_pairs={{0,24},{4,28},{8,16},{12,20},{16,8},{20,12},{24,0},{28,4},{1,25},{... | collective-permute-start | bytes 196616 | tf_op jit(solution)/shard_map/ppermute | solution.py:311
  45.5 1.5 %shard_map.63 = (bf16[8,256,256]{2,1,0:T(8,128)(2,1)S(1)}, f32[8,256,256]{2,1,0:T(8,128)S(1)}) custom-call(bf16[256,4096]{1,0:T(8,128)(2,1)S(1)} %get-tuple-element.55.q, bf16[256,4096]{1,0:T(8,128)(2,1)S(1)} %get-tuple-element.53.v, bf16[8,256,256]{2,1,0:T(8,128)(2,1)S(1)} %get-tuple-element.86.phi_k, bf16[4,256,128]{2,1,0:T(8,128)(2,1)S(1)} %shard_map.53.refs_0_.rest_0_, ...), custom_call_target="tpu_custom_call" | custom-call | tf_op jit(solution)/shard_map/pallas_call | solution.py:336
  48.1 2.1 %collective-permute-done.21.refs_0_ = bf16[128,256]{1,0:T(8,128)(2,1)S(1)} collective-permute-done((bf16[128,256]{1,0:T(8,128)(2,1)S(1)}, bf16[128,256]{1,0:T(8,128)(2,1)S(1)}, u32[]{:S(2)}, u32[]{:S(2)}) %collective-permute-start.21) | collective-permute-done | bytes 65568 | tf_op jit(solution)/shard_map/ppermute | solution.py:311
  50.4 1.6 %collective-permute-start.24 = (bf16[528,256]{1,0:T(8,128)(2,1)S(1)}, bf16[528,256]{1,0:T(8,128)(2,1)S(1)}, u32[]{:S(2)}, u32[]{:S(2)}) collective-permute-start(bf16[528,256]{1,0:T(8,128)(2,1)S(1)} %get-tuple-element.88), channel_id=1, source_target_pairs={{0,4},{4,0},{8,12},{12,8},{16,20},{20,16},{24,28},{28,24},{1,5},{5... | collective-permute-start | bytes 811016 | tf_op jit(solution)/shard_map/ppermute | solution.py:311
  52.9 4.1 %collective-permute-done.24.base = bf16[528,256]{1,0:T(8,128)(2,1)S(1)} collective-permute-done((bf16[528,256]{1,0:T(8,128)(2,1)S(1)}, bf16[528,256]{1,0:T(8,128)(2,1)S(1)}, u32[]{:S(2)}, u32[]{:S(2)}) %collective-permute-start.24) | collective-permute-done | bytes 270368 | tf_op jit(solution)/shard_map/ppermute | solution.py:311
  62.6 3.7 %collective-permute-done.25.base.refs_5_ = bf16[528,256]{1,0:T(8,128)(2,1)S(1)} collective-permute-done((bf16[528,256]{1,0:T(8,128)(2,1)S(1)}, bf16[528,256]{1,0:T(8,128)(2,1)S(1)}, u32[]{:S(2)}, u32[]{:S(2)}) %collective-permute-start.25) | collective-permute-done | bytes 270368 | tf_op jit(solution)/shard_map/ppermute | solution.py:308
  (69 shorter events, 22.1 us)
Async XLA Ops:
  0.0 4.0 %collective-permute-start = (bf16[8,256,128]{2,1,0:T(8,128)(2,1)}, bf16[8,256,128]{2,1,0:T(8,128)(2,1)S(1)}, u32[]{:S(2)}, u32[]{:S(2)}) collective-permute-start(bf16[8,256,128]{2,1,0:T(8,128)(2,1)} %f_far.1), channel_id=1, source_target_pairs={{0,1},{1,0},{2,3},{3,2},{4,5},{5,4},{6,7},{7,6},{8,9},{9,8},{10,11... | collective-permute-start | bytes 1572872 | tf_op jit(solution)/shard_map/ppermute | solution.py:308
  1.4 9.5 %collective-permute-start.1 = (bf16[4,256,128]{2,1,0:T(8,128)(2,1)S(1)}, bf16[4,256,128]{2,1,0:T(8,128)(2,1)S(1)}, u32[]{:S(2)}, u32[]{:S(2)}) collective-permute-start(bf16[4,256,128]{2,1,0:T(8,128)(2,1)S(1)} %constant_dynamic-slice_fusion), channel_id=1, source_target_pairs={{0,2},{1,3},{2,0},{3,1},{4,6},{5,7},{6,4},{7,5},{8,10},{9,11},{10,... | collective-permute-start | bytes 786440 | tf_op jit(solution)/shard_map/ppermute | solution.py:308
  6.7 3.6 %collective-permute-start.3 = (bf16[272,256]{1,0:T(8,128)(2,1)S(1)}, bf16[272,256]{1,0:T(8,128)(2,1)S(1)}, u32[]{:S(2)}, u32[]{:S(2)}) collective-permute-start(bf16[272,256]{1,0:T(8,128)(2,1)S(1)} %get-tuple-element.59), channel_id=1, source_target_pairs={{0,1},{1,0},{2,3},{3,2},{4,5},{5,4},{6,7},{7,6},{8,9},{9,8},{10,11... | collective-permute-start | bytes 417800 | tf_op jit(solution)/shard_map/ppermute | solution.py:308
  8.6 1.9 %collective-permute-start.5 = (bf16[272,256]{1,0:T(8,128)(2,1)S(1)}, bf16[272,256]{1,0:T(8,128)(2,1)S(1)}, u32[]{:S(2)}, u32[]{:S(2)}) collective-permute-start(bf16[272,256]{1,0:T(8,128)(2,1)S(1)} %get-tuple-element.62), channel_id=1, source_target_pairs={{0,1},{1,0},{2,3},{3,2},{4,5},{5,4},{6,7},{7,6},{8,9},{9,8},{10,11... | collective-permute-start | bytes 417800 | tf_op jit(solution)/shard_map/ppermute | solution.py:308
  11.0 3.4 %collective-permute-start.7 = (bf16[4,256,128]{2,1,0:T(8,128)(2,1)S(1)}, bf16[4,256,128]{2,1,0:T(8,128)(2,1)S(1)}, u32[]{:S(2)}, u32[]{:S(2)}) collective-permute-start(bf16[4,256,128]{2,1,0:T(8,128)(2,1)S(1)} %shard_map.50.refs_0_.rest_0_), channel_id=1, source_target_pairs={{0,1},{1,0},{2,3},{3,2},{4,5},{5,4},{6,7},{7,6},{8,9},{9,8},{10,11... | collective-permute-start | bytes 786440 | tf_op jit(solution)/shard_map/ppermute | solution.py:308
  11.1 8.7 %collective-permute-start.6 = (bf16[4,256,128]{2,1,0:T(8,128)(2,1)S(1)}, bf16[4,256,128]{2,1,0:T(8,128)(2,1)S(1)}, u32[]{:S(2)}, u32[]{:S(2)}) collective-permute-start(bf16[4,256,128]{2,1,0:T(8,128)(2,1)S(1)} %shard_map.50.refs_0_.rest_0_), channel_id=1, source_target_pairs={{0,4},{4,0},{8,12},{12,8},{16,20},{20,16},{24,28},{28,24},{1,5},{5... | collective-permute-start | bytes 786440 | tf_op jit(solution)/shard_map/ppermute | solution.py:311
  12.9 8.8 %collective-permute-start.16 = (bf16[528,256]{1,0:T(8,128)(2,1)S(1)}, bf16[528,256]{1,0:T(8,128)(2,1)S(1)}, u32[]{:S(2)}, u32[]{:S(2)}) collective-permute-start(bf16[528,256]{1,0:T(8,128)(2,1)S(1)} %shard_map.48.refs_1_.refs_2_), channel_id=1, source_target_pairs={{0,2},{1,3},{2,0},{3,1},{4,6},{5,7},{6,4},{7,5},{8,10},{9,11},{10,... | collective-permute-start | bytes 811016 | tf_op jit(solution)/shard_map/ppermute | solution.py:308
  15.9 2.5 %collective-permute-start.11 = (bf16[144,256]{1,0:T(8,128)(2,1)S(1)}, bf16[144,256]{1,0:T(8,128)(2,1)S(1)}, u32[]{:S(2)}, u32[]{:S(2)}) collective-permute-start(bf16[144,256]{1,0:T(8,128)(2,1)S(1)} %get-tuple-element.67), channel_id=1, source_target_pairs={{0,1},{1,0},{2,3},{3,2},{4,5},{5,4},{6,7},{7,6},{8,9},{9,8},{10,11... | collective-permute-start | bytes 221192 | tf_op jit(solution)/shard_map/ppermute | solution.py:308
  19.8 3.5 %collective-permute-start.12 = (bf16[4,256,128]{2,1,0:T(8,128)(2,1)S(1)}, bf16[4,256,128]{2,1,0:T(8,128)(2,1)S(1)}, u32[]{:S(2)}, u32[]{:S(2)}) collective-permute-start(bf16[4,256,128]{2,1,0:T(8,128)(2,1)S(1)} %shard_map.53.refs_0_.rest_0_), channel_id=1, source_target_pairs={{0,1},{1,0},{2,3},{3,2},{4,5},{5,4},{6,7},{7,6},{8,9},{9,8},{10,11... | collective-permute-start | bytes 786440 | tf_op jit(solution)/shard_map/ppermute | solution.py:308
  19.9 8.9 %collective-permute-start.15 = (bf16[528,256]{1,0:T(8,128)(2,1)S(1)}, bf16[528,256]{1,0:T(8,128)(2,1)S(1)}, u32[]{:S(2)}, u32[]{:S(2)}) collective-permute-start(bf16[528,256]{1,0:T(8,128)(2,1)S(1)} %shard_map.49.refs_2_), channel_id=1, source_target_pairs={{0,2},{1,3},{2,0},{3,1},{4,6},{5,7},{6,4},{7,5},{8,10},{9,11},{10,... | collective-permute-start | bytes 811016 | tf_op jit(solution)/shard_map/ppermute | solution.py:308
  21.8 8.6 %collective-permute-start.17 = (bf16[528,256]{1,0:T(8,128)(2,1)S(1)}, bf16[528,256]{1,0:T(8,128)(2,1)S(1)}, u32[]{:S(2)}, u32[]{:S(2)}) collective-permute-start(bf16[528,256]{1,0:T(8,128)(2,1)S(1)} %shard_map.57), channel_id=1, source_target_pairs={{0,4},{4,0},{8,12},{12,8},{16,20},{20,16},{24,28},{28,24},{1,5},{5... | collective-permute-start | bytes 811016 | tf_op jit(solution)/shard_map/ppermute | solution.py:311
  24.8 1.6 %collective-permute-start.14 = (bf16[272,256]{1,0:T(8,128)(2,1)S(1)}, bf16[272,256]{1,0:T(8,128)(2,1)S(1)}, u32[]{:S(2)}, u32[]{:S(2)}) collective-permute-start(bf16[272,256]{1,0:T(8,128)(2,1)S(1)} %get-tuple-element.70), channel_id=1, source_target_pairs={{0,1},{1,0},{2,3},{3,2},{4,5},{5,4},{6,7},{7,6},{8,9},{9,8},{10,11... | collective-permute-start | bytes 417800 | tf_op jit(solution)/shard_map/ppermute | solution.py:308
  30.5 9.2 %collective-permute-start.19 = (bf16[144,256]{1,0:T(8,128)(2,1)S(1)}, bf16[144,256]{1,0:T(8,128)(2,1)S(1)}, u32[]{:S(2)}, u32[]{:S(2)}) collective-permute-start(bf16[144,256]{1,0:T(8,128)(2,1)S(1)} %get-tuple-element.74), channel_id=1, source_target_pairs={{0,16},{4,20},{8,24},{12,28},{16,0},{20,4},{24,8},{28,12},{1,17},{... | collective-permute-start | bytes 221192 | tf_op jit(solution)/shard_map/ppermute | solution.py:311
  33.1 6.5 %collective-permute-start.20 = (bf16[144,256]{1,0:T(8,128)(2,1)S(1)}, bf16[144,256]{1,0:T(8,128)(2,1)S(1)}, u32[]{:S(2)}, u32[]{:S(2)}) collective-permute-start(bf16[144,256]{1,0:T(8,128)(2,1)S(1)} %get-tuple-element.75), channel_id=1, source_target_pairs={{0,8},{4,12},{8,0},{12,4},{16,24},{20,28},{24,16},{28,20},{1,9},{5... | collective-permute-start | bytes 221192 | tf_op jit(solution)/shard_map/ppermute | solution.py:311
  34.7 6.2 %collective-permute-start.18 = (bf16[144,256]{1,0:T(8,128)(2,1)S(1)}, bf16[144,256]{1,0:T(8,128)(2,1)S(1)}, u32[]{:S(2)}, u32[]{:S(2)}) collective-permute-start(bf16[144,256]{1,0:T(8,128)(2,1)S(1)} %get-tuple-element.71.rest_2_), channel_id=1, source_target_pairs={{0,24},{4,28},{8,16},{12,20},{16,8},{20,12},{24,0},{28,4},{1,25},{... | collective-permute-start | bytes 221192 | tf_op jit(solution)/shard_map/ppermute | solution.py:311
  41.1 6.7 %collective-permute-start.22 = (bf16[128,256]{1,0:T(8,128)(2,1)S(1)}, bf16[128,256]{1,0:T(8,128)(2,1)S(1)}, u32[]{:S(2)}, u32[]{:S(2)}) collective-permute-start(bf16[128,256]{1,0:T(8,128)(2,1)S(1)} %get-tuple-element.82), channel_id=1, source_target_pairs={{0,16},{4,20},{8,24},{12,28},{16,0},{20,4},{24,8},{28,12},{1,17},{... | collective-permute-start | bytes 196616 | tf_op jit(solution)/shard_map/ppermute | solution.py:311
  42.5 5.6 %collective-permute-start.23 = (bf16[128,256]{1,0:T(8,128)(2,1)S(1)}, bf16[128,256]{1,0:T(8,128)(2,1)S(1)}, u32[]{:S(2)}, u32[]{:S(2)}) collective-permute-start(bf16[128,256]{1,0:T(8,128)(2,1)S(1)} %get-tuple-element.83), channel_id=1, source_target_pairs={{0,8},{4,12},{8,0},{12,4},{16,24},{20,28},{24,16},{28,20},{1,9},{5... | collective-permute-start | bytes 196616 | tf_op jit(solution)/shard_map/ppermute | solution.py:311
  44.1 6.1 %collective-permute-start.21 = (bf16[128,256]{1,0:T(8,128)(2,1)S(1)}, bf16[128,256]{1,0:T(8,128)(2,1)S(1)}, u32[]{:S(2)}, u32[]{:S(2)}) collective-permute-start(bf16[128,256]{1,0:T(8,128)(2,1)S(1)} %get-tuple-element.81.rest_2_), channel_id=1, source_target_pairs={{0,24},{4,28},{8,16},{12,20},{16,8},{20,12},{24,0},{28,4},{1,25},{... | collective-permute-start | bytes 196616 | tf_op jit(solution)/shard_map/ppermute | solution.py:311
  50.4 6.5 %collective-permute-start.24 = (bf16[528,256]{1,0:T(8,128)(2,1)S(1)}, bf16[528,256]{1,0:T(8,128)(2,1)S(1)}, u32[]{:S(2)}, u32[]{:S(2)}) collective-permute-start(bf16[528,256]{1,0:T(8,128)(2,1)S(1)} %get-tuple-element.88), channel_id=1, source_target_pairs={{0,4},{4,0},{8,12},{12,8},{16,20},{20,16},{24,28},{28,24},{1,5},{5... | collective-permute-start | bytes 811016 | tf_op jit(solution)/shard_map/ppermute | solution.py:311
  52.3 6.5 %collective-permute-start.26 = (bf16[528,256]{1,0:T(8,128)(2,1)S(1)}, bf16[528,256]{1,0:T(8,128)(2,1)S(1)}, u32[]{:S(2)}, u32[]{:S(2)}) collective-permute-start(bf16[528,256]{1,0:T(8,128)(2,1)S(1)} %get-tuple-element.92), channel_id=1, source_target_pairs={{0,2},{1,3},{2,0},{3,1},{4,6},{5,7},{6,4},{7,5},{8,10},{9,11},{10,... | collective-permute-start | bytes 811016 | tf_op jit(solution)/shard_map/ppermute | solution.py:308
  52.9 6.1 %collective-permute-start.28 = (bf16[528,256]{1,0:T(8,128)(2,1)S(1)}, bf16[528,256]{1,0:T(8,128)(2,1)S(1)}, u32[]{:S(2)}, u32[]{:S(2)}) collective-permute-start(bf16[528,256]{1,0:T(8,128)(2,1)S(1)} %shard_map.68), channel_id=1, source_target_pairs={{0,1},{1,0},{2,3},{3,2},{4,5},{5,4},{6,7},{7,6},{8,9},{9,8},{10,11... | collective-permute-start | bytes 811016 | tf_op jit(solution)/shard_map/ppermute | solution.py:308
  57.2 3.0 %collective-permute-start.27 = (bf16[528,256]{1,0:T(8,128)(2,1)S(1)}, bf16[528,256]{1,0:T(8,128)(2,1)S(1)}, u32[]{:S(2)}, u32[]{:S(2)}) collective-permute-start(bf16[528,256]{1,0:T(8,128)(2,1)S(1)} %shard_map.67), channel_id=1, source_target_pairs={{0,1},{1,0},{2,3},{3,2},{4,5},{5,4},{6,7},{7,6},{8,9},{9,8},{10,11... | collective-permute-start | bytes 811016 | tf_op jit(solution)/shard_map/ppermute | solution.py:308
  57.3 8.9 %collective-permute-start.25 = (bf16[528,256]{1,0:T(8,128)(2,1)S(1)}, bf16[528,256]{1,0:T(8,128)(2,1)S(1)}, u32[]{:S(2)}, u32[]{:S(2)}) collective-permute-start(bf16[528,256]{1,0:T(8,128)(2,1)S(1)} %get-tuple-element.89), channel_id=1, source_target_pairs={{0,2},{1,3},{2,0},{3,1},{4,6},{5,7},{6,4},{7,5},{8,10},{9,11},{10,... | collective-permute-start | bytes 811016 | tf_op jit(solution)/shard_map/ppermute | solution.py:308
  58.9 7.5 %collective-permute-start.30 = (bf16[528,256]{1,0:T(8,128)(2,1)S(1)}, bf16[528,256]{1,0:T(8,128)(2,1)S(1)}, u32[]{:S(2)}, u32[]{:S(2)}) collective-permute-start(bf16[528,256]{1,0:T(8,128)(2,1)S(1)} %shard_map.73), channel_id=1, source_target_pairs={{0,1},{1,0},{2,3},{3,2},{4,5},{5,4},{6,7},{7,6},{8,9},{9,8},{10,11... | collective-permute-start | bytes 811016 | tf_op jit(solution)/shard_map/ppermute | solution.py:308
  (7 other events, 9.7 us)

commit v7 on v6

--- a/solution.py
+++ b/solution.py
@@ -434,7 +434,7 @@
         if key != later[0] and ny == 2:
             (rest,) = tie([dirs[key][0]], [piece[later[0]]])
             dirs[key] = (rest, head_swap(rest, 1))
-        states(key, [piece[first[0]]])
+        states(key, [])
 
     rows_of = {}
     for dy in reversed(range(ny)):

time: 69.3 us -> 69.3 us (level)
  no operation moved by 1% of the time
where the time goes in v7:
time: 69.3 us; the launch traced here: 69.1 us
  starting transfers between devices  24.3 us (35%)
  waiting for transfers between devices  22.6 us (33%)
  Pallas kernels  20.8 us (30%)
  local copies, waits for them, and re-layouts  0.97 us (1%)
    pallas_call x30, Pallas kernels, call(): pl.pallas_call(kernel, out_shape=out, in_specs=[far] * len(there) + [near...  20.8 us
    ppermute x9, starting transfers between devices, seq_swap(): return lax.ppermute(a, 'seq', [(i, i ^ bits) for i in range(seqs)])  13.9 us
    ppermute x22, waiting for transfers between devices, head_swap(): return lax.ppermute(a, 'head', [(i, i ^ bits) for i in range(heads)])  11.3 us
    ppermute x9, waiting for transfers between devices, seq_swap(): return lax.ppermute(a, 'seq', [(i, i ^ bits) for i in range(seqs)])  11.3 us
    ppermute x22, starting transfers between devices, head_swap(): return lax.ppermute(a, 'head', [(i, i ^ bits) for i in range(heads)])  10.4 us
  transfers between devices with their start and end apart: 31, of which 18 were waited for; matrix products, arithmetic and copies ran while one was open for 1% of the time, Pallas kernels for 28%

profile of v7, /device:TPU:0, one launch (start us, length us, event | category | flops | bytes accessed | tf_op | source)
XLA Modules:
  0.0 69.1 jit_solution(17578384766735126843)
XLA Ops:
  1.4 2.6 %collective-permute-start.1 = (bf16[4,256,128]{2,1,0:T(8,128)(2,1)S(1)}, bf16[4,256,128]{2,1,0:T(8,128)(2,1)S(1)}, u32[]{:S(2)}, u32[]{:S(2)}) collective-permute-start(bf16[4,256,128]{2,1,0:T(8,128)(2,1)S(1)} %constant_dynamic-slice_fusion), channel_id=1, source_target_pairs={{0,2},{1,3},{2,0},{3,1},{4,6},{5,7},{6,4},{7,5},{8,10},{9,11},{10,... | collective-permute-start | bytes 786440 | tf_op jit(solution)/shard_map/ppermute | solution.py:308
  4.0 2.7 %shard_map.46 = (bf16[8,256,256]{2,1,0:T(8,128)(2,1)S(1)}, bf16[256,256]{1,0:T(8,128)(2,1)S(1)}, bf16[272,256]{1,0:T(8,128)(2,1)S(1)}, bf16[528,256]{1,0:T(8,128...) custom-call(bf16[256,4096]{1,0:T(8,128)(2,1)} %bitcast.5, ...), custom_call_target="tpu_custom_call" | custom-call | tf_op jit(solution)/shard_map/pallas_call | solution.py:336
  7.0 1.6 %shard_map.47 = (bf16[8,256,256]{2,1,0:T(8,128)(2,1)S(1)}, bf16[256,256]{1,0:T(8,128)(2,1)S(1)}, bf16[272,256]{1,0:T(8,128)(2,1)S(1)}, bf16[528,256]{1,0:T(8,128)(2,1)S(1)}, bf16[256,4096]{1,0:T(8,128)(2,1)S(1)}) custom-call(bf16[256,4096]{1,0:T(8,128)(2,1)} %bitcast.4, bf16[256,4096]{1,0:T(8,128)(2,1)S(1)} %get-tuple-element.52.k, ...), custom_call_target="tpu_custom_call" | custom-call | tf_op jit(solution)/shard_map/pallas_call | solution.py:336
  11.1 1.8 %collective-permute-start.6 = (bf16[4,256,128]{2,1,0:T(8,128)(2,1)S(1)}, bf16[4,256,128]{2,1,0:T(8,128)(2,1)S(1)}, u32[]{:S(2)}, u32[]{:S(2)}) collective-permute-start(bf16[4,256,128]{2,1,0:T(8,128)(2,1)S(1)} %shard_map.50.refs_0_.rest_0_), channel_id=1, source_target_pairs={{0,4},{4,0},{8,12},{12,8},{16,20},{20,16},{24,28},{28,24},{1,5},{5... | collective-permute-start | bytes 786440 | tf_op jit(solution)/shard_map/ppermute | solution.py:311
  12.9 1.5 %collective-permute-start.16 = (bf16[528,256]{1,0:T(8,128)(2,1)S(1)}, bf16[528,256]{1,0:T(8,128)(2,1)S(1)}, u32[]{:S(2)}, u32[]{:S(2)}) collective-permute-start(bf16[528,256]{1,0:T(8,128)(2,1)S(1)} %shard_map.48.refs_1_), channel_id=1, source_target_pairs={{0,2},{1,3},{2,0},{3,1},{4,6},{5,7},{6,4},{7,5},{8,10},{9,11},{10,... | collective-permute-start | bytes 811016 | tf_op jit(solution)/shard_map/ppermute | solution.py:308
  14.4 1.4 %shard_map.51 = (bf16[8,256,256]{2,1,0:T(8,128)(2,1)S(1)}, bf16[128,256]{1,0:T(8,128)(2,1)S(1)}, bf16[128,256]{1,0:T(8,128)(2,1)S(1)}, bf16[128,256]{1,0:T(8,128...) custom-call(bf16[256,4096]{1,0:T(8,128)(2,1)S(1)} %get-tuple-element.52.k, ...), custom_call_target="tpu_custom_call" | custom-call | tf_op jit(solution)/shard_map/pallas_call | solution.py:336
  19.9 1.8 %collective-permute-start.15 = (bf16[528,256]{1,0:T(8,128)(2,1)S(1)}, bf16[528,256]{1,0:T(8,128)(2,1)S(1)}, u32[]{:S(2)}, u32[]{:S(2)}) collective-permute-start(bf16[528,256]{1,0:T(8,128)(2,1)S(1)} %shard_map.49.refs_2_), channel_id=1, source_target_pairs={{0,2},{1,3},{2,0},{3,1},{4,6},{5,7},{6,4},{7,5},{8,10},{9,11},{10,... | collective-permute-start | bytes 811016 | tf_op jit(solution)/shard_map/ppermute | solution.py:308
  21.8 1.6 %collective-permute-start.17 = (bf16[528,256]{1,0:T(8,128)(2,1)S(1)}, bf16[528,256]{1,0:T(8,128)(2,1)S(1)}, u32[]{:S(2)}, u32[]{:S(2)}) collective-permute-start(bf16[528,256]{1,0:T(8,128)(2,1)S(1)} %shard_map.57), channel_id=1, source_target_pairs={{0,4},{4,0},{8,12},{12,8},{16,20},{20,16},{24,28},{28,24},{1,5},{5... | collective-permute-start | bytes 811016 | tf_op jit(solution)/shard_map/ppermute | solution.py:311
  23.3 1.4 %shard_map.54 = (bf16[8,256,256]{2,1,0:T(8,128)(2,1)S(1)}, bf16[256,256]{1,0:T(8,128)(2,1)S(1)}, bf16[272,256]{1,0:T(8,128)(2,1)S(1)}, bf16[528,256]{1,0:T(8,128)(2,1)S(1)}) custom-call(bf16[256,4096]{1,0:T(8,128)(2,1)S(1)} %get-tuple-element.52.k, bf16[256,4096]{1,0:T(8,128)(2,1)S(1)} %get-tuple-element.53.v, ...), custom_call_target="tpu_custom_call" | custom-call | tf_op jit(solution)/shard_map/pallas_call | solution.py:336
  26.5 2.3 %collective-permute-done.15.refs_1_ = bf16[528,256]{1,0:T(8,128)(2,1)S(1)} collective-permute-done((bf16[528,256]{1,0:T(8,128)(2,1)S(1)}, bf16[528,256]{1,0:T(8,128)(2,1)S(1)}, u32[]{:S(2)}, u32[]{:S(2)}) %collective-permute-start.15) | collective-permute-done | bytes 270368 | tf_op jit(solution)/shard_map/ppermute | solution.py:308
  28.9 1.5 %collective-permute-done.17.refs_1_.refs_6_ = bf16[528,256]{1,0:T(8,128)(2,1)S(1)} collective-permute-done((bf16[528,256]{1,0:T(8,128)(2,1)S(1)}, bf16[528,256]{1,0:T(8,128)(2,1)S(1)}, u32[]{:S(2)}, u32[]{:S(2)}) %collective-permute-start.17) | collective-permute-done | bytes 270368 | tf_op jit(solution)/shard_map/ppermute | solution.py:311
  30.5 2.7 %collective-permute-start.19 = (bf16[144,256]{1,0:T(8,128)(2,1)S(1)}, bf16[144,256]{1,0:T(8,128)(2,1)S(1)}, u32[]{:S(2)}, u32[]{:S(2)}) collective-permute-start(bf16[144,256]{1,0:T(8,128)(2,1)S(1)} %get-tuple-element.74), channel_id=1, source_target_pairs={{0,16},{4,20},{8,24},{12,28},{16,0},{20,4},{24,8},{28,12},{1,17},{... | collective-permute-start | bytes 221192 | tf_op jit(solution)/shard_map/ppermute | solution.py:311
  33.1 1.6 %collective-permute-start.20 = (bf16[144,256]{1,0:T(8,128)(2,1)S(1)}, bf16[144,256]{1,0:T(8,128)(2,1)S(1)}, u32[]{:S(2)}, u32[]{:S(2)}) collective-permute-start(bf16[144,256]{1,0:T(8,128)(2,1)S(1)} %get-tuple-element.75), channel_id=1, source_target_pairs={{0,8},{4,12},{8,0},{12,4},{16,24},{20,28},{24,16},{28,20},{1,9},{5... | collective-permute-start | bytes 221192 | tf_op jit(solution)/shard_map/ppermute | solution.py:311
  34.9 1.5 %shard_map.61 = (bf16[8,256,256]{2,1,0:T(8,128)(2,1)S(1)}, f32[8,256,256]{2,1,0:T(8,128)S(1)}) custom-call(bf16[256,4096]{1,0:T(8,128)(2,1)S(1)} %get-tuple-element.55.q, bf16[256,4096]{1,0:T(8,128)(2,1)S(1)} %get-tuple-element.53.v, bf16[8,256,256]{2,1,0:T(8,128)(2,1)S(1)} %get-tuple-element.79.phi_k, bf16[4,256,128]{2,1,0:T(8,128)(2,1)S(1)} %shard_map.50.refs_0_.rest_0_, ...), custom_call_target="tpu_custom_call" | custom-call | tf_op jit(solution)/shard_map/pallas_call | solution.py:336
  36.4 1.5 %shard_map.60 = (bf16[8,256,256]{2,1,0:T(8,128)(2,1)S(1)}, f32[8,256,256]{2,1,0:T(8,128)S(1)}) custom-call(bf16[256,4096]{1,0:T(8,128)(2,1)S(1)} %get-tuple-element.55.q, bf16[256,4096]{1,0:T(8,128)(2,1)S(1)} %get-tuple-element.53.v, bf16[8,256,256]{2,1,0:T(8,128)(2,1)S(1)} %get-tuple-element.77.phi_k, ...), custom_call_target="tpu_custom_call" | custom-call | tf_op jit(solution)/shard_map/pallas_call | solution.py:336
  38.0 1.7 %shard_map.59 = (bf16[8,256,256]{2,1,0:T(8,128)(2,1)S(1)}, f32[8,256,256]{2,1,0:T(8,128)S(1)}) custom-call(bf16[256,4096]{1,0:T(8,128)(2,1)S(1)} %get-tuple-element.55.q, bf16[256,4096]{1,0:T(8,128)(2,1)S(1)} %get-tuple-element.53.v, bf16[8,256,256]{2,1,0:T(8,128)(2,1)S(1)} %get-tuple-element.56.phi_k, ...), custom_call_target="tpu_custom_call" | custom-call | tf_op jit(solution)/shard_map/pallas_call | solution.py:336
  41.1 1.5 %collective-permute-start.22 = (bf16[128,256]{1,0:T(8,128)(2,1)S(1)}, bf16[128,256]{1,0:T(8,128)(2,1)S(1)}, u32[]{:S(2)}, u32[]{:S(2)}) collective-permute-start(bf16[128,256]{1,0:T(8,128)(2,1)S(1)} %get-tuple-element.82), channel_id=1, source_target_pairs={{0,16},{4,20},{8,24},{12,28},{16,0},{20,4},{24,8},{28,12},{1,17},{... | collective-permute-start | bytes 196616 | tf_op jit(solution)/shard_map/ppermute | solution.py:311
  42.5 1.6 %collective-permute-start.23 = (bf16[128,256]{1,0:T(8,128)(2,1)S(1)}, bf16[128,256]{1,0:T(8,128)(2,1)S(1)}, u32[]{:S(2)}, u32[]{:S(2)}) collective-permute-start(bf16[128,256]{1,0:T(8,128)(2,1)S(1)} %get-tuple-element.83), channel_id=1, source_target_pairs={{0,8},{4,12},{8,0},{12,4},{16,24},{20,28},{24,16},{28,20},{1,9},{5... | collective-permute-start | bytes 196616 | tf_op jit(solution)/shard_map/ppermute | solution.py:311
  44.1 1.4 %collective-permute-start.21 = (bf16[128,256]{1,0:T(8,128)(2,1)S(1)}, bf16[128,256]{1,0:T(8,128)(2,1)S(1)}, u32[]{:S(2)}, u32[]{:S(2)}) collective-permute-start(bf16[128,256]{1,0:T(8,128)(2,1)S(1)} %get-tuple-element.81.rest_2_), channel_id=1, source_target_pairs={{0,24},{4,28},{8,16},{12,20},{16,8},{20,12},{24,0},{28,4},{1,25},{... | collective-permute-start | bytes 196616 | tf_op jit(solution)/shard_map/ppermute | solution.py:311
  45.5 1.5 %shard_map.63 = (bf16[8,256,256]{2,1,0:T(8,128)(2,1)S(1)}, f32[8,256,256]{2,1,0:T(8,128)S(1)}) custom-call(bf16[256,4096]{1,0:T(8,128)(2,1)S(1)} %get-tuple-element.55.q, bf16[256,4096]{1,0:T(8,128)(2,1)S(1)} %get-tuple-element.53.v, bf16[8,256,256]{2,1,0:T(8,128)(2,1)S(1)} %get-tuple-element.86.phi_k, bf16[4,256,128]{2,1,0:T(8,128)(2,1)S(1)} %shard_map.53.refs_0_.rest_0_, ...), custom_call_target="tpu_custom_call" | custom-call | tf_op jit(solution)/shard_map/pallas_call | solution.py:336
  48.1 2.1 %collective-permute-done.21.refs_0_ = bf16[128,256]{1,0:T(8,128)(2,1)S(1)} collective-permute-done((bf16[128,256]{1,0:T(8,128)(2,1)S(1)}, bf16[128,256]{1,0:T(8,128)(2,1)S(1)}, u32[]{:S(2)}, u32[]{:S(2)}) %collective-permute-start.21) | collective-permute-done | bytes 65568 | tf_op jit(solution)/shard_map/ppermute | solution.py:311
  50.4 1.6 %collective-permute-start.24 = (bf16[528,256]{1,0:T(8,128)(2,1)S(1)}, bf16[528,256]{1,0:T(8,128)(2,1)S(1)}, u32[]{:S(2)}, u32[]{:S(2)}) collective-permute-start(bf16[528,256]{1,0:T(8,128)(2,1)S(1)} %get-tuple-element.88), channel_id=1, source_target_pairs={{0,4},{4,0},{8,12},{12,8},{16,20},{20,16},{24,28},{28,24},{1,5},{5... | collective-permute-start | bytes 811016 | tf_op jit(solution)/shard_map/ppermute | solution.py:311
  52.9 4.1 %collective-permute-done.24.base = bf16[528,256]{1,0:T(8,128)(2,1)S(1)} collective-permute-done((bf16[528,256]{1,0:T(8,128)(2,1)S(1)}, bf16[528,256]{1,0:T(8,128)(2,1)S(1)}, u32[]{:S(2)}, u32[]{:S(2)}) %collective-permute-start.24) | collective-permute-done | bytes 270368 | tf_op jit(solution)/shard_map/ppermute | solution.py:311
  62.6 3.7 %collective-permute-done.25.base.refs_5_ = bf16[528,256]{1,0:T(8,128)(2,1)S(1)} collective-permute-done((bf16[528,256]{1,0:T(8,128)(2,1)S(1)}, bf16[528,256]{1,0:T(8,128)(2,1)S(1)}, u32[]{:S(2)}, u32[]{:S(2)}) %collective-permute-start.25) | collective-permute-done | bytes 270368 | tf_op jit(solution)/shard_map/ppermute | solution.py:308
  (69 shorter events, 22.1 us)
Async XLA Ops:
  0.0 4.0 %collective-permute-start = (bf16[8,256,128]{2,1,0:T(8,128)(2,1)}, bf16[8,256,128]{2,1,0:T(8,128)(2,1)S(1)}, u32[]{:S(2)}, u32[]{:S(2)}) collective-permute-start(bf16[8,256,128]{2,1,0:T(8,128)(2,1)} %f_far.1), channel_id=1, source_target_pairs={{0,1},{1,0},{2,3},{3,2},{4,5},{5,4},{6,7},{7,6},{8,9},{9,8},{10,11... | collective-permute-start | bytes 1572872 | tf_op jit(solution)/shard_map/ppermute | solution.py:308
  1.4 9.5 %collective-permute-start.1 = (bf16[4,256,128]{2,1,0:T(8,128)(2,1)S(1)}, bf16[4,256,128]{2,1,0:T(8,128)(2,1)S(1)}, u32[]{:S(2)}, u32[]{:S(2)}) collective-permute-start(bf16[4,256,128]{2,1,0:T(8,128)(2,1)S(1)} %constant_dynamic-slice_fusion), channel_id=1, source_target_pairs={{0,2},{1,3},{2,0},{3,1},{4,6},{5,7},{6,4},{7,5},{8,10},{9,11},{10,... | collective-permute-start | bytes 786440 | tf_op jit(solution)/shard_map/ppermute | solution.py:308
  6.7 3.6 %collective-permute-start.3 = (bf16[272,256]{1,0:T(8,128)(2,1)S(1)}, bf16[272,256]{1,0:T(8,128)(2,1)S(1)}, u32[]{:S(2)}, u32[]{:S(2)}) collective-permute-start(bf16[272,256]{1,0:T(8,128)(2,1)S(1)} %get-tuple-element.59), channel_id=1, source_target_pairs={{0,1},{1,0},{2,3},{3,2},{4,5},{5,4},{6,7},{7,6},{8,9},{9,8},{10,11... | collective-permute-start | bytes 417800 | tf_op jit(solution)/shard_map/ppermute | solution.py:308
  8.6 1.9 %collective-permute-start.5 = (bf16[272,256]{1,0:T(8,128)(2,1)S(1)}, bf16[272,256]{1,0:T(8,128)(2,1)S(1)}, u32[]{:S(2)}, u32[]{:S(2)}) collective-permute-start(bf16[272,256]{1,0:T(8,128)(2,1)S(1)} %get-tuple-element.62), channel_id=1, source_target_pairs={{0,1},{1,0},{2,3},{3,2},{4,5},{5,4},{6,7},{7,6},{8,9},{9,8},{10,11... | collective-permute-start | bytes 417800 | tf_op jit(solution)/shard_map/ppermute | solution.py:308
  11.0 3.4 %collective-permute-start.7 = (bf16[4,256,128]{2,1,0:T(8,128)(2,1)S(1)}, bf16[4,256,128]{2,1,0:T(8,128)(2,1)S(1)}, u32[]{:S(2)}, u32[]{:S(2)}) collective-permute-start(bf16[4,256,128]{2,1,0:T(8,128)(2,1)S(1)} %shard_map.50.refs_0_.rest_0_), channel_id=1, source_target_pairs={{0,1},{1,0},{2,3},{3,2},{4,5},{5,4},{6,7},{7,6},{8,9},{9,8},{10,11... | collective-permute-start | bytes 786440 | tf_op jit(solution)/shard_map/ppermute | solution.py:308
  11.1 8.7 %collective-permute-start.6 = (bf16[4,256,128]{2,1,0:T(8,128)(2,1)S(1)}, bf16[4,256,128]{2,1,0:T(8,128)(2,1)S(1)}, u32[]{:S(2)}, u32[]{:S(2)}) collective-permute-start(bf16[4,256,128]{2,1,0:T(8,128)(2,1)S(1)} %shard_map.50.refs_0_.rest_0_), channel_id=1, source_target_pairs={{0,4},{4,0},{8,12},{12,8},{16,20},{20,16},{24,28},{28,24},{1,5},{5... | collective-permute-start | bytes 786440 | tf_op jit(solution)/shard_map/ppermute | solution.py:311
  12.9 8.8 %collective-permute-start.16 = (bf16[528,256]{1,0:T(8,128)(2,1)S(1)}, bf16[528,256]{1,0:T(8,128)(2,1)S(1)}, u32[]{:S(2)}, u32[]{:S(2)}) collective-permute-start(bf16[528,256]{1,0:T(8,128)(2,1)S(1)} %shard_map.48.refs_1_), channel_id=1, source_target_pairs={{0,2},{1,3},{2,0},{3,1},{4,6},{5,7},{6,4},{7,5},{8,10},{9,11},{10,... | collective-permute-start | bytes 811016 | tf_op jit(solution)/shard_map/ppermute | solution.py:308
  15.9 2.5 %collective-permute-start.11 = (bf16[144,256]{1,0:T(8,128)(2,1)S(1)}, bf16[144,256]{1,0:T(8,128)(2,1)S(1)}, u32[]{:S(2)}, u32[]{:S(2)}) collective-permute-start(bf16[144,256]{1,0:T(8,128)(2,1)S(1)} %get-tuple-element.67), channel_id=1, source_target_pairs={{0,1},{1,0},{2,3},{3,2},{4,5},{5,4},{6,7},{7,6},{8,9},{9,8},{10,11... | collective-permute-start | bytes 221192 | tf_op jit(solution)/shard_map/ppermute | solution.py:308
  19.8 3.5 %collective-permute-start.12 = (bf16[4,256,128]{2,1,0:T(8,128)(2,1)S(1)}, bf16[4,256,128]{2,1,0:T(8,128)(2,1)S(1)}, u32[]{:S(2)}, u32[]{:S(2)}) collective-permute-start(bf16[4,256,128]{2,1,0:T(8,128)(2,1)S(1)} %shard_map.53.refs_0_.rest_0_), channel_id=1, source_target_pairs={{0,1},{1,0},{2,3},{3,2},{4,5},{5,4},{6,7},{7,6},{8,9},{9,8},{10,11... | collective-permute-start | bytes 786440 | tf_op jit(solution)/shard_map/ppermute | solution.py:308
  19.9 8.9 %collective-permute-start.15 = (bf16[528,256]{1,0:T(8,128)(2,1)S(1)}, bf16[528,256]{1,0:T(8,128)(2,1)S(1)}, u32[]{:S(2)}, u32[]{:S(2)}) collective-permute-start(bf16[528,256]{1,0:T(8,128)(2,1)S(1)} %shard_map.49.refs_2_), channel_id=1, source_target_pairs={{0,2},{1,3},{2,0},{3,1},{4,6},{5,7},{6,4},{7,5},{8,10},{9,11},{10,... | collective-permute-start | bytes 811016 | tf_op jit(solution)/shard_map/ppermute | solution.py:308
  21.8 8.6 %collective-permute-start.17 = (bf16[528,256]{1,0:T(8,128)(2,1)S(1)}, bf16[528,256]{1,0:T(8,128)(2,1)S(1)}, u32[]{:S(2)}, u32[]{:S(2)}) collective-permute-start(bf16[528,256]{1,0:T(8,128)(2,1)S(1)} %shard_map.57), channel_id=1, source_target_pairs={{0,4},{4,0},{8,12},{12,8},{16,20},{20,16},{24,28},{28,24},{1,5},{5... | collective-permute-start | bytes 811016 | tf_op jit(solution)/shard_map/ppermute | solution.py:311
  24.8 1.6 %collective-permute-start.14 = (bf16[272,256]{1,0:T(8,128)(2,1)S(1)}, bf16[272,256]{1,0:T(8,128)(2,1)S(1)}, u32[]{:S(2)}, u32[]{:S(2)}) collective-permute-start(bf16[272,256]{1,0:T(8,128)(2,1)S(1)} %get-tuple-element.70), channel_id=1, source_target_pairs={{0,1},{1,0},{2,3},{3,2},{4,5},{5,4},{6,7},{7,6},{8,9},{9,8},{10,11... | collective-permute-start | bytes 417800 | tf_op jit(solution)/shard_map/ppermute | solution.py:308
  30.5 9.2 %collective-permute-start.19 = (bf16[144,256]{1,0:T(8,128)(2,1)S(1)}, bf16[144,256]{1,0:T(8,128)(2,1)S(1)}, u32[]{:S(2)}, u32[]{:S(2)}) collective-permute-start(bf16[144,256]{1,0:T(8,128)(2,1)S(1)} %get-tuple-element.74), channel_id=1, source_target_pairs={{0,16},{4,20},{8,24},{12,28},{16,0},{20,4},{24,8},{28,12},{1,17},{... | collective-permute-start | bytes 221192 | tf_op jit(solution)/shard_map/ppermute | solution.py:311
  33.1 6.5 %collective-permute-start.20 = (bf16[144,256]{1,0:T(8,128)(2,1)S(1)}, bf16[144,256]{1,0:T(8,128)(2,1)S(1)}, u32[]{:S(2)}, u32[]{:S(2)}) collective-permute-start(bf16[144,256]{1,0:T(8,128)(2,1)S(1)} %get-tuple-element.75), channel_id=1, source_target_pairs={{0,8},{4,12},{8,0},{12,4},{16,24},{20,28},{24,16},{28,20},{1,9},{5... | collective-permute-start | bytes 221192 | tf_op jit(solution)/shard_map/ppermute | solution.py:311
  34.7 6.2 %collective-permute-start.18 = (bf16[144,256]{1,0:T(8,128)(2,1)S(1)}, bf16[144,256]{1,0:T(8,128)(2,1)S(1)}, u32[]{:S(2)}, u32[]{:S(2)}) collective-permute-start(bf16[144,256]{1,0:T(8,128)(2,1)S(1)} %get-tuple-element.71.rest_2_), channel_id=1, source_target_pairs={{0,24},{4,28},{8,16},{12,20},{16,8},{20,12},{24,0},{28,4},{1,25},{... | collective-permute-start | bytes 221192 | tf_op jit(solution)/shard_map/ppermute | solution.py:311
  41.1 6.7 %collective-permute-start.22 = (bf16[128,256]{1,0:T(8,128)(2,1)S(1)}, bf16[128,256]{1,0:T(8,128)(2,1)S(1)}, u32[]{:S(2)}, u32[]{:S(2)}) collective-permute-start(bf16[128,256]{1,0:T(8,128)(2,1)S(1)} %get-tuple-element.82), channel_id=1, source_target_pairs={{0,16},{4,20},{8,24},{12,28},{16,0},{20,4},{24,8},{28,12},{1,17},{... | collective-permute-start | bytes 196616 | tf_op jit(solution)/shard_map/ppermute | solution.py:311
  42.5 5.6 %collective-permute-start.23 = (bf16[128,256]{1,0:T(8,128)(2,1)S(1)}, bf16[128,256]{1,0:T(8,128)(2,1)S(1)}, u32[]{:S(2)}, u32[]{:S(2)}) collective-permute-start(bf16[128,256]{1,0:T(8,128)(2,1)S(1)} %get-tuple-element.83), channel_id=1, source_target_pairs={{0,8},{4,12},{8,0},{12,4},{16,24},{20,28},{24,16},{28,20},{1,9},{5... | collective-permute-start | bytes 196616 | tf_op jit(solution)/shard_map/ppermute | solution.py:311
  44.1 6.1 %collective-permute-start.21 = (bf16[128,256]{1,0:T(8,128)(2,1)S(1)}, bf16[128,256]{1,0:T(8,128)(2,1)S(1)}, u32[]{:S(2)}, u32[]{:S(2)}) collective-permute-start(bf16[128,256]{1,0:T(8,128)(2,1)S(1)} %get-tuple-element.81.rest_2_), channel_id=1, source_target_pairs={{0,24},{4,28},{8,16},{12,20},{16,8},{20,12},{24,0},{28,4},{1,25},{... | collective-permute-start | bytes 196616 | tf_op jit(solution)/shard_map/ppermute | solution.py:311
  50.4 6.5 %collective-permute-start.24 = (bf16[528,256]{1,0:T(8,128)(2,1)S(1)}, bf16[528,256]{1,0:T(8,128)(2,1)S(1)}, u32[]{:S(2)}, u32[]{:S(2)}) collective-permute-start(bf16[528,256]{1,0:T(8,128)(2,1)S(1)} %get-tuple-element.88), channel_id=1, source_target_pairs={{0,4},{4,0},{8,12},{12,8},{16,20},{20,16},{24,28},{28,24},{1,5},{5... | collective-permute-start | bytes 811016 | tf_op jit(solution)/shard_map/ppermute | solution.py:311
  52.3 6.5 %collective-permute-start.26 = (bf16[528,256]{1,0:T(8,128)(2,1)S(1)}, bf16[528,256]{1,0:T(8,128)(2,1)S(1)}, u32[]{:S(2)}, u32[]{:S(2)}) collective-permute-start(bf16[528,256]{1,0:T(8,128)(2,1)S(1)} %get-tuple-element.92), channel_id=1, source_target_pairs={{0,2},{1,3},{2,0},{3,1},{4,6},{5,7},{6,4},{7,5},{8,10},{9,11},{10,... | collective-permute-start | bytes 811016 | tf_op jit(solution)/shard_map/ppermute | solution.py:308
  52.9 6.1 %collective-permute-start.28 = (bf16[528,256]{1,0:T(8,128)(2,1)S(1)}, bf16[528,256]{1,0:T(8,128)(2,1)S(1)}, u32[]{:S(2)}, u32[]{:S(2)}) collective-permute-start(bf16[528,256]{1,0:T(8,128)(2,1)S(1)} %shard_map.68), channel_id=1, source_target_pairs={{0,1},{1,0},{2,3},{3,2},{4,5},{5,4},{6,7},{7,6},{8,9},{9,8},{10,11... | collective-permute-start | bytes 811016 | tf_op jit(solution)/shard_map/ppermute | solution.py:308
  57.2 3.0 %collective-permute-start.27 = (bf16[528,256]{1,0:T(8,128)(2,1)S(1)}, bf16[528,256]{1,0:T(8,128)(2,1)S(1)}, u32[]{:S(2)}, u32[]{:S(2)}) collective-permute-start(bf16[528,256]{1,0:T(8,128)(2,1)S(1)} %shard_map.67), channel_id=1, source_target_pairs={{0,1},{1,0},{2,3},{3,2},{4,5},{5,4},{6,7},{7,6},{8,9},{9,8},{10,11... | collective-permute-start | bytes 811016 | tf_op jit(solution)/shard_map/ppermute | solution.py:308
  57.3 8.9 %collective-permute-start.25 = (bf16[528,256]{1,0:T(8,128)(2,1)S(1)}, bf16[528,256]{1,0:T(8,128)(2,1)S(1)}, u32[]{:S(2)}, u32[]{:S(2)}) collective-permute-start(bf16[528,256]{1,0:T(8,128)(2,1)S(1)} %get-tuple-element.89), channel_id=1, source_target_pairs={{0,2},{1,3},{2,0},{3,1},{4,6},{5,7},{6,4},{7,5},{8,10},{9,11},{10,... | collective-permute-start | bytes 811016 | tf_op jit(solution)/shard_map/ppermute | solution.py:308
  58.9 7.5 %collective-permute-start.30 = (bf16[528,256]{1,0:T(8,128)(2,1)S(1)}, bf16[528,256]{1,0:T(8,128)(2,1)S(1)}, u32[]{:S(2)}, u32[]{:S(2)}) collective-permute-start(bf16[528,256]{1,0:T(8,128)(2,1)S(1)} %shard_map.73), channel_id=1, source_target_pairs={{0,1},{1,0},{2,3},{3,2},{4,5},{5,4},{6,7},{7,6},{8,9},{9,8},{10,11... | collective-permute-start | bytes 811016 | tf_op jit(solution)/shard_map/ppermute | solution.py:308
  (7 other events, 9.7 us)
